TPU v7x, 512 devices: a whole 4x8x8 slice. The times are simulated.
512 devices in a mesh: top: 16 (over y, core), leaf: 32 (over x, z).
Axes of the slice: x: 4, y: 8, z: 8, core: 2. Of those that a mesh axis runs over, the one named last changes fastest.
Arguments:
- traction_vectors: float32 [4096, 192, 128], P(('top', 'leaf')), may hold values from -6 to 6
- row_basis: float32 [4096, 32, 192], P(('top', 'leaf')), may hold values from -0.4375 to 0.4375
- up_leaf: float32 [4096, 1024], P(('top', 'leaf')), may hold values from -0.75 to 0.75
- up_pair: float32 [2048, 1024], P(('top', 'leaf')), may hold values from -0.5 to 0.5
- up_device: float32 [512, 1024], P(('top', 'leaf')), may hold values from -0.1875 to 0.1875
- couple_leaf: float32 [4096, 6, 1024], P(('top', 'leaf')), may hold values from -0.4375 to 0.4375
- pair_coupling_blocks: float32 [2048, 6, 1024], P(('top', 'leaf')), may hold values from -0.4375 to 0.4375
- couple_device: float32 [512, 6, 1024], P(('top', 'leaf')), may hold values from -0.4375 to 0.4375
- couple_top: float32 [16, 4, 1024], P('top'), may hold values from -0.5 to 0.5
- list_leaf: int32 [4096, 6], P(('top', 'leaf')), may hold values from 0 to 4095, as said below
- list_pair: int32 [2048, 6], P(('top', 'leaf')), may hold values from 0 to 2047, as said below
- list_device: int32 [512, 6], P(('top', 'leaf')), may hold values from 0 to 511
- list_top: int32 [16, 4], P('top'), may hold values from 0 to 15
- mask_leaf: int32 [4096, 6], P(('top', 'leaf')), may hold values 0 or 1
- mask_pair: int32 [2048, 6], P(('top', 'leaf')), may hold values 0 or 1
- mask_device: int32 [512, 6], P(('top', 'leaf')), may hold values 0 or 1
- mask_top: int32 [16, 4], P('top'), may hold values 0 or 1
- down_leaf: float32 [4096, 1024], P(('top', 'leaf')), may hold values from -1 to 1
- down_pair: float32 [2048, 1024], P(('top', 'leaf')), may hold values from -1 to 1
- down_device: float32 [512, 1024], P(('top', 'leaf')), may hold values from -1 to 1
- col_basis: float32 [4096, 32, 192], P(('top', 'leaf')), may hold values from -0.5 to 0.5
Outputs:
- product: float32 [4096, 192, 128], P(('top', 'leaf'))
Inputs may be any that keep to these rules, and one draw needn't show every extreme that they name: `list_leaf`: entry (i, k) lies in the same block of 256 leaf clusters as i, and from (i // 8 - 1) * 8 to (i // 8 + 2) * 8 - 1. `list_pair`: entry (p, k) lies in the same block of 128 pair clusters as p, and from (p // 4 - 1) * 4 to (p // 4 + 2) * 4 - 1.
All inputs are finite; a program needn't handle non-finite values. No bound on the sum of `mask_leaf` or of `mask_pair` or of `mask_device` or of `mask_top` on one device may be relied on, other than what follows from the above.
Results may differ from a plain program's by a relative error of at most 0.0001.
Values sent between devices are 32-bit elements; how exact they have to be, the bound alone decides.
No kernel may reach another device: no remote copies, remote signals or barrier semaphores. Data moves between devices by JAX's collectives and lax.ppermute only.
A program may use at most 64 MiB of HBM per device.

v0:
```python
import jax
import jax.numpy as jnp
from jax import lax
from jax.sharding import PartitionSpec as P

RANK = 32


TOPMOST_PRECISION = lax.Precision.HIGHEST


def with_halo(block, sides, width):
    for axis, dim in sides:
        count = lax.axis_size(axis)
        forward = [(i, i + 1) for i in range(count - 1)]
        backward = [(target, source) for source, target in forward]
        low = lax.ppermute(
            lax.slice_in_dim(block, block.shape[dim] - width, None, axis=dim), axis, forward
        )
        high = lax.ppermute(lax.slice_in_dim(block, 0, width, axis=dim), axis, backward)
        block = jnp.concatenate([low, block, high], axis=dim)
    return block


def square(flat_blocks):
    return flat_blocks.reshape(flat_blocks.shape[:-1] + (RANK, RANK))


def couple(blocks, sources, index, mask):
    accumulated_output = jnp.zeros((blocks.shape[0], RANK, sources.shape[-1]), jnp.float32)
    for slot in range(index.shape[1]):
        selected_entries = jnp.take(sources, index[:, slot], axis=0)
        quadrature_weight = (
            square(blocks[:, slot]) * mask[:, slot].astype(jnp.float32)[:, None, None]
        )
        accumulated_output = accumulated_output + jnp.einsum(
            "qup,qpj->quj", quadrature_weight, selected_entries, precision=TOPMOST_PRECISION
        )
    return accumulated_output


def local_rows(global_index, per_dev, position, row_of_blocks, offset):
    relative = global_index - position * per_dev + per_dev
    return relative // per_dev * row_of_blocks + offset + relative % per_dev


def collect(coeff_device):
    return lax.all_gather(coeff_device, ("top", "leaf"), axis=0, tiled=True)


def body(
    traction_vectors,
    row_basis,
    up_leaf,
    up_pair,
    up_device,
    couple_leaf,
    pair_coupling_blocks,
    couple_device,
    couple_top,
    list_leaf,
    list_pair,
    list_device,
    list_top,
    mask_leaf,
    mask_pair,
    mask_device,
    mask_top,
    down_leaf,
    down_pair,
    down_device,
    col_basis,
):
    leaf_count = traction_vectors.shape[0]
    pair_count = leaf_count // 2
    columns = traction_vectors.shape[2]
    position = lax.axis_index("top") * lax.axis_size("leaf") + lax.axis_index("leaf")
    coeff_leaf = jnp.einsum(
        "lre,len->lrn", row_basis, traction_vectors, precision=TOPMOST_PRECISION
    )
    coeff_pair = jnp.einsum(
        "pcab,pcan->pbn",
        square(up_leaf).reshape(pair_count, 2, RANK, RANK),
        coeff_leaf.reshape(pair_count, 2, RANK, columns),
        precision=TOPMOST_PRECISION,
    )
    coeff_device = jnp.einsum(
        "cab,can->bn", square(up_pair), coeff_pair, precision=TOPMOST_PRECISION
    )[None]
    top_term = jnp.dot(square(up_device)[0].T, coeff_device[0], precision=TOPMOST_PRECISION)
    stacked = jnp.concatenate([coeff_leaf, coeff_pair], axis=0)
    padded = with_halo(stacked, (("leaf", 0),), stacked.shape[0])
    device_table = collect(coeff_device)
    own_top = lax.psum(top_term, "leaf")
    coeff_top = lax.all_gather(own_top[None], "top", axis=0, tiled=True)
    row_of_blocks = stacked.shape[0]
    rows_leaf = local_rows(list_leaf, leaf_count, position, row_of_blocks, 0)
    rows_pair = local_rows(list_pair, pair_count, position, row_of_blocks, leaf_count)
    far_leaf = couple(couple_leaf, padded, rows_leaf, mask_leaf)
    far_pair = couple(pair_coupling_blocks, padded, rows_pair, mask_pair)
    far_device = couple(couple_device, device_table, list_device, mask_device)
    far_top = couple(couple_top, coeff_top, list_top, mask_top)
    local_device = far_device[0] + jnp.dot(
        square(down_device)[0], far_top[0], precision=TOPMOST_PRECISION
    )
    resident_pair_index = far_pair + jnp.einsum(
        "cab,bn->can", square(down_pair), local_device, precision=TOPMOST_PRECISION
    )
    local_leaf = far_leaf + jnp.einsum(
        "pcab,pbn->pcan",
        square(down_leaf).reshape(pair_count, 2, RANK, RANK),
        resident_pair_index,
        precision=TOPMOST_PRECISION,
    ).reshape(leaf_count, RANK, columns)
    return jnp.einsum("lre,lrn->len", col_basis, local_leaf, precision=TOPMOST_PRECISION)


def solution(mesh):
    return jax.shard_map(
        body,
        mesh=mesh,
        in_specs=(
            P(("top", "leaf"), None, None),
            P(("top", "leaf"), None, None),
            P(("top", "leaf"), None),
            P(("top", "leaf"), None),
            P(("top", "leaf"), None),
            P(("top", "leaf"), None, None),
            P(("top", "leaf"), None, None),
            P(("top", "leaf"), None, None),
            P("top", None, None),
            P(("top", "leaf"), None),
            P(("top", "leaf"), None),
            P(("top", "leaf"), None),
            P("top", None),
            P(("top", "leaf"), None),
            P(("top", "leaf"), None),
            P(("top", "leaf"), None),
            P("top", None),
            P(("top", "leaf"), None),
            P(("top", "leaf"), None),
            P(("top", "leaf"), None),
            P(("top", "leaf"), None, None),
        ),
        out_specs=P(("top", "leaf"), None, None),
        check_vma=False,
    )
```

profile of v0, /device:TPU:1, one launch (start us, length us, event | category | flops | bytes accessed | tf_op | source)
XLA Modules:
  0.0 288.7 jit_solution(16151323623756244918)
XLA Ops:
  6.5 0.9 reshape_reshape.6
  7.5 0.8 reshape.277
  8.3 1.9 fusion.169
  10.5 0.9 fusion.170
  11.4 1.3 collective-permute-start.1
  12.7 5.5 %collective-permute-start = (f32[12,32,128]{2,1,0:T(8,128)S(1)}, f32[12,32,128]{2,1,0:T(8,128)S(1)}, u32[]{:S(2)}, u32[]{:S(2)}) collective-permute-start(f32[12,32,128]{2,1,0:T(8,128)S(1)} %pad_maximum_fusion.1), channel_id=1, source_target_pairs={{0,1},{1,2},{2,3},{3,4},{4,5},{5,6},{6,7},{7,8},{8,9},{9,10},{10,1... | collective-permute-start | bytes 589832 | tf_op jit(solution)/shard_map/ppermute | solution.py:17
  18.2 1.5 fusion.167
  30.9 1.5 fusion.165
  39.9 0.8 fusion.164
  40.8 0.7 reshape_squeeze.52
  41.8 1.5 fusion.168
  47.3 0.8 multiply_reduce_fusion.4
  48.8 0.7 mul.315
  49.5 0.7 mul.319
  50.2 0.7 mul.323
  50.8 0.7 mul.327
  51.5 1.5 fusion.166
  55.5 0.9 multiply_reduce_fusion
  57.0 1.3 reduce.94
  58.6 1.4 reduce.95
  60.0 0.7 squeeze_reshape.7
  60.6 0.8 reshape.288
  61.4 0.9 reshape_reshape.7
  62.3 0.9 fusion.163
  63.8 0.9 convolution_bitcast_fusion.4
  64.7 119.1 %psum.7 = f32[1,32,128]{2,1,0:T(8,128)S(1)} all-reduce(f32[1,32,128]{2,1,0:T(8,128)S(1)} %convolution_bitcast_fusion.4), channel_id=1, replica_groups=mesh['top'=16,'leaf'=32] {'leaf'}, use_global_device_ids=true, to_apply=%region_0.4 | all-reduce | flops 4096 | bytes 32768 | tf_op jit(solution)/shard_map/psum | solution.py:94
  183.8 0.7 fusion.138
  188.3 0.7 fusion.121
  192.9 1.7 convert_reduce_fusion.6
  194.6 1.7 convert_reduce_fusion
  196.4 46.5 %all_gather.7 = f32[16,32,128]{2,1,0:T(8,128)S(1)} all-gather(f32[1,32,128]{2,1,0:T(8,128)S(1)} %psum.7), channel_id=1, replica_groups=mesh['top'=16,'leaf'=32] {'top'}, dimensions={0}, use_global_device_ids=true | all-gather | bytes 278528 | tf_op jit(solution)/shard_map/all_gather | solution.py:95
  246.8 0.8 convolution_add_fusion.10
  248.1 0.7 gather_fusion.7
  248.8 1.3 gather_fusion.6
  250.1 1.3 gather_fusion.8
  251.4 1.3 gather_fusion.9
  252.7 1.3 gather_fusion.10
  253.9 1.3 gather_fusion.11
  255.2 0.7 gather_fusion.1
  255.9 0.7 gather_fusion
  256.6 0.7 gather_fusion.2
  257.3 0.7 gather_fusion.3
  258.0 0.7 gather_fusion.4
  258.7 0.7 gather_fusion.5
  259.3 0.9 fusion.22
  260.3 1.1 convolution_add_fusion.9
  261.4 1.1 convolution_add_fusion.8
  262.6 1.1 convolution_add_fusion.7
  263.7 1.1 convolution_add_fusion.6
  264.8 1.1 convolution_add_fusion.5
  265.9 1.0 fusion.9
  266.9 1.0 convolution_add_fusion.4
  267.9 1.0 convolution_add_fusion.3
  268.9 1.0 convolution_add_fusion.2
  269.9 1.0 convolution_add_fusion.1
  270.9 0.9 fusion.77
  271.8 0.9 convolution_add_fusion.17
  272.7 0.9 convolution_add_fusion.16
  273.6 0.9 convolution_add_fusion.15
  274.5 0.9 convolution_add_fusion.14
  275.3 0.9 convolution_add_fusion.13
  276.2 0.9 fusion.4
  277.6 0.9 fusion
  278.5 3.3 %convolution_bitcast_fusion = f32[8,192,128]{2,1,0:T(8,128)} fusion(f32[8,32,128]{2,1,0:T(8,128)S(1)} %fusion, f32[8,32,192]{2,1,0:T(8,128)} %param.49), kind=kOutput, calls=%fused_computation.12 | convolution fusion | flops 75497472 | bytes 1114112 | tf_op jit(solution)/shard_map/lre,lrn->len/dot_general | solution.py:115
  (61 shorter events, 15.6 us)
Async XLA Ops:
  6.5 1.7 copy-start
  6.5 264.4 %all-gather.3.cloned.1.call-start = ((), (), s32[]{:S(2)}) async-start(), calls=%async_computation | async-start | bytes 8404992 | tf_op jit(solution)/shard_map/all_gather | solution.py:48
  11.4 236.6 %collective-permute-start.1 = (f32[12,32,128]{2,1,0:T(8,128)S(1)}, f32[12,32,128]{2,1,0:T(8,128)S(1)}, u32[]{:S(2)}, u32[]{:S(2)}) collective-permute-start(f32[12,32,128]{2,1,0:T(8,128)S(1)} %pad_maximum_fusion.1), channel_id=1, source_target_pairs={{1,0},{2,1},{3,2},{4,3},{5,4},{6,5},{7,6},{8,7},{9,8},{10,9},{11,1... | collective-permute-start | bytes 589832 | tf_op jit(solution)/shard_map/ppermute | solution.py:20
  12.7 235.3 %collective-permute-start = (f32[12,32,128]{2,1,0:T(8,128)S(1)}, f32[12,32,128]{2,1,0:T(8,128)S(1)}, u32[]{:S(2)}, u32[]{:S(2)}) collective-permute-start(f32[12,32,128]{2,1,0:T(8,128)S(1)} %pad_maximum_fusion.1), channel_id=1, source_target_pairs={{0,1},{1,2},{2,3},{3,4},{4,5},{5,6},{6,7},{7,8},{8,9},{9,10},{10,1... | collective-permute-start | bytes 589832 | tf_op jit(solution)/shard_map/ppermute | solution.py:17
Sparse Core Ops, SparseCore 0:
  11.9 133.7 all-gather.2
where the time goes:
time: 291 us; the launch traced here: 289 us
  blocking collectives  166 us (57%)
  between operations  38.8 us (13%)
  local copies, waits for them, and re-layouts  29.4 us (10%)
  matrix products  27.5 us (9%)
  other arithmetic  20.5 us (7%)
  starting transfers between devices  6.75 us (2%)
    psum x1, blocking collectives, body(): own_top = lax.psum(top_term, 'leaf')  119 us
    all_gather x1, blocking collectives, body(): coeff_top = lax.all_gather(own_top[None], 'top', axis=0, tiled=True)  46.5 us
    dot_general x22, matrix products, couple(): jnp.einsum('qup,qpj->quj', quadrature_weight, selected_entries, precision...  18.8 us
    gather x12, local copies, waits for them, and re-layouts, couple(): selected_entries = jnp.take(sources, index[:, slot], axis=0)  11.2 us
    gather x12, other arithmetic  7.17 us
  transfers between devices with their start and end apart: 3, of which 0 were waited for; matrix products, arithmetic and copies ran while one was open for 21% of the time, Pallas kernels for 0%

commit v1 on v0

v1 whole, which is shorter than its diff:
```python
import jax
import jax.numpy as jnp
from jax import lax
from jax.experimental import pallas as pl
from jax.experimental.pallas import tpu as pltpu
from jax.sharding import PartitionSpec as P

RANK = 32
COLS = 128
QUADS = 4
ROWS8 = 8
F32 = jnp.float32
BF16 = jnp.bfloat16
VMEM_LIMIT = 32 * 1024 * 1024
ALMOST_ALL = 60 * 1024 * 1024


def split(x):
    high = x.astype(BF16)
    return high, (x - high.astype(F32)).astype(BF16)


def dot(a, b, contract=((1,), (0,))):
    return lax.dot_general(a, b, (contract, ((), ())), preferred_element_type=F32)


def dot_split(a, b_high, b_low):
    rows = a.shape[0]
    a_high, a_low = split(a)
    both = dot(jnp.concatenate([a_high, a_low], axis=0), b_high)
    return both[:rows] + both[rows:] + dot(a_high, b_low)


def dot_first(a, b):
    a_high, a_low = split(a)
    b_high, b_low = split(b)
    return dot(
        jnp.concatenate([a_high, a_high, a_low], axis=0),
        jnp.concatenate([b_high, b_low, b_high], axis=0),
        ((0,), (0,)),
    )


def lanes(rows=ROWS8):
    return lax.broadcasted_iota(jnp.int32, (rows, COLS), 1)


def square(flat):
    return jnp.concatenate([flat[:, RANK * q : RANK * (q + 1)] for q in range(QUADS)], axis=0)


def beside(flats):
    group = lanes() // RANK
    rows = []
    for q in range(QUADS):
        row = None
        for k, flat in enumerate(flats):
            shift = (RANK * (k - q)) % COLS
            moved = pltpu.roll(flat, shift, 1) if shift else flat
            row = moved if row is None else jnp.where(group == k, moved, row)
        rows.append(row)
    return jnp.concatenate(rows, axis=0)


def quad_rows(ref, start):
    return jnp.concatenate(
        [ref[pl.ds(start + q, ROWS8, stride=QUADS), :] for q in range(QUADS)], axis=0
    )


def store_natural(ref, start, x):
    for q in range(QUADS):
        ref[pl.ds(start + q, ROWS8, stride=QUADS), :] = x[ROWS8 * q : ROWS8 * (q + 1)]


def weights(couple, down, top, list_d, mask_d, list_t, mask_t, natural):
    slots, top_slots = list_d.shape[1], list_t.shape[1]
    flats = [couple[ROWS8 * k : ROWS8 * (k + 1), :] * mask_d[0, k].astype(F32) for k in range(slots)]
    lane = lanes(RANK)
    ids = jnp.zeros((RANK, COLS), F32)
    for k in range(slots):
        ids = jnp.where(lane == 64 + k, list_d[0, k].astype(F32), ids)
    for k in range(top_slots):
        ids = jnp.where(lane == 64 + slots + k, list_t[0, k].astype(F32), ids)
    tops = [
        top[pl.ds(k, ROWS8, stride=top_slots), :] * mask_t[0, k].astype(F32) for k in range(top_slots)
    ]
    store_natural(natural, 0, beside(tops))
    top_high, top_low = split(natural[...])
    return (
        beside(flats[:4]),
        jnp.where(lane < 64, beside(flats[4:]), ids),
        dot_split(square(down[...]), top_high, top_low),
    )


def first_kernel(*refs):
    count = 12
    sources, (weight_ref, stack_ref, send_ref), scratch = refs[:count], refs[count : count + 3], refs[count + 3 :]
    held, (sems, traction, traction_sems, natural) = scratch[:count - 1], scratch[count - 1 :]
    copies = [pltpu.make_async_copy(s, h, sems.at[n]) for n, (s, h) in enumerate(zip(sources[1:], held))]
    leaves = sources[0].shape[0]
    pairs = leaves // 2
    tractions = [
        pltpu.make_async_copy(sources[0].at[i], traction.at[i], traction_sems.at[i]) for i in range(leaves)
    ]
    for copy in copies + tractions:
        copy.start()
    couple, down, top, list_d, mask_d, list_t, mask_t, basis, up_leaf, up_pair, up_device = held
    for copy in copies:
        copy.wait()
    for n, block in enumerate(weights(couple, down, top, list_d, mask_d, list_t, mask_t, natural)):
        for t in range(weight_ref.shape[0]):
            weight_ref[t, RANK * n : RANK * (n + 1), :] = block
    for i in range(leaves):
        tractions[i].wait()
        high, low = split(traction[i])
        stack_ref[RANK * i : RANK * (i + 1), :] = dot_split(basis[i], high, low)
    for p in range(pairs):
        weight = [square(up_leaf[pl.ds(i, ROWS8, stride=leaves), :]) for i in (2 * p, 2 * p + 1)]
        value = [quad_rows(stack_ref, RANK * i) for i in (2 * p, 2 * p + 1)]
        at = RANK * (leaves + p)
        stack_ref[at : at + RANK, :] = dot_first(
            jnp.concatenate(weight, axis=0), jnp.concatenate(value, axis=0)
        )
    weight = [square(up_pair[pl.ds(p, ROWS8, stride=pairs), :]) for p in range(pairs)]
    value = [quad_rows(stack_ref, RANK * (leaves + p)) for p in range(pairs)]
    coeff = dot_first(jnp.concatenate(weight, axis=0), jnp.concatenate(value, axis=0))
    up = up_device[...]
    for z in range(send_ref.shape[0]):
        send_ref[z, 0:RANK, :] = coeff
        send_ref[z, RANK : RANK + ROWS8, :] = up


def far_kernel(
    low_ref, own_ref, high_ref, couple_leaf, couple_pair, down_leaf, down_pair, basis,
    list_leaf, mask_leaf, list_pair, mask_pair, fixed_ref, slope_ref, near_high, near_low, natural,
):
    leaves, slots = list_leaf.shape
    pairs = list_pair.shape[0]
    blocks = leaves + pairs
    top = lax.axis_index("y") * lax.axis_size("core") + lax.axis_index("core")
    leaf = lax.axis_index("x") * lax.axis_size("z") + lax.axis_index("z")
    position = top * (lax.axis_size("x") * lax.axis_size("z")) + leaf
    size = blocks * RANK
    for n, ref in enumerate((low_ref, own_ref, high_ref)):
        high, low = split(ref[...])
        near_high[n * size : (n + 1) * size, :] = high
        near_low[n * size : (n + 1) * size, :] = low
    none = jnp.zeros((RANK, COLS), BF16)
    near_high[3 * size : 3 * size + RANK, :] = none
    near_low[3 * size : 3 * size + RANK, :] = none

    def near(index, mask, per_dev, offset):
        relative = index - position * per_dev + per_dev
        block = relative // per_dev * blocks + offset + relative % per_dev
        start = pl.multiple_of(jnp.where(mask == 0, 3 * blocks, block) * RANK, RANK)
        return near_high[pl.ds(start, RANK), :], near_low[pl.ds(start, RANK), :]

    for p in range(pairs):
        flats = [couple_pair[pl.ds(k * ROWS8 * pairs + p, ROWS8, stride=pairs), :] for k in range(slots)]
        weight = jnp.concatenate([beside(flats[:4]), beside(flats[4:])], axis=1)
        taken = [near(list_pair[p, k], mask_pair[p, k], pairs, leaves) for k in range(slots)]
        rows = [jnp.concatenate([t[n] for t in taken] + [none, none], axis=0) for n in (0, 1)]
        at = 2 * RANK * p
        store_natural(natural, at, dot_split(weight, *rows))
        store_natural(natural, at + RANK, beside([down_pair[pl.ds(p, ROWS8, stride=pairs), :]] * 4))
        sums = split(natural[at : at + RANK, :])
        downs = split(natural[at + RANK : at + 2 * RANK, :])
        for i in (2 * p, 2 * p + 1):
            flats = [
                couple_leaf[pl.ds(k * ROWS8 * leaves + i, ROWS8, stride=leaves), :] for k in range(slots)
            ] + [down_leaf[pl.ds(i, ROWS8, stride=leaves), :]]
            weight = jnp.concatenate([beside(flats[:4]), beside(flats[4:])], axis=1)
            taken = [near(list_leaf[i, k], mask_leaf[i, k], leaves, 0) for k in range(slots)]
            rows = [
                jnp.concatenate(
                    [
                        jnp.concatenate([t[n] for t in taken] + [sums[n], none], axis=0),
                        jnp.concatenate([none] * slots + [downs[n], none], axis=0),
                    ],
                    axis=1,
                )
                for n in (0, 1)
            ]
            here = dot_split(weight, *rows)
            at = 2 * RANK * (pairs + i)
            store_natural(natural, at, here[:, :COLS])
            store_natural(natural, at + RANK, here[:, COLS:])
            here = jnp.concatenate([natural[at : at + RANK, :], natural[at + RANK : at + 2 * RANK, :]], axis=1)
            both = dot_first(basis[i], here)
            fixed_ref[i] = both[:, :COLS]
            slope = both[:, COLS:]
            slope_high = slope.astype(BF16).astype(F32)
            lane = lanes(slope.shape[0])
            slope_ref[i] = jnp.where(
                lane < 64, slope_high, jnp.where(lane < 96, slope - slope_high, 0.0)
            ).astype(BF16)


def part_kernel(*refs):
    buffers = len(refs) - 6
    coeff_refs = refs[:buffers]
    weight_ref, ids_ref, out_ref, coeff_high, coeff_low, gathered = refs[buffers:]
    targets = weight_ref.shape[0]
    across = buffers // 2
    deep = coeff_refs[0].shape[0]
    subs = across * deep
    slots, top_slots = 6, 4
    row, core, here = lax.axis_index("y"), lax.axis_index("core"), lax.axis_index("x")
    none = jnp.zeros((RANK, COLS), BF16)
    blocks = [(ref, z) for ref in coeff_refs for z in range(deep)]
    for d, (ref, z) in enumerate(blocks):
        value = ref[z, 0:RANK, :]
        gathered[RANK * d : RANK * (d + 1), :] = value
        high, low = split(value)
        coeff_high[RANK * d : RANK * (d + 1), :] = high
        coeff_low[RANK * d : RANK * (d + 1), :] = low
    coeff_high[2 * RANK * subs : RANK * (2 * subs + 1), :] = none
    coeff_low[2 * RANK * subs : RANK * (2 * subs + 1), :] = none
    tops = []
    for g in range(2):
        up = jnp.concatenate(
            [ref[z, RANK : RANK + ROWS8, :] for ref, z in blocks[g * subs : (g + 1) * subs]], axis=0
        )
        value = jnp.concatenate(
            [
                gathered[pl.ds(RANK * subs * g + q, ROWS8 * subs, stride=QUADS), :]
                for q in range(QUADS)
            ],
            axis=1,
        )
        every = dot_first(up, value)
        top = jnp.zeros((RANK, COLS), F32)
        for q in range(QUADS):
            top = top + every[RANK * q : RANK * (q + 1), COLS * q : COLS * (q + 1)]
        tops.append(split(top))
    lane_group = lanes(RANK) // RANK
    top_weight = []
    for t in range(targets):
        used = [jnp.zeros((RANK, COLS), F32)] * 2
        for k in range(top_slots):
            owner = ids_ref[t, 64 + slots + k].astype(jnp.int32)
            for g in range(2):
                group = row * 2 + (core if g == 0 else 1 - core)
                used[g] = jnp.where(lane_group == k, jnp.where(owner == group, 1.0, 0.0), used[g])
        block = weight_ref[t, 2 * RANK : 3 * RANK, :]
        top_weight.append(jnp.concatenate([block * used[0], block * used[1]], axis=1))
    top_part = dot_split(
        jnp.concatenate(top_weight, axis=0),
        jnp.concatenate([tops[0][0]] * 4 + [tops[1][0]] * 4, axis=0),
        jnp.concatenate([tops[0][1]] * 4 + [tops[1][1]] * 4, axis=0),
    )

    def starts(t):
        found = []
        for k in range(slots):
            index = ids_ref[t, 64 + k].astype(jnp.int32)
            group, sub = index // subs, index % subs
            place = (here + across - sub // deep) % across * deep + sub % deep
            place = place + jnp.where(group % 2 == core, 0, subs)
            block = jnp.where(group // 2 == row, place, 2 * subs)
            found.append(pl.multiple_of(block * RANK, RANK))
        return found

    for t in range(0, targets, 2):
        pair = [starts(t), starts(t + 1)]
        rows = [
            jnp.concatenate(
                [jnp.concatenate([ref[pl.ds(s, RANK), :] for s in one], axis=0) for one in pair], axis=1
            )
            for ref in (coeff_high, coeff_low)
        ]
        weight = [
            jnp.concatenate([weight_ref[u, 0:RANK, :], weight_ref[u, RANK : 2 * RANK, :64]], axis=1)
            for u in (t, t + 1)
        ]
        both = dot_split(jnp.concatenate(weight, axis=0), *rows)
        out_ref[t] = both[:RANK, :COLS] + top_part[RANK * t : RANK * (t + 1)]
        out_ref[t + 1] = both[RANK:, COLS:] + top_part[RANK * (t + 1) : RANK * (t + 2)]


def last_kernel(parts_ref, fixed_ref, slope_ref, out_ref, natural):
    total = parts_ref[0]
    for t in range(1, parts_ref.shape[0]):
        total = total + parts_ref[t]
    store_natural(natural, 0, total)
    high, low = split(natural[...])
    rows = jnp.concatenate([high, low, high, jnp.zeros((RANK, COLS), BF16)], axis=0)
    for i in range(out_ref.shape[0]):
        out_ref[i] = fixed_ref[i] + dot(slope_ref[i], rows)


def whole(kernel, out, args, smem=(), hbm=(), scratch=(), flops=0, limit=VMEM_LIMIT):
    vmem = pl.BlockSpec(memory_space=pltpu.VMEM)
    scalars = pl.BlockSpec(memory_space=pltpu.SMEM)
    far = pl.BlockSpec(memory_space=pltpu.HBM)
    size = sum(a.size * a.dtype.itemsize for a in args)
    outs = out if isinstance(out, tuple) else (out,)
    size += sum(o.size * o.dtype.itemsize for o in outs)
    return pl.pallas_call(
        kernel,
        out_shape=out,
        in_specs=[scalars if n in smem else far if n in hbm else vmem for n in range(len(args))],
        out_specs=tuple(vmem for _ in out) if isinstance(out, tuple) else vmem,
        scratch_shapes=list(scratch),
        compiler_params=pltpu.CompilerParams(vmem_limit_bytes=limit),
        cost_estimate=pl.CostEstimate(flops=flops, bytes_accessed=size, transcendentals=0),
    )(*args)


def rows_of(x):
    if x.ndim == 2:
        return x.reshape(x.shape[0], ROWS8, COLS).transpose(1, 0, 2).reshape(-1, COLS)
    return x.reshape(x.shape[0], x.shape[1], ROWS8, COLS).transpose(1, 2, 0, 3).reshape(-1, COLS)


def body(
    traction_vectors,
    row_basis,
    up_leaf,
    up_pair,
    up_device,
    couple_leaf,
    pair_coupling_blocks,
    couple_device,
    couple_top,
    list_leaf,
    list_pair,
    list_device,
    list_top,
    mask_leaf,
    mask_pair,
    mask_device,
    mask_top,
    down_leaf,
    down_pair,
    down_device,
    col_basis,
):
    def shape(*dims, dtype=F32):
        return jax.ShapeDtypeStruct(dims, dtype)

    leaves, entries, _ = traction_vectors.shape
    blocks = leaves + leaves // 2
    across, deep = lax.axis_size("x"), lax.axis_size("z")
    targets = lax.axis_size("y")
    subs = across * deep
    first = (
        traction_vectors, rows_of(couple_device), rows_of(down_device), rows_of(couple_top[0]),
        list_device, mask_device, list_top, mask_top,
        row_basis, rows_of(up_leaf), rows_of(up_pair), rows_of(up_device),
    )
    scalars = (4, 5, 6, 7)
    held = [
        (pltpu.SMEM if n in scalars else pltpu.VMEM)(a.shape, a.dtype) for n, a in enumerate(first) if n
    ]
    weights, stack, send = whole(
        first_kernel,
        (shape(targets, 3 * RANK, COLS), shape(blocks * RANK, COLS), shape(deep, RANK + ROWS8, COLS)),
        first,
        hbm=range(len(first)),
        scratch=[
            *held,
            pltpu.SemaphoreType.DMA((len(held),)),
            pltpu.VMEM(traction_vectors.shape, F32),
            pltpu.SemaphoreType.DMA((leaves,)),
            pltpu.VMEM((RANK, COLS), F32),
        ],
        flops=6 * 10**7,
        limit=ALMOST_ALL,
    )
    weights = lax.all_to_all(weights, "y", 0, 0, tiled=True)
    coeffs = lax.all_to_all(send, "z", 0, 0, tiled=True)
    coeffs = [coeffs] + [
        lax.ppermute(coeffs, "x", [(i, (i + step) % across) for i in range(across)])
        for step in range(1, across)
    ]
    coeffs[-1], stack = lax.optimization_barrier((coeffs[-1], stack))
    coeffs = coeffs + [lax.ppermute(block, "core", [(0, 1), (1, 0)]) for block in coeffs]
    leaf_axes = ("x", "z")
    low = lax.ppermute(stack, leaf_axes, [(i, i + 1) for i in range(subs - 1)])
    high = lax.ppermute(stack, leaf_axes, [(i + 1, i) for i in range(subs - 1)])
    near = pltpu.VMEM(((3 * blocks + 1) * RANK, COLS), BF16)
    fixed, slope = whole(
        far_kernel,
        (shape(leaves, entries, COLS), shape(leaves, entries, COLS, dtype=BF16)),
        (
            low, stack, high, rows_of(couple_leaf), rows_of(pair_coupling_blocks),
            rows_of(down_leaf), rows_of(down_pair), col_basis,
            list_leaf, mask_leaf, list_pair, mask_pair,
        ),
        smem=(8, 9, 10, 11),
        scratch=[near, near, pltpu.VMEM((2 * RANK * blocks, COLS), F32)],
        flops=10**8,
    )
    parts = whole(
        part_kernel,
        shape(targets, RANK, COLS),
        (*coeffs, weights, weights[:, RANK, :]),
        smem=(2 * across + 1,),
        scratch=[
            pltpu.VMEM(((2 * subs + 1) * RANK, COLS), BF16),
            pltpu.VMEM(((2 * subs + 1) * RANK, COLS), BF16),
            pltpu.VMEM((2 * subs * RANK, COLS), F32),
        ],
        flops=10**8,
    )
    parts = lax.all_to_all(parts, "y", 0, 0, tiled=True)
    return whole(
        last_kernel,
        shape(leaves, entries, COLS),
        (parts, fixed, slope),
        scratch=[pltpu.VMEM((RANK, COLS), F32)],
        flops=5 * 10**7,
    )


def solution(mesh):
    deep = max(1, mesh.shape["leaf"] // 4)
    sizes = (mesh.shape["top"] // 2, 2, mesh.shape["leaf"] // deep, deep)
    fine = jax.sharding.Mesh(mesh.devices.reshape(sizes), ("y", "core", "x", "z"))
    top, both = ("y", "core"), ("y", "core", "x", "z")
    return jax.shard_map(
        body,
        mesh=fine,
        in_specs=(
            P(both, None, None),
            P(both, None, None),
            P(both, None),
            P(both, None),
            P(both, None),
            P(both, None, None),
            P(both, None, None),
            P(both, None, None),
            P(top, None, None),
            P(both, None),
            P(both, None),
            P(both, None),
            P(top, None),
            P(both, None),
            P(both, None),
            P(both, None),
            P(top, None),
            P(both, None),
            P(both, None),
            P(both, None),
            P(both, None, None),
        ),
        out_specs=P(both, None, None),
        check_vma=False,
    )
```

time: 291 us -> 79.8 us (0.27)
  the two profiles are of different devices: /device:TPU:1 before, /device:TPU:10 now
where the time goes in v1:
time: 79.8 us; the launch traced here: 79.1 us
  starting transfers between devices  40 us (50%)
  blocking collectives  20.1 us (25%)
  Pallas kernels  10.5 us (13%)
  waiting for transfers between devices  7.65 us (10%)
    all_to_all x1, blocking collectives, body(): coeffs = lax.all_to_all(send, 'z', 0, 0, tiled=True)  20.1 us
    ppermute x3, starting transfers between devices, body(): lax.ppermute(coeffs, 'x', [(i, (i + step) % across) for i in range(across)])  10.5 us
    pallas_call x4, Pallas kernels, whole(): pl.pallas_call(kernel, out_shape=out, in_specs=[scalars if n in smem else...  10.5 us
    ppermute x4, starting transfers between devices, body(): lax.ppermute(block, 'core', [(0, 1), (1, 0)])  8.65 us
    all_to_all x1, starting transfers between devices, body(): weights = lax.all_to_all(weights, 'y', 0, 0, tiled=True)  7.55 us
    all_to_all x1, starting transfers between devices, body(): parts = lax.all_to_all(parts, 'y', 0, 0, tiled=True)  7.36 us
    ppermute x1, waiting for transfers between devices, body(): low = lax.ppermute(stack, leaf_axes, [(i, i + 1) for i in range(subs - 1)])  4.04 us
    ppermute x1, starting transfers between devices, body(): low = lax.ppermute(stack, leaf_axes, [(i, i + 1) for i in range(subs - 1)])  3.92 us
  transfers between devices with their start and end apart: 11, of which 3 were waited for; matrix products, arithmetic and copies ran while one was open for 0% of the time, Pallas kernels for 3%

profile of v1, /device:TPU:10, one launch (start us, length us, event | category | flops | bytes accessed | tf_op | source)
XLA Modules:
  0.0 79.1 jit_solution(3268226100269870389)
XLA Ops:
  0.0 3.9 %shard_map.199 = (f32[8,96,128]{2,1,0:T(8,128)}, f32[384,128]{1,0:T(8,128)}, f32[8,40,128]{2,1,0:T(8,128)}) custom-call(f32[8,192,128]{2,1,0:T(8,128)} %refs_0_.1, f32[48,128]{1,0:T(8,128)} %bitcast.47, f32[8,128]{1,0:T(8,128)} %bitcast.50, f32[32,128]{1,0:T(8,128)} %bitcast.48, s32[1,6]{1,0:T(1,128)} %refs_4_.1, s32[1,6]{1,0:T(1,128)} %refs_5_.1, ...), custom_call_target="tpu_custom_call" | custom-call | flops 60000000 | bytes 1835088 | tf_op jit(solution)/shard_map/pallas_call | solution.py:301
  4.0 20.1 %all_to_all.15.refs_0_ = f32[8,40,128]{2,1,0:T(8,128)S(1)} all-to-all(f32[8,40,128]{2,1,0:T(8,128)} %get-tuple-element.12), channel_id=1, replica_groups=mesh['y'=8,'core'=2,'x'=4,'z'=8] {'z'}, dimensions={0} | all-to-all | bytes 327680 | tf_op jit(solution)/shard_map/all_to_all | solution.py:374
  24.0 7.5 %all-to-all-start.1 = ((f32[8,96,128]{2,1,0:T(8,128)}), f32[8,96,128]{2,1,0:T(8,128)S(1)}, u32[]{:S(2)}, u32[]{:S(2)}) async-start(f32[8,96,128]{2,1,0:T(8,128)} %get-tuple-element.15), calls=%async_computation.1 | async-start | bytes 786432 | tf_op jit(solution)/shard_map/all_to_all | solution.py:373
  31.6 2.4 %collective-permute-start.2 = (f32[8,40,128]{2,1,0:T(8,128)S(1)}, f32[8,40,128]{2,1,0:T(8,128)S(1)}, u32[]{:S(2)}, u32[]{:S(2)}) collective-permute-start(f32[8,40,128]{2,1,0:T(8,128)S(1)} %all_to_all.15.refs_0_), channel_id=1, source_target_pairs={{0,24},{8,0},{16,8},{24,16},{1,25},{9,1},{17,9},{25,17},{2,26},{10... | collective-permute-start | bytes 491528 | tf_op jit(solution)/shard_map/ppermute | solution.py:376
  34.0 4.3 %collective-permute-start.1 = (f32[8,40,128]{2,1,0:T(8,128)S(1)}, f32[8,40,128]{2,1,0:T(8,128)S(1)}, u32[]{:S(2)}, u32[]{:S(2)}) collective-permute-start(f32[8,40,128]{2,1,0:T(8,128)S(1)} %all_to_all.15.refs_0_), channel_id=1, source_target_pairs={{0,16},{8,24},{16,0},{24,8},{1,17},{9,25},{17,1},{25,9},{2,18},{10... | collective-permute-start | bytes 491528 | tf_op jit(solution)/shard_map/ppermute | solution.py:376
  38.4 3.7 %collective-permute-start = (f32[8,40,128]{2,1,0:T(8,128)S(1)}, f32[8,40,128]{2,1,0:T(8,128)S(1)}, u32[]{:S(2)}, u32[]{:S(2)}) collective-permute-start(f32[8,40,128]{2,1,0:T(8,128)S(1)} %all_to_all.15.refs_0_), channel_id=1, source_target_pairs={{0,8},{8,16},{16,24},{24,0},{1,9},{9,17},{17,25},{25,1},{2,10},{10... | collective-permute-start | bytes 491528 | tf_op jit(solution)/shard_map/ppermute | solution.py:376
  42.1 1.9 %collective-permute-start.3 = (f32[8,40,128]{2,1,0:T(8,128)S(1)}, f32[8,40,128]{2,1,0:T(8,128)S(1)}, u32[]{:S(2)}, u32[]{:S(2)}) collective-permute-start(f32[8,40,128]{2,1,0:T(8,128)S(1)} %all_to_all.15.refs_0_), channel_id=1, source_target_pairs={{0,32},{32,0},{1,33},{33,1},{2,34},{34,2},{3,35},{35,3},{4,36},{36... | collective-permute-start | bytes 491528 | tf_op jit(solution)/shard_map/ppermute | solution.py:380
  44.0 0.0 collective-permute-done.2.refs_3_
  44.0 2.4 %collective-permute-start.6 = (f32[8,40,128]{2,1,0:T(8,128)S(1)}, f32[8,40,128]{2,1,0:T(8,128)S(1)}, u32[]{:S(2)}, u32[]{:S(2)}) collective-permute-start(f32[8,40,128]{2,1,0:T(8,128)S(1)} %collective-permute-done.2.refs_3_), channel_id=1, source_target_pairs={{0,32},{32,0},{1,33},{33,1},{2,34},{34,2},{3,35},{35,3},{4,36},{36... | collective-permute-start | bytes 491528 | tf_op jit(solution)/shard_map/ppermute | solution.py:380
  46.4 0.0 collective-permute-done.1.refs_2_
  46.4 1.9 %collective-permute-start.5 = (f32[8,40,128]{2,1,0:T(8,128)S(1)}, f32[8,40,128]{2,1,0:T(8,128)S(1)}, u32[]{:S(2)}, u32[]{:S(2)}) collective-permute-start(f32[8,40,128]{2,1,0:T(8,128)S(1)} %collective-permute-done.1.refs_2_), channel_id=1, source_target_pairs={{0,32},{32,0},{1,33},{33,1},{2,34},{34,2},{3,35},{35,3},{4,36},{36... | collective-permute-start | bytes 491528 | tf_op jit(solution)/shard_map/ppermute | solution.py:380
  48.4 0.0 collective-permute-done.refs_1_
  48.4 2.4 %collective-permute-start.4 = (f32[8,40,128]{2,1,0:T(8,128)S(1)}, f32[8,40,128]{2,1,0:T(8,128)S(1)}, u32[]{:S(2)}, u32[]{:S(2)}) collective-permute-start(f32[8,40,128]{2,1,0:T(8,128)S(1)} %collective-permute-done.refs_1_), channel_id=1, source_target_pairs={{0,32},{32,0},{1,33},{33,1},{2,34},{34,2},{3,35},{35,3},{4,36},{36... | collective-permute-start | bytes 491528 | tf_op jit(solution)/shard_map/ppermute | solution.py:380
  50.8 0.0 all-to-all-done.1.refs_8_
  50.8 0.0 collective-permute-done.3.refs_4_
  50.8 0.0 collective-permute-done.6.refs_7_
  50.8 0.0 collective-permute-done.5.refs_6_
  50.9 0.9 %collective-permute-done.4.refs_5_ = f32[8,40,128]{2,1,0:T(8,128)S(1)} collective-permute-done((f32[8,40,128]{2,1,0:T(8,128)S(1)}, f32[8,40,128]{2,1,0:T(8,128)S(1)}, u32[]{:S(2)}, u32[]{:S(2)}) %collective-permute-start.4) | collective-permute-done | bytes 163872 | tf_op jit(solution)/shard_map/ppermute | solution.py:380
  51.8 0.0 copy-start.2
  51.8 0.0 copy-start.1
  51.8 0.0 copy-start.3
  51.8 0.0 copy-start.4
  51.8 0.0 copy-start.5
  51.8 0.0 copy-start.7
  51.8 0.0 copy-start.9
  51.8 3.0 %shard_map.200 = f32[8,32,128]{2,1,0:T(8,128)} custom-call(f32[8,40,128]{2,1,0:T(8,128)S(1)} %all_to_all.15.refs_0_, f32[8,40,128]{2,1,0:T(8,128)S(1)} %collective-permute-done.refs_1_, f32[8,40,128]{2,1,0:T(8,128)S(1)} %collective-permute-done.1.refs_2_, f32[8,40,128]{2,1,0:T(8,128)S(1)} %collective-permute-done.2.refs_3_, ...), custom_call_target="tpu_custom_call" | custom-call | flops 100000000 | bytes 1839104 | tf_op jit(solution)/shard_map/pallas_call | solution.py:301
  54.8 0.0 copy-start
  54.8 7.4 %all-to-all-start.2 = ((f32[8,32,128]{2,1,0:T(8,128)}), f32[8,32,128]{2,1,0:T(8,128)S(1)}, u32[]{:S(2)}, u32[]{:S(2)}) async-start(f32[8,32,128]{2,1,0:T(8,128)} %shard_map.200), calls=%async_computation.2 | async-start | bytes 262144 | tf_op jit(solution)/shard_map/all_to_all | solution.py:409
  62.2 0.0 copy-done.2
  62.2 0.0 copy-start.6
  62.2 2.0 %collective-permute-start.8 = (f32[384,128]{1,0:T(8,128)S(1)}, f32[384,128]{1,0:T(8,128)S(1)}, u32[]{:S(2)}, u32[]{:S(2)}) collective-permute-start(f32[384,128]{1,0:T(8,128)S(1)} %copy-done.2), channel_id=1, source_target_pairs={{1,0},{2,1},{3,2},{4,3},{5,4},{6,5},{7,6},{8,7},{9,8},{10,9},{11,1... | collective-permute-start | bytes 589832 | tf_op jit(solution)/shard_map/ppermute | solution.py:383
  64.2 3.9 %collective-permute-start.7 = (f32[384,128]{1,0:T(8,128)S(1)}, f32[384,128]{1,0:T(8,128)S(1)}, u32[]{:S(2)}, u32[]{:S(2)}) collective-permute-start(f32[384,128]{1,0:T(8,128)S(1)} %copy-done.2), channel_id=1, source_target_pairs={{0,1},{1,2},{2,3},{3,4},{4,5},{5,6},{6,7},{7,8},{8,9},{9,10},{10,1... | collective-permute-start | bytes 589832 | tf_op jit(solution)/shard_map/ppermute | solution.py:382
  68.2 2.6 %collective-permute-done.8.high_ref = f32[384,128]{1,0:T(8,128)S(1)} collective-permute-done((f32[384,128]{1,0:T(8,128)S(1)}, f32[384,128]{1,0:T(8,128)S(1)}, u32[]{:S(2)}, u32[]{:S(2)}) %collective-permute-start.8) | collective-permute-done | bytes 196640 | tf_op jit(solution)/shard_map/ppermute | solution.py:383
  70.8 4.0 %collective-permute-done.7.low_ref = f32[384,128]{1,0:T(8,128)S(1)} collective-permute-done((f32[384,128]{1,0:T(8,128)S(1)}, f32[384,128]{1,0:T(8,128)S(1)}, u32[]{:S(2)}, u32[]{:S(2)}) %collective-permute-start.7) | collective-permute-done | bytes 196640 | tf_op jit(solution)/shard_map/ppermute | solution.py:382
  74.9 0.0 copy-start.8
  74.9 0.0 copy-done.1
  74.9 0.0 copy-done.3
  74.9 0.0 copy-done.4
  74.9 0.0 copy-done.5
  74.9 0.0 copy-done.7
  74.9 0.0 copy-done.9
  74.9 0.0 copy-done
  74.9 0.0 copy-done.6
  74.9 0.6 copy-done.8
  75.5 2.4 %shard_map.201 = (f32[8,192,128]{2,1,0:T(8,128)S(1)}, bf16[8,192,128]{2,1,0:T(8,128)(2,1)S(1)}) custom-call(f32[384,128]{1,0:T(8,128)S(1)} %collective-permute-done.7.low_ref, f32[384,128]{1,0:T(8,128)S(1)} %copy-done.2, f32[384,128]{1,0:T(8,128)S(1)} %collective-permute-done.8.high_ref, f32[384,128]{1,0:T(8,128)S(1)} %bitcast.41, f32[192,128]{1,0:T(8,128)S(1)} %bitcast.42, ...), custom_call_target="tpu_custom_call" | custom-call | flops 100000000 | bytes 2310720 | tf_op jit(solution)/shard_map/pallas_call | solution.py:301
  77.9 0.0 all-to-all-done.2.parts_ref
  77.9 1.1 %shard_map.202 = f32[8,192,128]{2,1,0:T(8,128)} custom-call(f32[8,32,128]{2,1,0:T(8,128)S(1)} %all-to-all-done.2.parts_ref, f32[8,192,128]{2,1,0:T(8,128)S(1)} %get-tuple-element.17.fixed_ref, bf16[8,192,128]{2,1,0:T(8,128)(2,1)S(1)} %get-tuple-element.18.slope_ref), custom_call_target="tpu_custom_call" | custom-call | flops 50000000 | bytes 2097152 | tf_op jit(solution)/shard_map/pallas_call | solution.py:301
  (1 shorter events, 0.0 us)
Async XLA Ops:
  24.0 26.8 %all-to-all-start.1 = ((f32[8,96,128]{2,1,0:T(8,128)}), f32[8,96,128]{2,1,0:T(8,128)S(1)}, u32[]{:S(2)}, u32[]{:S(2)}) async-start(f32[8,96,128]{2,1,0:T(8,128)} %get-tuple-element.15), calls=%async_computation.1 | async-start | bytes 786432 | tf_op jit(solution)/shard_map/all_to_all | solution.py:373
  31.6 12.4 %collective-permute-start.2 = (f32[8,40,128]{2,1,0:T(8,128)S(1)}, f32[8,40,128]{2,1,0:T(8,128)S(1)}, u32[]{:S(2)}, u32[]{:S(2)}) collective-permute-start(f32[8,40,128]{2,1,0:T(8,128)S(1)} %all_to_all.15.refs_0_), channel_id=1, source_target_pairs={{0,24},{8,0},{16,8},{24,16},{1,25},{9,1},{17,9},{25,17},{2,26},{10... | collective-permute-start | bytes 491528 | tf_op jit(solution)/shard_map/ppermute | solution.py:376
  34.0 12.4 %collective-permute-start.1 = (f32[8,40,128]{2,1,0:T(8,128)S(1)}, f32[8,40,128]{2,1,0:T(8,128)S(1)}, u32[]{:S(2)}, u32[]{:S(2)}) collective-permute-start(f32[8,40,128]{2,1,0:T(8,128)S(1)} %all_to_all.15.refs_0_), channel_id=1, source_target_pairs={{0,16},{8,24},{16,0},{24,8},{1,17},{9,25},{17,1},{25,9},{2,18},{10... | collective-permute-start | bytes 491528 | tf_op jit(solution)/shard_map/ppermute | solution.py:376
  38.4 10.0 %collective-permute-start = (f32[8,40,128]{2,1,0:T(8,128)S(1)}, f32[8,40,128]{2,1,0:T(8,128)S(1)}, u32[]{:S(2)}, u32[]{:S(2)}) collective-permute-start(f32[8,40,128]{2,1,0:T(8,128)S(1)} %all_to_all.15.refs_0_), channel_id=1, source_target_pairs={{0,8},{8,16},{16,24},{24,0},{1,9},{9,17},{17,25},{25,1},{2,10},{10... | collective-permute-start | bytes 491528 | tf_op jit(solution)/shard_map/ppermute | solution.py:376
  42.1 8.7 %collective-permute-start.3 = (f32[8,40,128]{2,1,0:T(8,128)S(1)}, f32[8,40,128]{2,1,0:T(8,128)S(1)}, u32[]{:S(2)}, u32[]{:S(2)}) collective-permute-start(f32[8,40,128]{2,1,0:T(8,128)S(1)} %all_to_all.15.refs_0_), channel_id=1, source_target_pairs={{0,32},{32,0},{1,33},{33,1},{2,34},{34,2},{3,35},{35,3},{4,36},{36... | collective-permute-start | bytes 491528 | tf_op jit(solution)/shard_map/ppermute | solution.py:380
  44.0 6.8 %collective-permute-start.6 = (f32[8,40,128]{2,1,0:T(8,128)S(1)}, f32[8,40,128]{2,1,0:T(8,128)S(1)}, u32[]{:S(2)}, u32[]{:S(2)}) collective-permute-start(f32[8,40,128]{2,1,0:T(8,128)S(1)} %collective-permute-done.2.refs_3_), channel_id=1, source_target_pairs={{0,32},{32,0},{1,33},{33,1},{2,34},{34,2},{3,35},{35,3},{4,36},{36... | collective-permute-start | bytes 491528 | tf_op jit(solution)/shard_map/ppermute | solution.py:380
  46.4 4.4 %collective-permute-start.5 = (f32[8,40,128]{2,1,0:T(8,128)S(1)}, f32[8,40,128]{2,1,0:T(8,128)S(1)}, u32[]{:S(2)}, u32[]{:S(2)}) collective-permute-start(f32[8,40,128]{2,1,0:T(8,128)S(1)} %collective-permute-done.1.refs_2_), channel_id=1, source_target_pairs={{0,32},{32,0},{1,33},{33,1},{2,34},{34,2},{3,35},{35,3},{4,36},{36... | collective-permute-start | bytes 491528 | tf_op jit(solution)/shard_map/ppermute | solution.py:380
  48.4 3.4 %collective-permute-start.4 = (f32[8,40,128]{2,1,0:T(8,128)S(1)}, f32[8,40,128]{2,1,0:T(8,128)S(1)}, u32[]{:S(2)}, u32[]{:S(2)}) collective-permute-start(f32[8,40,128]{2,1,0:T(8,128)S(1)} %collective-permute-done.refs_1_), channel_id=1, source_target_pairs={{0,32},{32,0},{1,33},{33,1},{2,34},{34,2},{3,35},{35,3},{4,36},{36... | collective-permute-start | bytes 491528 | tf_op jit(solution)/shard_map/ppermute | solution.py:380
  51.8 10.4 %copy-start.2 = (f32[384,128]{1,0:T(8,128)S(1)}, f32[384,128]{1,0:T(8,128)}, u32[]{:S(2)}) copy-start(f32[384,128]{1,0:T(8,128)} %get-tuple-element.16.own_ref) | copy-start | bytes 589828
  51.8 23.1 %copy-start.1 = (f32[8,6,1024]{2,0,1:T(8,128)S(1)}, f32[8,6,1024]{2,0,1:T(8,128)}, u32[]{:S(2)}) copy-start(f32[8,6,1024]{2,0,1:T(8,128)} %param.26) | copy-start | bytes 589828
  51.8 23.1 %copy-start.3 = (f32[4,6,1024]{2,0,1:T(4,128)S(1)}, f32[4,6,1024]{2,0,1:T(4,128)}, u32[]{:S(2)}) copy-start(f32[4,6,1024]{2,0,1:T(4,128)} %param.27) | copy-start | bytes 294916
  51.8 23.1 %copy-start.4 = (f32[8,1024]{1,0:T(8,128)S(1)}, f32[8,1024]{1,0:T(8,128)}, u32[]{:S(2)}) copy-start(f32[8,1024]{1,0:T(8,128)} %param.38) | copy-start | bytes 98308
  51.8 23.1 %copy-start.5 = (f32[4,1024]{1,0:T(4,128)S(1)}, f32[4,1024]{1,0:T(4,128)}, u32[]{:S(2)}) copy-start(f32[4,1024]{1,0:T(4,128)} %param.39) | copy-start | bytes 49156
  51.8 23.1 %copy-start.7 = (s32[8,6]{1,0:T(8,128)S(1)}, s32[8,6]{1,0:T(8,128)}, u32[]{:S(2)}) copy-start(s32[8,6]{1,0:T(8,128)} %mask_leaf.1) | copy-start | bytes 580
  51.8 23.1 %copy-start.9 = (s32[4,6]{1,0:T(4,128)S(1)}, s32[4,6]{1,0:T(4,128)}, u32[]{:S(2)}) copy-start(s32[4,6]{1,0:T(4,128)} %mask_pair.1) | copy-start | bytes 292
  54.8 20.1 %copy-start = (f32[8,32,192]{2,1,0:T(8,128)S(1)}, f32[8,32,192]{2,1,0:T(8,128)}, u32[]{:S(2)}) copy-start(f32[8,32,192]{2,1,0:T(8,128)} %basis.1) | copy-start | bytes 589828
  54.8 23.1 %all-to-all-start.2 = ((f32[8,32,128]{2,1,0:T(8,128)}), f32[8,32,128]{2,1,0:T(8,128)S(1)}, u32[]{:S(2)}, u32[]{:S(2)}) async-start(f32[8,32,128]{2,1,0:T(8,128)} %shard_map.200), calls=%async_computation.2 | async-start | bytes 262144 | tf_op jit(solution)/shard_map/all_to_all | solution.py:409
  62.2 12.7 %copy-start.6 = (s32[8,6]{1,0:T(8,128)S(1)}, s32[8,6]{1,0:T(8,128)}, u32[]{:S(2)}) copy-start(s32[8,6]{1,0:T(8,128)} %list_leaf.1) | copy-start | bytes 580
  62.2 8.6 %collective-permute-start.8 = (f32[384,128]{1,0:T(8,128)S(1)}, f32[384,128]{1,0:T(8,128)S(1)}, u32[]{:S(2)}, u32[]{:S(2)}) collective-permute-start(f32[384,128]{1,0:T(8,128)S(1)} %copy-done.2), channel_id=1, source_target_pairs={{1,0},{2,1},{3,2},{4,3},{5,4},{6,5},{7,6},{8,7},{9,8},{10,9},{11,1... | collective-permute-start | bytes 589832 | tf_op jit(solution)/shard_map/ppermute | solution.py:383
  64.2 10.6 %collective-permute-start.7 = (f32[384,128]{1,0:T(8,128)S(1)}, f32[384,128]{1,0:T(8,128)S(1)}, u32[]{:S(2)}, u32[]{:S(2)}) collective-permute-start(f32[384,128]{1,0:T(8,128)S(1)} %copy-done.2), channel_id=1, source_target_pairs={{0,1},{1,2},{2,3},{3,4},{4,5},{5,6},{6,7},{7,8},{8,9},{9,10},{10,1... | collective-permute-start | bytes 589832 | tf_op jit(solution)/shard_map/ppermute | solution.py:382
  74.9 0.7 copy-start.8

commit v2 on v1

--- a/solution.py
+++ b/solution.py
@@ -198,73 +198,58 @@
             ).astype(BF16)
 
 
-def part_kernel(*refs):
-    buffers = len(refs) - 6
-    coeff_refs = refs[:buffers]
-    weight_ref, ids_ref, out_ref, coeff_high, coeff_low, gathered = refs[buffers:]
-    targets = weight_ref.shape[0]
-    across = buffers // 2
-    deep = coeff_refs[0].shape[0]
-    subs = across * deep
+def part_kernel(
+    coeff_ref, weight_own, weight_other, ids_own, ids_other, out_ref, coeff_high, coeff_low, gathered
+):
+    rows_y = weight_own.shape[0]
+    subs = coeff_ref.shape[0]
     slots, top_slots = 6, 4
-    row, core, here = lax.axis_index("y"), lax.axis_index("core"), lax.axis_index("x")
+    core = lax.axis_index("core")
+    group = lax.axis_index("y") * 2 + core
     none = jnp.zeros((RANK, COLS), BF16)
-    blocks = [(ref, z) for ref in coeff_refs for z in range(deep)]
-    for d, (ref, z) in enumerate(blocks):
-        value = ref[z, 0:RANK, :]
+    for d in range(subs):
+        value = coeff_ref[d, 0:RANK, :]
         gathered[RANK * d : RANK * (d + 1), :] = value
         high, low = split(value)
         coeff_high[RANK * d : RANK * (d + 1), :] = high
         coeff_low[RANK * d : RANK * (d + 1), :] = low
-    coeff_high[2 * RANK * subs : RANK * (2 * subs + 1), :] = none
-    coeff_low[2 * RANK * subs : RANK * (2 * subs + 1), :] = none
-    tops = []
-    for g in range(2):
-        up = jnp.concatenate(
-            [ref[z, RANK : RANK + ROWS8, :] for ref, z in blocks[g * subs : (g + 1) * subs]], axis=0
-        )
-        value = jnp.concatenate(
-            [
-                gathered[pl.ds(RANK * subs * g + q, ROWS8 * subs, stride=QUADS), :]
-                for q in range(QUADS)
-            ],
-            axis=1,
-        )
-        every = dot_first(up, value)
-        top = jnp.zeros((RANK, COLS), F32)
-        for q in range(QUADS):
-            top = top + every[RANK * q : RANK * (q + 1), COLS * q : COLS * (q + 1)]
-        tops.append(split(top))
+    coeff_high[RANK * subs : RANK * (subs + 1), :] = none
+    coeff_low[RANK * subs : RANK * (subs + 1), :] = none
+    up = jnp.concatenate([coeff_ref[d, RANK : RANK + ROWS8, :] for d in range(subs)], axis=0)
+    value = jnp.concatenate(
+        [gathered[pl.ds(q, ROWS8 * subs, stride=QUADS), :] for q in range(QUADS)], axis=1
+    )
+    every = dot_first(up, value)
+    top = jnp.zeros((RANK, COLS), F32)
+    for q in range(QUADS):
+        top = top + every[RANK * q : RANK * (q + 1), COLS * q : COLS * (q + 1)]
     lane_group = lanes(RANK) // RANK
+    targets = [(w, ids, n, y) for n, (w, ids) in enumerate(((weight_own, ids_own), (weight_other, ids_other))) for y in range(rows_y)]
     top_weight = []
-    for t in range(targets):
-        used = [jnp.zeros((RANK, COLS), F32)] * 2
+    for weight_ref, ids_ref, _, y in targets:
+        used = jnp.zeros((RANK, COLS), F32)
         for k in range(top_slots):
-            owner = ids_ref[t, 64 + slots + k].astype(jnp.int32)
-            for g in range(2):
-                group = row * 2 + (core if g == 0 else 1 - core)
-                used[g] = jnp.where(lane_group == k, jnp.where(owner == group, 1.0, 0.0), used[g])
-        block = weight_ref[t, 2 * RANK : 3 * RANK, :]
-        top_weight.append(jnp.concatenate([block * used[0], block * used[1]], axis=1))
+            owner = ids_ref[y, 64 + slots + k].astype(jnp.int32)
+            used = jnp.where(lane_group == k, jnp.where(owner == group, 1.0, 0.0), used)
+        top_weight.append(weight_ref[y, 2 * RANK : 3 * RANK, :] * used)
+    top_high, top_low = split(top)
     top_part = dot_split(
         jnp.concatenate(top_weight, axis=0),
-        jnp.concatenate([tops[0][0]] * 4 + [tops[1][0]] * 4, axis=0),
-        jnp.concatenate([tops[0][1]] * 4 + [tops[1][1]] * 4, axis=0),
-    )
-
-    def starts(t):
+        jnp.concatenate([top_high] * 4, axis=0),
+        jnp.concatenate([top_low] * 4, axis=0),
+    )
+
+    def starts(ids_ref, y):
         found = []
         for k in range(slots):
-            index = ids_ref[t, 64 + k].astype(jnp.int32)
-            group, sub = index // subs, index % subs
-            place = (here + across - sub // deep) % across * deep + sub % deep
-            place = place + jnp.where(group % 2 == core, 0, subs)
-            block = jnp.where(group // 2 == row, place, 2 * subs)
+            index = ids_ref[y, 64 + k].astype(jnp.int32)
+            block = jnp.where(index // subs == group, index % subs, subs)
             found.append(pl.multiple_of(block * RANK, RANK))
         return found
 
-    for t in range(0, targets, 2):
-        pair = [starts(t), starts(t + 1)]
+    for t in range(0, len(targets), 2):
+        two = targets[t : t + 2]
+        pair = [starts(ids_ref, y) for _, ids_ref, _, y in two]
         rows = [
             jnp.concatenate(
                 [jnp.concatenate([ref[pl.ds(s, RANK), :] for s in one], axis=0) for one in pair], axis=1
@@ -272,12 +257,13 @@
             for ref in (coeff_high, coeff_low)
         ]
         weight = [
-            jnp.concatenate([weight_ref[u, 0:RANK, :], weight_ref[u, RANK : 2 * RANK, :64]], axis=1)
-            for u in (t, t + 1)
+            jnp.concatenate([w[y, 0:RANK, :], w[y, RANK : 2 * RANK, :64]], axis=1) for w, _, _, y in two
         ]
         both = dot_split(jnp.concatenate(weight, axis=0), *rows)
-        out_ref[t] = both[:RANK, :COLS] + top_part[RANK * t : RANK * (t + 1)]
-        out_ref[t + 1] = both[RANK:, COLS:] + top_part[RANK * (t + 1) : RANK * (t + 2)]
+        for n, (_, _, other, y) in enumerate(two):
+            at = 2 * y + (1 - core if other else core)
+            mine = both[RANK * n : RANK * (n + 1), COLS * n : COLS * (n + 1)]
+            out_ref[at] = mine + top_part[RANK * (t + n) : RANK * (t + n + 1)]
 
 
 def last_kernel(parts_ref, fixed_ref, slope_ref, out_ref, natural):
@@ -343,9 +329,8 @@
 
     leaves, entries, _ = traction_vectors.shape
     blocks = leaves + leaves // 2
-    across, deep = lax.axis_size("x"), lax.axis_size("z")
     targets = lax.axis_size("y")
-    subs = across * deep
+    subs = lax.axis_size("x") * lax.axis_size("z")
     first = (
         traction_vectors, rows_of(couple_device), rows_of(down_device), rows_of(couple_top[0]),
         list_device, mask_device, list_top, mask_top,
@@ -357,7 +342,7 @@
     ]
     weights, stack, send = whole(
         first_kernel,
-        (shape(targets, 3 * RANK, COLS), shape(blocks * RANK, COLS), shape(deep, RANK + ROWS8, COLS)),
+        (shape(targets, 3 * RANK, COLS), shape(blocks * RANK, COLS), shape(subs, RANK + ROWS8, COLS)),
         first,
         hbm=range(len(first)),
         scratch=[
@@ -371,16 +356,12 @@
         limit=ALMOST_ALL,
     )
     weights = lax.all_to_all(weights, "y", 0, 0, tiled=True)
-    coeffs = lax.all_to_all(send, "z", 0, 0, tiled=True)
-    coeffs = [coeffs] + [
-        lax.ppermute(coeffs, "x", [(i, (i + step) % across) for i in range(across)])
-        for step in range(1, across)
-    ]
-    coeffs[-1], stack = lax.optimization_barrier((coeffs[-1], stack))
-    coeffs = coeffs + [lax.ppermute(block, "core", [(0, 1), (1, 0)]) for block in coeffs]
+    coeffs = lax.all_to_all(send, ("x", "z"), 0, 0, tiled=True)
     leaf_axes = ("x", "z")
     low = lax.ppermute(stack, leaf_axes, [(i, i + 1) for i in range(subs - 1)])
     high = lax.ppermute(stack, leaf_axes, [(i + 1, i) for i in range(subs - 1)])
+    other = lax.ppermute(weights, "core", [(0, 1), (1, 0)])
+    coeffs, low, high = lax.optimization_barrier((coeffs, low, high))
     near = pltpu.VMEM(((3 * blocks + 1) * RANK, COLS), BF16)
     fixed, slope = whole(
         far_kernel,
@@ -396,17 +377,17 @@
     )
     parts = whole(
         part_kernel,
-        shape(targets, RANK, COLS),
-        (*coeffs, weights, weights[:, RANK, :]),
-        smem=(2 * across + 1,),
+        shape(2 * targets, RANK, COLS),
+        (coeffs, weights, other, weights[:, RANK, :], other[:, RANK, :]),
+        smem=(3, 4),
         scratch=[
-            pltpu.VMEM(((2 * subs + 1) * RANK, COLS), BF16),
-            pltpu.VMEM(((2 * subs + 1) * RANK, COLS), BF16),
-            pltpu.VMEM((2 * subs * RANK, COLS), F32),
+            pltpu.VMEM(((subs + 1) * RANK, COLS), BF16),
+            pltpu.VMEM(((subs + 1) * RANK, COLS), BF16),
+            pltpu.VMEM((subs * RANK, COLS), F32),
         ],
         flops=10**8,
     )
-    parts = lax.all_to_all(parts, "y", 0, 0, tiled=True)
+    parts = lax.all_to_all(parts, ("y", "core"), 0, 0, tiled=True)
     return whole(
         last_kernel,
         shape(leaves, entries, COLS),

time: 79.8 us -> 80.4 us (level)
  the two profiles are of different devices: /device:TPU:10 before, /device:TPU:1 now
where the time goes in v2:
time: 80.4 us; the launch traced here: 80 us
  starting transfers between devices  31.7 us (39%)
  blocking collectives  19.1 us (24%)
  waiting for transfers between devices  17.5 us (22%)
  Pallas kernels  10.4 us (13%)
  local copies, waits for them, and re-layouts  0.96 us (1%)
    all_to_all x1, blocking collectives, body(): weights = lax.all_to_all(weights, 'y', 0, 0, tiled=True)  19.1 us
    all_to_all x1, starting transfers between devices, body(): coeffs = lax.all_to_all(send, ('x', 'z'), 0, 0, tiled=True)  14.9 us
    pallas_call x4, Pallas kernels, whole(): pl.pallas_call(kernel, out_shape=out, in_specs=[scalars if n in smem else...  10.4 us
    ppermute x1, waiting for transfers between devices, body(): high = lax.ppermute(stack, leaf_axes, [(i + 1, i) for i in range(subs - 1)])  8.76 us
    all_to_all x1, waiting for transfers between devices, body(): parts = lax.all_to_all(parts, ('y', 'core'), 0, 0, tiled=True)  8.76 us
    all_to_all x1, starting transfers between devices, body(): parts = lax.all_to_all(parts, ('y', 'core'), 0, 0, tiled=True)  7.1 us
    ppermute x1, starting transfers between devices, body(): other = lax.ppermute(weights, 'core', [(0, 1), (1, 0)])  4.31 us
    ppermute x1, starting transfers between devices, body(): low = lax.ppermute(stack, leaf_axes, [(i, i + 1) for i in range(subs - 1)])  4.05 us
  transfers between devices with their start and end apart: 5, of which 2 were waited for; matrix products, arithmetic and copies ran while one was open for 0% of the time, Pallas kernels for 3%

profile of v2, /device:TPU:1, one launch (start us, length us, event | category | flops | bytes accessed | tf_op | source)
XLA Modules:
  0.0 80.0 jit_solution(1754729295958864798)
XLA Ops:
  0.0 4.1 %shard_map.199 = (f32[8,96,128]{2,1,0:T(8,128)}, f32[384,128]{1,0:T(8,128)}, f32[32,40,128]{2,1,0:T(8,128)}) custom-call(f32[8,192,128]{2,1,0:T(8,128)} %refs_0_.1, f32[48,128]{1,0:T(8,128)} %bitcast.47, f32[8,128]{1,0:T(8,128)} %bitcast.50, f32[32,128]{1,0:T(8,128)} %bitcast.48, s32[1,6]{1,0:T(1,128)} %refs_4_.1, s32[1,6]{1,0:T(1,128)} %refs_5_.1, ...), custom_call_target="tpu_custom_call" | custom-call | flops 60000000 | bytes 2326608 | tf_op jit(solution)/shard_map/pallas_call | solution.py:287
  4.1 19.1 %all_to_all.15.weight_own = f32[8,96,128]{2,1,0:T(8,128)S(1)} all-to-all(f32[8,96,128]{2,1,0:T(8,128)} %get-tuple-element.16), channel_id=1, replica_groups=mesh['y'=8,'core'=2,'x'=4,'z'=8] {'y'}, dimensions={0} | all-to-all | bytes 786432 | tf_op jit(solution)/shard_map/all_to_all | solution.py:358
  23.3 14.9 %all-to-all-start = ((f32[32,40,128]{2,1,0:T(8,128)}), f32[32,40,128]{2,1,0:T(8,128)S(1)}, u32[]{:S(2)}, u32[]{:S(2)}) async-start(f32[32,40,128]{2,1,0:T(8,128)} %get-tuple-element.13), calls=%async_computation | async-start | bytes 1310720 | tf_op jit(solution)/shard_map/all_to_all | solution.py:359
  38.2 0.0 copy-start.2
  38.2 0.2 copy.31
  38.5 4.3 %collective-permute-start.2 = (f32[8,96,128]{2,0,1:T(8,128)S(1)}, f32[8,96,128]{2,0,1:T(8,128)S(1)}, u32[]{:S(2)}, u32[]{:S(2)}) collective-permute-start(f32[8,96,128]{2,0,1:T(8,128)S(1)} %copy.31), channel_id=1, source_target_pairs={{0,32},{32,0},{1,33},{33,1},{2,34},{34,2},{3,35},{35,3},{4,36},{36... | collective-permute-start | bytes 1179656 | tf_op jit(solution)/shard_map/ppermute | solution.py:363
  42.8 0.0 copy-done.2
  42.8 1.3 %collective-permute-start.1 = (f32[384,128]{1,0:T(8,128)S(1)}, f32[384,128]{1,0:T(8,128)S(1)}, u32[]{:S(2)}, u32[]{:S(2)}) collective-permute-start(f32[384,128]{1,0:T(8,128)S(1)} %copy-done.2), channel_id=1, source_target_pairs={{1,0},{2,1},{3,2},{4,3},{5,4},{6,5},{7,6},{8,7},{9,8},{10,9},{11,1... | collective-permute-start | bytes 589832 | tf_op jit(solution)/shard_map/ppermute | solution.py:362
  44.1 4.1 %collective-permute-start = (f32[384,128]{1,0:T(8,128)S(1)}, f32[384,128]{1,0:T(8,128)S(1)}, u32[]{:S(2)}, u32[]{:S(2)}) collective-permute-start(f32[384,128]{1,0:T(8,128)S(1)} %copy-done.2), channel_id=1, source_target_pairs={{0,1},{1,2},{2,3},{3,4},{4,5},{5,6},{6,7},{7,8},{8,9},{9,10},{10,1... | collective-permute-start | bytes 589832 | tf_op jit(solution)/shard_map/ppermute | solution.py:361
  48.2 0.0 collective-permute-done.2
  48.2 0.1 copy.33.weight_other
  48.3 8.8 %collective-permute-done.1.high_ref = f32[384,128]{1,0:T(8,128)S(1)} collective-permute-done((f32[384,128]{1,0:T(8,128)S(1)}, f32[384,128]{1,0:T(8,128)S(1)}, u32[]{:S(2)}, u32[]{:S(2)}) %collective-permute-start.1) | collective-permute-done | bytes 196640 | tf_op jit(solution)/shard_map/ppermute | solution.py:362
  57.0 0.0 collective-permute-done.low_ref
  57.0 0.0 all-to-all-done.coeff_ref
  57.0 0.0 copy-start.3
  57.0 2.8 %shard_map.200 = f32[16,32,128]{2,1,0:T(8,128)} custom-call(f32[32,40,128]{2,1,0:T(8,128)S(1)} %all-to-all-done.coeff_ref, f32[8,96,128]{2,1,0:T(8,128)S(1)} %all_to_all.15.weight_own, f32[8,96,128]{2,1,0:T(8,128)S(1)} %copy.33.weight_other, f32[8,128]{1,0:T(8,128)S(1)} %slice_bitcast_fusion.1.ids_own, f32[8,128]{1,0:T(8,128)S(1)} %slice_bitcast_fusion.ids_other), custom_call_target="tpu_custom_call" | custom-call | flops 100000000 | bytes 1712128 | tf_op jit(solution)/shard_map/pallas_call | solution.py:287
  59.8 0.0 copy-start
  59.8 0.0 copy-start.1
  59.8 0.0 copy-start.4
  59.8 0.0 copy-start.5
  59.8 0.0 copy-start.7
  59.8 0.0 copy-start.9
  59.8 7.1 %all-to-all-start.2 = ((f32[16,32,128]{2,1,0:T(8,128)}), f32[16,32,128]{2,1,0:T(8,128)S(1)}, u32[]{:S(2)}, u32[]{:S(2)}) async-start(f32[16,32,128]{2,1,0:T(8,128)} %shard_map.200), calls=%async_computation.2 | async-start | bytes 524288 | tf_op jit(solution)/shard_map/all_to_all | solution.py:390
  66.9 0.0 copy-start.6
  66.9 0.0 copy-start.8
  67.0 0.0 copy-done.3
  67.0 0.0 copy-done
  67.0 0.0 copy-done.1
  67.0 0.0 copy-done.4
  67.0 0.0 copy-done.5
  67.0 0.0 copy-done.7
  67.0 0.0 copy-done.9
  67.0 0.6 copy-done.6
  67.6 0.0 copy-done.8
  67.6 2.4 %shard_map.201 = (f32[8,192,128]{2,1,0:T(8,128)S(1)}, bf16[8,192,128]{2,1,0:T(8,128)(2,1)S(1)}) custom-call(f32[384,128]{1,0:T(8,128)S(1)} %collective-permute-done.low_ref, f32[384,128]{1,0:T(8,128)S(1)} %copy-done.2, f32[384,128]{1,0:T(8,128)S(1)} %collective-permute-done.1.high_ref, f32[384,128]{1,0:T(8,128)S(1)} %bitcast.42, f32[192,128]{1,0:T(8,128)S(1)} %bitcast.43, ...), custom_call_target="tpu_custom_call" | custom-call | flops 100000000 | bytes 2310720 | tf_op jit(solution)/shard_map/pallas_call | solution.py:287
  70.0 8.8 %all-to-all-done.2.parts_ref = f32[16,32,128]{2,1,0:T(8,128)S(1)} async-done(((f32[16,32,128]{2,1,0:T(8,128)}), f32[16,32,128]{2,1,0:T(8,128)S(1)}, u32[]{:S(2)}, u32[]{:S(2)}) %all-to-all-start.2) | async-done | bytes 262176 | tf_op jit(solution)/shard_map/all_to_all | solution.py:390
  78.8 1.2 %shard_map.202 = f32[8,192,128]{2,1,0:T(8,128)} custom-call(f32[16,32,128]{2,1,0:T(8,128)S(1)} %all-to-all-done.2.parts_ref, f32[8,192,128]{2,1,0:T(8,128)S(1)} %get-tuple-element.19.fixed_ref, bf16[8,192,128]{2,1,0:T(8,128)(2,1)S(1)} %get-tuple-element.20.slope_ref), custom_call_target="tpu_custom_call" | custom-call | flops 50000000 | bytes 2228224 | tf_op jit(solution)/shard_map/pallas_call | solution.py:287
  (2 shorter events, 0.0 us)
Async XLA Ops:
  23.3 33.8 %all-to-all-start = ((f32[32,40,128]{2,1,0:T(8,128)}), f32[32,40,128]{2,1,0:T(8,128)S(1)}, u32[]{:S(2)}, u32[]{:S(2)}) async-start(f32[32,40,128]{2,1,0:T(8,128)} %get-tuple-element.13), calls=%async_computation | async-start | bytes 1310720 | tf_op jit(solution)/shard_map/all_to_all | solution.py:359
  38.2 4.6 %copy-start.2 = (f32[384,128]{1,0:T(8,128)S(1)}, f32[384,128]{1,0:T(8,128)}, u32[]{:S(2)}) copy-start(f32[384,128]{1,0:T(8,128)} %get-tuple-element.14.own_ref) | copy-start | bytes 589828
  38.5 9.7 %collective-permute-start.2 = (f32[8,96,128]{2,0,1:T(8,128)S(1)}, f32[8,96,128]{2,0,1:T(8,128)S(1)}, u32[]{:S(2)}, u32[]{:S(2)}) collective-permute-start(f32[8,96,128]{2,0,1:T(8,128)S(1)} %copy.31), channel_id=1, source_target_pairs={{0,32},{32,0},{1,33},{33,1},{2,34},{34,2},{3,35},{35,3},{4,36},{36... | collective-permute-start | bytes 1179656 | tf_op jit(solution)/shard_map/ppermute | solution.py:363
  42.8 14.2 %collective-permute-start.1 = (f32[384,128]{1,0:T(8,128)S(1)}, f32[384,128]{1,0:T(8,128)S(1)}, u32[]{:S(2)}, u32[]{:S(2)}) collective-permute-start(f32[384,128]{1,0:T(8,128)S(1)} %copy-done.2), channel_id=1, source_target_pairs={{1,0},{2,1},{3,2},{4,3},{5,4},{6,5},{7,6},{8,7},{9,8},{10,9},{11,1... | collective-permute-start | bytes 589832 | tf_op jit(solution)/shard_map/ppermute | solution.py:362
  44.1 12.9 %collective-permute-start = (f32[384,128]{1,0:T(8,128)S(1)}, f32[384,128]{1,0:T(8,128)S(1)}, u32[]{:S(2)}, u32[]{:S(2)}) collective-permute-start(f32[384,128]{1,0:T(8,128)S(1)} %copy-done.2), channel_id=1, source_target_pairs={{0,1},{1,2},{2,3},{3,4},{4,5},{5,6},{6,7},{7,8},{8,9},{9,10},{10,1... | collective-permute-start | bytes 589832 | tf_op jit(solution)/shard_map/ppermute | solution.py:361
  57.0 9.9 %copy-start.3 = (f32[4,6,1024]{2,0,1:T(4,128)S(1)}, f32[4,6,1024]{2,0,1:T(4,128)}, u32[]{:S(2)}) copy-start(f32[4,6,1024]{2,0,1:T(4,128)} %param.27) | copy-start | bytes 294916
  59.8 7.2 %copy-start = (f32[8,32,192]{2,1,0:T(8,128)S(1)}, f32[8,32,192]{2,1,0:T(8,128)}, u32[]{:S(2)}) copy-start(f32[8,32,192]{2,1,0:T(8,128)} %basis.1) | copy-start | bytes 589828
  59.8 7.2 %copy-start.1 = (f32[8,6,1024]{2,0,1:T(8,128)S(1)}, f32[8,6,1024]{2,0,1:T(8,128)}, u32[]{:S(2)}) copy-start(f32[8,6,1024]{2,0,1:T(8,128)} %param.26) | copy-start | bytes 589828
  59.8 7.2 %copy-start.4 = (f32[8,1024]{1,0:T(8,128)S(1)}, f32[8,1024]{1,0:T(8,128)}, u32[]{:S(2)}) copy-start(f32[8,1024]{1,0:T(8,128)} %param.38) | copy-start | bytes 98308
  59.8 7.2 %copy-start.5 = (f32[4,1024]{1,0:T(4,128)S(1)}, f32[4,1024]{1,0:T(4,128)}, u32[]{:S(2)}) copy-start(f32[4,1024]{1,0:T(4,128)} %param.39) | copy-start | bytes 49156
  59.8 7.2 %copy-start.7 = (s32[8,6]{1,0:T(8,128)S(1)}, s32[8,6]{1,0:T(8,128)}, u32[]{:S(2)}) copy-start(s32[8,6]{1,0:T(8,128)} %mask_leaf.1) | copy-start | bytes 580
  59.8 7.2 %copy-start.9 = (s32[4,6]{1,0:T(4,128)S(1)}, s32[4,6]{1,0:T(4,128)}, u32[]{:S(2)}) copy-start(s32[4,6]{1,0:T(4,128)} %mask_pair.1) | copy-start | bytes 292
  59.8 19.0 %all-to-all-start.2 = ((f32[16,32,128]{2,1,0:T(8,128)}), f32[16,32,128]{2,1,0:T(8,128)S(1)}, u32[]{:S(2)}, u32[]{:S(2)}) async-start(f32[16,32,128]{2,1,0:T(8,128)} %shard_map.200), calls=%async_computation.2 | async-start | bytes 524288 | tf_op jit(solution)/shard_map/all_to_all | solution.py:390
  66.9 0.7 copy-start.6
  66.9 0.7 copy-start.8

commit v3 on v2

--- a/solution.py
+++ b/solution.py
@@ -110,8 +110,7 @@
     for copy in copies:
         copy.wait()
     for n, block in enumerate(weights(couple, down, top, list_d, mask_d, list_t, mask_t, natural)):
-        for t in range(weight_ref.shape[0]):
-            weight_ref[t, RANK * n : RANK * (n + 1), :] = block
+        weight_ref[0, RANK * n : RANK * (n + 1), :] = block
     for i in range(leaves):
         tractions[i].wait()
         high, low = split(traction[i])
@@ -198,14 +197,25 @@
             ).astype(BF16)
 
 
+def steps(count):
+    found = []
+    while count > 1:
+        count //= 2
+        found.append(count)
+    return found
+
+
 def part_kernel(
     coeff_ref, weight_own, weight_other, ids_own, ids_other, out_ref, coeff_high, coeff_low, gathered
 ):
     rows_y = weight_own.shape[0]
     subs = coeff_ref.shape[0]
     slots, top_slots = 6, 4
-    core = lax.axis_index("core")
-    group = lax.axis_index("y") * 2 + core
+    core, row = lax.axis_index("core"), lax.axis_index("y")
+    group = row * 2 + core
+    back = [0]
+    for step in steps(rows_y):
+        back = back + [b + step for b in back]
     none = jnp.zeros((RANK, COLS), BF16)
     for d in range(subs):
         value = coeff_ref[d, 0:RANK, :]
@@ -261,7 +271,7 @@
         ]
         both = dot_split(jnp.concatenate(weight, axis=0), *rows)
         for n, (_, _, other, y) in enumerate(two):
-            at = 2 * y + (1 - core if other else core)
+            at = 2 * ((row + rows_y - back[y]) % rows_y) + (1 - core if other else core)
             mine = both[RANK * n : RANK * (n + 1), COLS * n : COLS * (n + 1)]
             out_ref[at] = mine + top_part[RANK * (t + n) : RANK * (t + n + 1)]
 
@@ -342,7 +352,7 @@
     ]
     weights, stack, send = whole(
         first_kernel,
-        (shape(targets, 3 * RANK, COLS), shape(blocks * RANK, COLS), shape(subs, RANK + ROWS8, COLS)),
+        (shape(1, 3 * RANK, COLS), shape(blocks * RANK, COLS), shape(subs, RANK + ROWS8, COLS)),
         first,
         hbm=range(len(first)),
         scratch=[
@@ -355,7 +365,9 @@
         flops=6 * 10**7,
         limit=ALMOST_ALL,
     )
-    weights = lax.all_to_all(weights, "y", 0, 0, tiled=True)
+    for step in steps(targets):
+        come = lax.ppermute(weights, "y", [(i, (i + step) % targets) for i in range(targets)])
+        weights = jnp.concatenate([weights, come], axis=0)
     coeffs = lax.all_to_all(send, ("x", "z"), 0, 0, tiled=True)
     leaf_axes = ("x", "z")
     low = lax.ppermute(stack, leaf_axes, [(i, i + 1) for i in range(subs - 1)])

time: 80.4 us -> 82.6 us (1.027)
  the two profiles are of different devices: /device:TPU:1 before, /device:TPU:7 now
where the time goes in v3:
time: 82.6 us; the launch traced here: 82.1 us
  starting transfers between devices  39.7 us (48%)
  waiting for transfers between devices  30.5 us (37%)
  Pallas kernels  10.4 us (13%)
    ppermute x3, waiting for transfers between devices, body(): lax.ppermute(weights, 'y', [(i, (i + step) % targets) for i in range(targ...  13.6 us
    all_to_all x1, starting transfers between devices, body(): coeffs = lax.all_to_all(send, ('x', 'z'), 0, 0, tiled=True)  13 us
    ppermute x3, starting transfers between devices, body(): lax.ppermute(weights, 'y', [(i, (i + step) % targets) for i in range(targ...  11.9 us
    pallas_call x4, Pallas kernels, whole(): pl.pallas_call(kernel, out_shape=out, in_specs=[scalars if n in smem else...  10.4 us
    all_to_all x1, waiting for transfers between devices, body(): parts = lax.all_to_all(parts, ('y', 'core'), 0, 0, tiled=True)  8.76 us
    ppermute x1, waiting for transfers between devices, body(): low = lax.ppermute(stack, leaf_axes, [(i, i + 1) for i in range(subs - 1)])  5.91 us
    all_to_all x1, starting transfers between devices, body(): parts = lax.all_to_all(parts, ('y', 'core'), 0, 0, tiled=True)  4.58 us
    ppermute x1, starting transfers between devices, body(): high = lax.ppermute(stack, leaf_axes, [(i + 1, i) for i in range(subs - 1)])  4.18 us
  transfers between devices with their start and end apart: 8, of which 5 were waited for; matrix products, arithmetic and copies ran while one was open for 1% of the time, Pallas kernels for 3%

profile of v3, /device:TPU:7, one launch (start us, length us, event | category | flops | bytes accessed | tf_op | source)
XLA Modules:
  0.0 82.1 jit_solution(5354335565901920459)
XLA Ops:
  0.0 4.1 %shard_map.199 = (f32[1,96,128]{2,1,0:T(8,128)}, f32[384,128]{1,0:T(8,128)}, f32[32,40,128]{2,1,0:T(8,128)}) custom-call(f32[8,192,128]{2,1,0:T(8,128)} %refs_0_.1, f32[48,128]{1,0:T(8,128)} %bitcast.52, f32[8,128]{1,0:T(8,128)} %bitcast.55, f32[32,128]{1,0:T(8,128)} %bitcast.53, s32[1,6]{1,0:T(1,128)} %refs_4_.1, s32[1,6]{1,0:T(1,128)} %refs_5_.1, ...), custom_call_target="tpu_custom_call" | custom-call | flops 60000000 | bytes 1982544 | tf_op jit(solution)/shard_map/pallas_call | solution.py:297
  4.1 7.5 %collective-permute-start.2 = (f32[1,96,128]{2,0,1:T(1,128)}, f32[1,96,128]{2,0,1:T(1,128)S(1)}, u32[]{:S(2)}, u32[]{:S(2)}) collective-permute-start(f32[1,96,128]{2,0,1:T(1,128)} %bitcast.47), channel_id=1, source_target_pairs={{0,256},{64,320},{128,384},{192,448},{256,0},{320,64},{384,128},{4... | collective-permute-start | bytes 147464 | tf_op jit(solution)/shard_map/ppermute | solution.py:369
  11.6 0.0 copy-start.10
  11.6 13.0 %all-to-all-start = ((f32[32,40,128]{2,1,0:T(8,128)}), f32[32,40,128]{2,1,0:T(8,128)S(1)}, u32[]{:S(2)}, u32[]{:S(2)}) async-start(f32[32,40,128]{2,1,0:T(8,128)} %get-tuple-element.13), calls=%async_computation | async-start | bytes 1310720 | tf_op jit(solution)/shard_map/all_to_all | solution.py:371
  24.6 0.0 collective-permute-done.2
  24.7 0.0 copy-done.10
  24.7 0.1 pad_maximum_fusion.2
  24.8 2.4 %collective-permute-start.3 = (f32[2,96,128]{2,0,1:T(2,128)S(1)}, f32[2,96,128]{2,0,1:T(2,128)S(1)}, u32[]{:S(2)}, u32[]{:S(2)}) collective-permute-start(f32[2,96,128]{2,0,1:T(2,128)S(1)} %pad_maximum_fusion.2), channel_id=1, source_target_pairs={{0,128},{64,192},{128,256},{192,320},{256,384},{320,448},{384,0},{... | collective-permute-start | bytes 294920 | tf_op jit(solution)/shard_map/ppermute | solution.py:369
  27.2 7.3 %collective-permute-done.3 = f32[2,96,128]{2,0,1:T(2,128)S(1)} collective-permute-done((f32[2,96,128]{2,0,1:T(2,128)S(1)}, f32[2,96,128]{2,0,1:T(2,128)S(1)}, u32[]{:S(2)}, u32[]{:S(2)}) %collective-permute-start.3) | collective-permute-done | bytes 98336 | tf_op jit(solution)/shard_map/ppermute | solution.py:369
  34.5 0.1 pad_maximum_fusion.1
  34.6 0.0 copy-start.2
  34.6 2.1 %collective-permute-start.4 = (f32[4,96,128]{2,0,1:T(4,128)S(1)}, f32[4,96,128]{2,0,1:T(4,128)S(1)}, u32[]{:S(2)}, u32[]{:S(2)}) collective-permute-start(f32[4,96,128]{2,0,1:T(4,128)S(1)} %pad_maximum_fusion.1), channel_id=1, source_target_pairs={{0,64},{64,128},{128,192},{192,256},{256,320},{320,384},{384,448},... | collective-permute-start | bytes 589832 | tf_op jit(solution)/shard_map/ppermute | solution.py:369
  36.7 6.3 %collective-permute-done.4 = f32[4,96,128]{2,0,1:T(4,128)S(1)} collective-permute-done((f32[4,96,128]{2,0,1:T(4,128)S(1)}, f32[4,96,128]{2,0,1:T(4,128)S(1)}, u32[]{:S(2)}, u32[]{:S(2)}) %collective-permute-start.4) | collective-permute-done | bytes 196640 | tf_op jit(solution)/shard_map/ppermute | solution.py:369
  43.0 0.2 pad_maximum_fusion
  43.2 4.1 %collective-permute-start.5 = (f32[8,96,128]{2,0,1:T(8,128)S(1)}, f32[8,96,128]{2,0,1:T(8,128)S(1)}, u32[]{:S(2)}, u32[]{:S(2)}) collective-permute-start(f32[8,96,128]{2,0,1:T(8,128)S(1)} %pad_maximum_fusion), channel_id=1, source_target_pairs={{0,32},{32,0},{1,33},{33,1},{2,34},{34,2},{3,35},{35,3},{4,36},{36... | collective-permute-start | bytes 1179656 | tf_op jit(solution)/shard_map/ppermute | solution.py:375
  47.3 0.0 copy-done.2
  47.3 4.2 %collective-permute-start.1 = (f32[384,128]{1,0:T(8,128)S(1)}, f32[384,128]{1,0:T(8,128)S(1)}, u32[]{:S(2)}, u32[]{:S(2)}) collective-permute-start(f32[384,128]{1,0:T(8,128)S(1)} %copy-done.2), channel_id=1, source_target_pairs={{1,0},{2,1},{3,2},{4,3},{5,4},{6,5},{7,6},{8,7},{9,8},{10,9},{11,1... | collective-permute-start | bytes 589832 | tf_op jit(solution)/shard_map/ppermute | solution.py:374
  51.5 1.9 %collective-permute-start = (f32[384,128]{1,0:T(8,128)S(1)}, f32[384,128]{1,0:T(8,128)S(1)}, u32[]{:S(2)}, u32[]{:S(2)}) collective-permute-start(f32[384,128]{1,0:T(8,128)S(1)} %copy-done.2), channel_id=1, source_target_pairs={{0,1},{1,2},{2,3},{3,4},{4,5},{5,6},{6,7},{7,8},{8,9},{9,10},{10,1... | collective-permute-start | bytes 589832 | tf_op jit(solution)/shard_map/ppermute | solution.py:373
  53.4 0.1 copy.28.weight_own
  53.5 0.0 collective-permute-done.5
  53.5 0.1 copy.29.weight_other
  53.6 2.2 %collective-permute-done.1.high_ref = f32[384,128]{1,0:T(8,128)S(1)} collective-permute-done((f32[384,128]{1,0:T(8,128)S(1)}, f32[384,128]{1,0:T(8,128)S(1)}, u32[]{:S(2)}, u32[]{:S(2)}) %collective-permute-start.1) | collective-permute-done | bytes 196640 | tf_op jit(solution)/shard_map/ppermute | solution.py:374
  55.8 5.9 %collective-permute-done.low_ref = f32[384,128]{1,0:T(8,128)S(1)} collective-permute-done((f32[384,128]{1,0:T(8,128)S(1)}, f32[384,128]{1,0:T(8,128)S(1)}, u32[]{:S(2)}, u32[]{:S(2)}) %collective-permute-start) | collective-permute-done | bytes 196640 | tf_op jit(solution)/shard_map/ppermute | solution.py:373
  61.7 0.0 all-to-all-done.coeff_ref
  61.7 0.0 copy-start.3
  61.7 2.8 %shard_map.200 = f32[16,32,128]{2,1,0:T(8,128)} custom-call(f32[32,40,128]{2,1,0:T(8,128)S(1)} %all-to-all-done.coeff_ref, f32[8,96,128]{2,1,0:T(8,128)S(1)} %copy.28.weight_own, f32[8,96,128]{2,1,0:T(8,128)S(1)} %copy.29.weight_other, f32[8,128]{1,0:T(8,128)S(1)} %slice_bitcast_fusion.1.ids_own, f32[8,128]{1,0:T(8,128)S(1)} %slice_bitcast_fusion.ids_other), custom_call_target="tpu_custom_call" | custom-call | flops 100000000 | bytes 1712128 | tf_op jit(solution)/shard_map/pallas_call | solution.py:297
  64.5 0.0 copy-start
  64.5 0.0 copy-start.1
  64.5 0.0 copy-start.4
  64.5 0.0 copy-start.5
  64.5 0.0 copy-start.7
  64.5 0.0 copy-start.9
  64.5 4.6 %all-to-all-start.1 = ((f32[16,32,128]{2,1,0:T(8,128)}), f32[16,32,128]{2,1,0:T(8,128)S(1)}, u32[]{:S(2)}, u32[]{:S(2)}) async-start(f32[16,32,128]{2,1,0:T(8,128)} %shard_map.200), calls=%async_computation.1 | async-start | bytes 524288 | tf_op jit(solution)/shard_map/all_to_all | solution.py:402
  69.1 0.0 copy-start.6
  69.1 0.0 copy-start.8
  69.1 0.0 copy-done.3
  69.1 0.0 copy-done
  69.1 0.0 copy-done.1
  69.1 0.0 copy-done.4
  69.1 0.0 copy-done.5
  69.1 0.0 copy-done.7
  69.2 0.0 copy-done.9
  69.2 0.6 copy-done.6
  69.8 0.0 copy-done.8
  69.8 2.4 %shard_map.201 = (f32[8,192,128]{2,1,0:T(8,128)S(1)}, bf16[8,192,128]{2,1,0:T(8,128)(2,1)S(1)}) custom-call(f32[384,128]{1,0:T(8,128)S(1)} %collective-permute-done.low_ref, f32[384,128]{1,0:T(8,128)S(1)} %copy-done.2, f32[384,128]{1,0:T(8,128)S(1)} %collective-permute-done.1.high_ref, f32[384,128]{1,0:T(8,128)S(1)} %bitcast.43, f32[192,128]{1,0:T(8,128)S(1)} %bitcast.44, ...), custom_call_target="tpu_custom_call" | custom-call | flops 100000000 | bytes 2310720 | tf_op jit(solution)/shard_map/pallas_call | solution.py:297
  72.2 8.8 %all-to-all-done.1.parts_ref = f32[16,32,128]{2,1,0:T(8,128)S(1)} async-done(((f32[16,32,128]{2,1,0:T(8,128)}), f32[16,32,128]{2,1,0:T(8,128)S(1)}, u32[]{:S(2)}, u32[]{:S(2)}) %all-to-all-start.1) | async-done | bytes 262176 | tf_op jit(solution)/shard_map/all_to_all | solution.py:402
  80.9 1.2 %shard_map.202 = f32[8,192,128]{2,1,0:T(8,128)} custom-call(f32[16,32,128]{2,1,0:T(8,128)S(1)} %all-to-all-done.1.parts_ref, f32[8,192,128]{2,1,0:T(8,128)S(1)} %get-tuple-element.19.fixed_ref, bf16[8,192,128]{2,1,0:T(8,128)(2,1)S(1)} %get-tuple-element.20.slope_ref), custom_call_target="tpu_custom_call" | custom-call | flops 50000000 | bytes 2228224 | tf_op jit(solution)/shard_map/pallas_call | solution.py:297
  (2 shorter events, 0.0 us)
Async XLA Ops:
  4.1 20.5 %collective-permute-start.2 = (f32[1,96,128]{2,0,1:T(1,128)}, f32[1,96,128]{2,0,1:T(1,128)S(1)}, u32[]{:S(2)}, u32[]{:S(2)}) collective-permute-start(f32[1,96,128]{2,0,1:T(1,128)} %bitcast.47), channel_id=1, source_target_pairs={{0,256},{64,320},{128,384},{192,448},{256,0},{320,64},{384,128},{4... | collective-permute-start | bytes 147464 | tf_op jit(solution)/shard_map/ppermute | solution.py:369
  11.6 13.1 %copy-start.10 = (f32[1,96,128]{2,1,0:T(8,128)S(1)}, f32[1,96,128]{2,1,0:T(8,128)}, u32[]{:S(2)}) copy-start(f32[1,96,128]{2,1,0:T(8,128)} %get-tuple-element.16) | copy-start | bytes 147460
  11.6 50.1 %all-to-all-start = ((f32[32,40,128]{2,1,0:T(8,128)}), f32[32,40,128]{2,1,0:T(8,128)S(1)}, u32[]{:S(2)}, u32[]{:S(2)}) async-start(f32[32,40,128]{2,1,0:T(8,128)} %get-tuple-element.13), calls=%async_computation | async-start | bytes 1310720 | tf_op jit(solution)/shard_map/all_to_all | solution.py:371
  24.8 9.7 %collective-permute-start.3 = (f32[2,96,128]{2,0,1:T(2,128)S(1)}, f32[2,96,128]{2,0,1:T(2,128)S(1)}, u32[]{:S(2)}, u32[]{:S(2)}) collective-permute-start(f32[2,96,128]{2,0,1:T(2,128)S(1)} %pad_maximum_fusion.2), channel_id=1, source_target_pairs={{0,128},{64,192},{128,256},{192,320},{256,384},{320,448},{384,0},{... | collective-permute-start | bytes 294920 | tf_op jit(solution)/shard_map/ppermute | solution.py:369
  34.6 12.7 %copy-start.2 = (f32[384,128]{1,0:T(8,128)S(1)}, f32[384,128]{1,0:T(8,128)}, u32[]{:S(2)}) copy-start(f32[384,128]{1,0:T(8,128)} %get-tuple-element.14.own_ref) | copy-start | bytes 589828
  34.6 8.4 %collective-permute-start.4 = (f32[4,96,128]{2,0,1:T(4,128)S(1)}, f32[4,96,128]{2,0,1:T(4,128)S(1)}, u32[]{:S(2)}, u32[]{:S(2)}) collective-permute-start(f32[4,96,128]{2,0,1:T(4,128)S(1)} %pad_maximum_fusion.1), channel_id=1, source_target_pairs={{0,64},{64,128},{128,192},{192,256},{256,320},{320,384},{384,448},... | collective-permute-start | bytes 589832 | tf_op jit(solution)/shard_map/ppermute | solution.py:369
  43.2 10.3 %collective-permute-start.5 = (f32[8,96,128]{2,0,1:T(8,128)S(1)}, f32[8,96,128]{2,0,1:T(8,128)S(1)}, u32[]{:S(2)}, u32[]{:S(2)}) collective-permute-start(f32[8,96,128]{2,0,1:T(8,128)S(1)} %pad_maximum_fusion), channel_id=1, source_target_pairs={{0,32},{32,0},{1,33},{33,1},{2,34},{34,2},{3,35},{35,3},{4,36},{36... | collective-permute-start | bytes 1179656 | tf_op jit(solution)/shard_map/ppermute | solution.py:375
  47.3 8.5 %collective-permute-start.1 = (f32[384,128]{1,0:T(8,128)S(1)}, f32[384,128]{1,0:T(8,128)S(1)}, u32[]{:S(2)}, u32[]{:S(2)}) collective-permute-start(f32[384,128]{1,0:T(8,128)S(1)} %copy-done.2), channel_id=1, source_target_pairs={{1,0},{2,1},{3,2},{4,3},{5,4},{6,5},{7,6},{8,7},{9,8},{10,9},{11,1... | collective-permute-start | bytes 589832 | tf_op jit(solution)/shard_map/ppermute | solution.py:374
  51.5 10.2 %collective-permute-start = (f32[384,128]{1,0:T(8,128)S(1)}, f32[384,128]{1,0:T(8,128)S(1)}, u32[]{:S(2)}, u32[]{:S(2)}) collective-permute-start(f32[384,128]{1,0:T(8,128)S(1)} %copy-done.2), channel_id=1, source_target_pairs={{0,1},{1,2},{2,3},{3,4},{4,5},{5,6},{6,7},{7,8},{8,9},{9,10},{10,1... | collective-permute-start | bytes 589832 | tf_op jit(solution)/shard_map/ppermute | solution.py:373
  61.7 7.4 %copy-start.3 = (f32[4,6,1024]{2,0,1:T(4,128)S(1)}, f32[4,6,1024]{2,0,1:T(4,128)}, u32[]{:S(2)}) copy-start(f32[4,6,1024]{2,0,1:T(4,128)} %param.27) | copy-start | bytes 294916
  64.5 4.6 %copy-start = (f32[8,32,192]{2,1,0:T(8,128)S(1)}, f32[8,32,192]{2,1,0:T(8,128)}, u32[]{:S(2)}) copy-start(f32[8,32,192]{2,1,0:T(8,128)} %basis.1) | copy-start | bytes 589828
  64.5 4.7 %copy-start.1 = (f32[8,6,1024]{2,0,1:T(8,128)S(1)}, f32[8,6,1024]{2,0,1:T(8,128)}, u32[]{:S(2)}) copy-start(f32[8,6,1024]{2,0,1:T(8,128)} %param.26) | copy-start | bytes 589828
  64.5 4.7 %copy-start.4 = (f32[8,1024]{1,0:T(8,128)S(1)}, f32[8,1024]{1,0:T(8,128)}, u32[]{:S(2)}) copy-start(f32[8,1024]{1,0:T(8,128)} %param.38) | copy-start | bytes 98308
  64.5 4.7 %copy-start.5 = (f32[4,1024]{1,0:T(4,128)S(1)}, f32[4,1024]{1,0:T(4,128)}, u32[]{:S(2)}) copy-start(f32[4,1024]{1,0:T(4,128)} %param.39) | copy-start | bytes 49156
  64.5 4.7 %copy-start.7 = (s32[8,6]{1,0:T(8,128)S(1)}, s32[8,6]{1,0:T(8,128)}, u32[]{:S(2)}) copy-start(s32[8,6]{1,0:T(8,128)} %mask_leaf.1) | copy-start | bytes 580
  64.5 4.7 %copy-start.9 = (s32[4,6]{1,0:T(4,128)S(1)}, s32[4,6]{1,0:T(4,128)}, u32[]{:S(2)}) copy-start(s32[4,6]{1,0:T(4,128)} %mask_pair.1) | copy-start | bytes 292
  64.5 16.4 %all-to-all-start.1 = ((f32[16,32,128]{2,1,0:T(8,128)}), f32[16,32,128]{2,1,0:T(8,128)S(1)}, u32[]{:S(2)}, u32[]{:S(2)}) async-start(f32[16,32,128]{2,1,0:T(8,128)} %shard_map.200), calls=%async_computation.1 | async-start | bytes 524288 | tf_op jit(solution)/shard_map/all_to_all | solution.py:402
  69.1 0.7 copy-start.6
  69.1 0.7 copy-start.8

commit v4 on v1

--- a/solution.py
+++ b/solution.py
@@ -110,8 +110,7 @@
     for copy in copies:
         copy.wait()
     for n, block in enumerate(weights(couple, down, top, list_d, mask_d, list_t, mask_t, natural)):
-        for t in range(weight_ref.shape[0]):
-            weight_ref[t, RANK * n : RANK * (n + 1), :] = block
+        weight_ref[0, RANK * n : RANK * (n + 1), :] = block
     for i in range(leaves):
         tractions[i].wait()
         high, low = split(traction[i])
@@ -198,30 +197,34 @@
             ).astype(BF16)
 
 
+def shifts(count):
+    half = count // 2
+    return [s if s <= half // 2 else s - half for s in range(1, half)]
+
+
 def part_kernel(*refs):
-    buffers = len(refs) - 6
-    coeff_refs = refs[:buffers]
-    weight_ref, ids_ref, out_ref, coeff_high, coeff_low, gathered = refs[buffers:]
-    targets = weight_ref.shape[0]
-    across = buffers // 2
-    deep = coeff_refs[0].shape[0]
-    subs = across * deep
+    buffers = (len(refs) - 6) // 2
+    coeff_own, coeff_other = refs[:2]
+    weight_refs, ids_refs = refs[2 : 2 + buffers], refs[2 + buffers : 2 + 2 * buffers]
+    out_ref, coeff_high, coeff_low, gathered = refs[2 + 2 * buffers :]
+    subs = coeff_own.shape[0]
+    rows_y = 2 * buffers
     slots, top_slots = 6, 4
-    row, core, here = lax.axis_index("y"), lax.axis_index("core"), lax.axis_index("x")
+    row, core = lax.axis_index("y"), lax.axis_index("core")
     none = jnp.zeros((RANK, COLS), BF16)
-    blocks = [(ref, z) for ref in coeff_refs for z in range(deep)]
-    for d, (ref, z) in enumerate(blocks):
-        value = ref[z, 0:RANK, :]
-        gathered[RANK * d : RANK * (d + 1), :] = value
+    blocks = [(ref, d) for ref in (coeff_own, coeff_other) for d in range(subs)]
+    for n, (ref, d) in enumerate(blocks):
+        value = ref[d, 0:RANK, :]
+        gathered[RANK * n : RANK * (n + 1), :] = value
         high, low = split(value)
-        coeff_high[RANK * d : RANK * (d + 1), :] = high
-        coeff_low[RANK * d : RANK * (d + 1), :] = low
+        coeff_high[RANK * n : RANK * (n + 1), :] = high
+        coeff_low[RANK * n : RANK * (n + 1), :] = low
     coeff_high[2 * RANK * subs : RANK * (2 * subs + 1), :] = none
     coeff_low[2 * RANK * subs : RANK * (2 * subs + 1), :] = none
     tops = []
     for g in range(2):
         up = jnp.concatenate(
-            [ref[z, RANK : RANK + ROWS8, :] for ref, z in blocks[g * subs : (g + 1) * subs]], axis=0
+            [ref[d, RANK : RANK + ROWS8, :] for ref, d in blocks[g * subs : (g + 1) * subs]], axis=0
         )
         value = jnp.concatenate(
             [
@@ -236,15 +239,18 @@
             top = top + every[RANK * q : RANK * (q + 1), COLS * q : COLS * (q + 1)]
         tops.append(split(top))
     lane_group = lanes(RANK) // RANK
+    targets = []
+    for weight_ref, ids_ref, shift in zip(weight_refs, ids_refs, [0] + shifts(rows_y)):
+        targets += [(weight_ref, ids_ref, n, shift + n * buffers) for n in range(2)]
     top_weight = []
-    for t in range(targets):
+    for weight_ref, ids_ref, n, _ in targets:
         used = [jnp.zeros((RANK, COLS), F32)] * 2
         for k in range(top_slots):
-            owner = ids_ref[t, 64 + slots + k].astype(jnp.int32)
+            owner = ids_ref[n, 64 + slots + k].astype(jnp.int32)
             for g in range(2):
                 group = row * 2 + (core if g == 0 else 1 - core)
                 used[g] = jnp.where(lane_group == k, jnp.where(owner == group, 1.0, 0.0), used[g])
-        block = weight_ref[t, 2 * RANK : 3 * RANK, :]
+        block = weight_ref[n, 2 * RANK : 3 * RANK, :]
         top_weight.append(jnp.concatenate([block * used[0], block * used[1]], axis=1))
     top_part = dot_split(
         jnp.concatenate(top_weight, axis=0),
@@ -252,19 +258,19 @@
         jnp.concatenate([tops[0][1]] * 4 + [tops[1][1]] * 4, axis=0),
     )
 
-    def starts(t):
+    def starts(ids_ref, n):
         found = []
         for k in range(slots):
-            index = ids_ref[t, 64 + k].astype(jnp.int32)
+            index = ids_ref[n, 64 + k].astype(jnp.int32)
             group, sub = index // subs, index % subs
-            place = (here + across - sub // deep) % across * deep + sub % deep
-            place = place + jnp.where(group % 2 == core, 0, subs)
+            place = sub + jnp.where(group % 2 == core, 0, subs)
             block = jnp.where(group // 2 == row, place, 2 * subs)
             found.append(pl.multiple_of(block * RANK, RANK))
         return found
 
-    for t in range(0, targets, 2):
-        pair = [starts(t), starts(t + 1)]
+    for t in range(0, rows_y, 2):
+        two = targets[t : t + 2]
+        pair = [starts(ids_ref, n) for _, ids_ref, n, _ in two]
         rows = [
             jnp.concatenate(
                 [jnp.concatenate([ref[pl.ds(s, RANK), :] for s in one], axis=0) for one in pair], axis=1
@@ -272,12 +278,13 @@
             for ref in (coeff_high, coeff_low)
         ]
         weight = [
-            jnp.concatenate([weight_ref[u, 0:RANK, :], weight_ref[u, RANK : 2 * RANK, :64]], axis=1)
-            for u in (t, t + 1)
+            jnp.concatenate([w[n, 0:RANK, :], w[n, RANK : 2 * RANK, :64]], axis=1) for w, _, n, _ in two
         ]
         both = dot_split(jnp.concatenate(weight, axis=0), *rows)
-        out_ref[t] = both[:RANK, :COLS] + top_part[RANK * t : RANK * (t + 1)]
-        out_ref[t + 1] = both[RANK:, COLS:] + top_part[RANK * (t + 1) : RANK * (t + 2)]
+        for m, (_, _, _, offset) in enumerate(two):
+            at = (row + 2 * rows_y - offset) % rows_y
+            mine = both[RANK * m : RANK * (m + 1), COLS * m : COLS * (m + 1)]
+            out_ref[at] = mine + top_part[RANK * (t + m) : RANK * (t + m + 1)]
 
 
 def last_kernel(parts_ref, fixed_ref, slope_ref, out_ref, natural):
@@ -343,9 +350,8 @@
 
     leaves, entries, _ = traction_vectors.shape
     blocks = leaves + leaves // 2
-    across, deep = lax.axis_size("x"), lax.axis_size("z")
     targets = lax.axis_size("y")
-    subs = across * deep
+    subs = lax.axis_size("x") * lax.axis_size("z")
     first = (
         traction_vectors, rows_of(couple_device), rows_of(down_device), rows_of(couple_top[0]),
         list_device, mask_device, list_top, mask_top,
@@ -357,7 +363,7 @@
     ]
     weights, stack, send = whole(
         first_kernel,
-        (shape(targets, 3 * RANK, COLS), shape(blocks * RANK, COLS), shape(deep, RANK + ROWS8, COLS)),
+        (shape(1, 3 * RANK, COLS), shape(blocks * RANK, COLS), shape(subs, RANK + ROWS8, COLS)),
         first,
         hbm=range(len(first)),
         scratch=[
@@ -370,17 +376,17 @@
         flops=6 * 10**7,
         limit=ALMOST_ALL,
     )
-    weights = lax.all_to_all(weights, "y", 0, 0, tiled=True)
-    coeffs = lax.all_to_all(send, "z", 0, 0, tiled=True)
-    coeffs = [coeffs] + [
-        lax.ppermute(coeffs, "x", [(i, (i + step) % across) for i in range(across)])
-        for step in range(1, across)
-    ]
-    coeffs[-1], stack = lax.optimization_barrier((coeffs[-1], stack))
-    coeffs = coeffs + [lax.ppermute(block, "core", [(0, 1), (1, 0)]) for block in coeffs]
+    def over_y(block, step):
+        return lax.ppermute(block, "y", [(i, (i + step) % targets) for i in range(targets)])
+
+    weights = jnp.concatenate([weights, over_y(weights, targets // 2)], axis=0)
+    coeffs = lax.all_to_all(send, ("x", "z"), 0, 0, tiled=True)
+    weights = [weights] + [over_y(weights, step) for step in shifts(targets)]
     leaf_axes = ("x", "z")
     low = lax.ppermute(stack, leaf_axes, [(i, i + 1) for i in range(subs - 1)])
     high = lax.ppermute(stack, leaf_axes, [(i + 1, i) for i in range(subs - 1)])
+    coeffs, low, high, weights = lax.optimization_barrier((coeffs, low, high, weights))
+    other = lax.ppermute(coeffs, "core", [(0, 1), (1, 0)])
     near = pltpu.VMEM(((3 * blocks + 1) * RANK, COLS), BF16)
     fixed, slope = whole(
         far_kernel,
@@ -397,8 +403,8 @@
     parts = whole(
         part_kernel,
         shape(targets, RANK, COLS),
-        (*coeffs, weights, weights[:, RANK, :]),
-        smem=(2 * across + 1,),
+        (coeffs, other, *weights, *(block[:, RANK, :] for block in weights)),
+        smem=range(2 + len(weights), 2 + 2 * len(weights)),
         scratch=[
             pltpu.VMEM(((2 * subs + 1) * RANK, COLS), BF16),
             pltpu.VMEM(((2 * subs + 1) * RANK, COLS), BF16),

time: 79.8 us -> 68.6 us (0.86)
  the two profiles are of different devices: /device:TPU:10 before, /device:TPU:6 now
where the time goes in v4:
time: 68.6 us; the launch traced here: 68.1 us
  starting transfers between devices  46 us (67%)
  waiting for transfers between devices  10.7 us (16%)
  Pallas kernels  10.3 us (15%)
  local copies, waits for them, and re-layouts  0.7 us (1%)
    ppermute x4, starting transfers between devices, over_y(): lax.ppermute(block, 'y', [(i, (i + step) % targets) for i in range(target...  17.5 us
    all_to_all x1, starting transfers between devices, body(): coeffs = lax.all_to_all(send, ('x', 'z'), 0, 0, tiled=True)  13.6 us
    pallas_call x4, Pallas kernels, whole(): pl.pallas_call(kernel, out_shape=out, in_specs=[scalars if n in smem else...  10.3 us
    all_to_all x1, waiting for transfers between devices, body(): parts = lax.all_to_all(parts, 'y', 0, 0, tiled=True)  6.27 us
    all_to_all x1, starting transfers between devices, body(): parts = lax.all_to_all(parts, 'y', 0, 0, tiled=True)  5.07 us
    ppermute x1, starting transfers between devices, body(): high = lax.ppermute(stack, leaf_axes, [(i + 1, i) for i in range(subs - 1)])  4.57 us
    ppermute x1, starting transfers between devices, body(): low = lax.ppermute(stack, leaf_axes, [(i, i + 1) for i in range(subs - 1)])  3.38 us
    ppermute x4, waiting for transfers between devices, over_y(): lax.ppermute(block, 'y', [(i, (i + step) % targets) for i in range(target...  2.49 us
  transfers between devices with their start and end apart: 9, of which 3 were waited for; matrix products, arithmetic and copies ran while one was open for 0% of the time, Pallas kernels for 4%

profile of v4, /device:TPU:6, one launch (start us, length us, event | category | flops | bytes accessed | tf_op | source)
XLA Modules:
  0.0 68.1 jit_solution(6726951569980197120)
XLA Ops:
  0.0 4.1 %shard_map.199 = (f32[1,96,128]{2,1,0:T(8,128)}, f32[384,128]{1,0:T(8,128)}, f32[32,40,128]{2,1,0:T(8,128)}) custom-call(f32[8,192,128]{2,1,0:T(8,128)} %refs_0_.1, f32[48,128]{1,0:T(8,128)} %bitcast.54, f32[8,128]{1,0:T(8,128)} %bitcast.57, f32[32,128]{1,0:T(8,128)} %bitcast.55, s32[1,6]{1,0:T(1,128)} %refs_4_.1, s32[1,6]{1,0:T(1,128)} %refs_5_.1, ...), custom_call_target="tpu_custom_call" | custom-call | flops 60000000 | bytes 1982544 | tf_op jit(solution)/shard_map/pallas_call | solution.py:308
  4.1 0.0 copy-start.10
  4.1 0.0 copy-start.2
  4.2 13.6 %all-to-all-start = ((f32[32,40,128]{2,1,0:T(8,128)}), f32[32,40,128]{2,1,0:T(8,128)S(1)}, u32[]{:S(2)}, u32[]{:S(2)}) async-start(f32[32,40,128]{2,1,0:T(8,128)} %get-tuple-element.17), calls=%async_computation | async-start | bytes 1310720 | tf_op jit(solution)/shard_map/all_to_all | solution.py:383
  17.8 0.0 copy-done.10
  17.8 7.7 %collective-permute-start.2 = (f32[1,96,128]{2,0,1:T(1,128)S(1)}, f32[1,96,128]{2,0,1:T(1,128)S(1)}, u32[]{:S(2)}, u32[]{:S(2)}) collective-permute-start(f32[1,96,128]{2,0,1:T(1,128)S(1)} %bitcast.51), channel_id=1, source_target_pairs={{0,256},{64,320},{128,384},{192,448},{256,0},{320,64},{384,128},{4... | collective-permute-start | bytes 147464 | tf_op jit(solution)/shard_map/ppermute | solution.py:380
  25.5 0.0 copy-done.2
  25.5 3.4 %collective-permute-start = (f32[384,128]{1,0:T(8,128)S(1)}, f32[384,128]{1,0:T(8,128)S(1)}, u32[]{:S(2)}, u32[]{:S(2)}) collective-permute-start(f32[384,128]{1,0:T(8,128)S(1)} %copy-done.2), channel_id=1, source_target_pairs={{0,1},{1,2},{2,3},{3,4},{4,5},{5,6},{6,7},{7,8},{8,9},{9,10},{10,1... | collective-permute-start | bytes 589832 | tf_op jit(solution)/shard_map/ppermute | solution.py:386
  28.9 4.6 %collective-permute-start.1 = (f32[384,128]{1,0:T(8,128)S(1)}, f32[384,128]{1,0:T(8,128)S(1)}, u32[]{:S(2)}, u32[]{:S(2)}) collective-permute-start(f32[384,128]{1,0:T(8,128)S(1)} %copy-done.2), channel_id=1, source_target_pairs={{1,0},{2,1},{3,2},{4,3},{5,4},{6,5},{7,6},{8,7},{9,8},{10,9},{11,1... | collective-permute-start | bytes 589832 | tf_op jit(solution)/shard_map/ppermute | solution.py:387
  33.5 0.0 collective-permute-done.2
  33.5 0.1 pad_maximum_fusion
  33.6 2.6 %collective-permute-start.3 = (f32[2,96,128]{2,0,1:T(2,128)S(1)}, f32[2,96,128]{2,0,1:T(2,128)S(1)}, u32[]{:S(2)}, u32[]{:S(2)}) collective-permute-start(f32[2,96,128]{2,0,1:T(2,128)S(1)} %pad_maximum_fusion), channel_id=1, source_target_pairs={{0,64},{64,128},{128,192},{192,256},{256,320},{320,384},{384,448},... | collective-permute-start | bytes 294920 | tf_op jit(solution)/shard_map/ppermute | solution.py:380
  36.2 2.7 %collective-permute-start.4 = (f32[2,96,128]{2,0,1:T(2,128)S(1)}, f32[2,96,128]{2,0,1:T(2,128)S(1)}, u32[]{:S(2)}, u32[]{:S(2)}) collective-permute-start(f32[2,96,128]{2,0,1:T(2,128)S(1)} %pad_maximum_fusion), channel_id=1, source_target_pairs={{0,128},{64,192},{128,256},{192,320},{256,384},{320,448},{384,0},{... | collective-permute-start | bytes 294920 | tf_op jit(solution)/shard_map/ppermute | solution.py:380
  38.9 4.5 %collective-permute-start.5 = (f32[2,96,128]{2,0,1:T(2,128)S(1)}, f32[2,96,128]{2,0,1:T(2,128)S(1)}, u32[]{:S(2)}, u32[]{:S(2)}) collective-permute-start(f32[2,96,128]{2,0,1:T(2,128)S(1)} %pad_maximum_fusion), channel_id=1, source_target_pairs={{0,448},{64,0},{128,64},{192,128},{256,192},{320,256},{384,320},{4... | collective-permute-start | bytes 294920 | tf_op jit(solution)/shard_map/ppermute | solution.py:380
  43.4 0.0 collective-permute-done.3
  43.4 2.5 %collective-permute-done.4 = f32[2,96,128]{2,0,1:T(2,128)S(1)} collective-permute-done((f32[2,96,128]{2,0,1:T(2,128)S(1)}, f32[2,96,128]{2,0,1:T(2,128)S(1)}, u32[]{:S(2)}, u32[]{:S(2)}) %collective-permute-start.4) | collective-permute-done | bytes 98336 | tf_op jit(solution)/shard_map/ppermute | solution.py:380
  45.9 0.0 collective-permute-done.5
  45.9 0.0 collective-permute-done.low_ref
  45.9 0.0 collective-permute-done.1.high_ref
  45.9 0.0 all-to-all-done.refs_0_
  45.9 1.9 %collective-permute-start.6 = (f32[32,40,128]{2,1,0:T(8,128)S(1)}, f32[32,40,128]{2,1,0:T(8,128)S(1)}, u32[]{:S(2)}, u32[]{:S(2)}) collective-permute-start(f32[32,40,128]{2,1,0:T(8,128)S(1)} %all-to-all-done.refs_0_), channel_id=1, source_target_pairs={{0,32},{32,0},{1,33},{33,1},{2,34},{34,2},{3,35},{35,3},{4,36},{36... | collective-permute-start | bytes 1966088 | tf_op jit(solution)/shard_map/ppermute | solution.py:389
  47.9 2.0 %collective-permute-done.6.refs_1_ = f32[32,40,128]{2,1,0:T(8,128)S(1)} collective-permute-done((f32[32,40,128]{2,1,0:T(8,128)S(1)}, f32[32,40,128]{2,1,0:T(8,128)S(1)}, u32[]{:S(2)}, u32[]{:S(2)}) %collective-permute-start.6) | collective-permute-done | bytes 655392 | tf_op jit(solution)/shard_map/ppermute | solution.py:389
  49.9 0.0 copy-start.1
  49.9 0.0 copy-start.3
  49.9 0.0 copy-start.4
  49.9 0.0 copy-start.5
  49.9 0.0 copy-start.7
  49.9 0.0 copy-start.9
  49.9 2.6 %shard_map.200 = f32[8,32,128]{2,1,0:T(8,128)} custom-call(f32[32,40,128]{2,1,0:T(8,128)S(1)} %all-to-all-done.refs_0_, f32[32,40,128]{2,1,0:T(8,128)S(1)} %collective-permute-done.6.refs_1_, f32[2,96,128]{2,1,0:T(8,128)S(1)} %copy.26.refs_2_, f32[2,96,128]{2,1,0:T(8,128)S(1)} %copy.27.refs_3_, f32[2,96,128]{2,1,0:T(8,128)S(1)} %copy.28.refs_4_, ...), custom_call_target="tpu_custom_call" | custom-call | flops 100000000 | bytes 1839104 | tf_op jit(solution)/shard_map/pallas_call | solution.py:308
  52.5 0.0 copy-start
  52.5 5.1 %all-to-all-start.1 = ((f32[8,32,128]{2,1,0:T(8,128)}), f32[8,32,128]{2,1,0:T(8,128)S(1)}, u32[]{:S(2)}, u32[]{:S(2)}) async-start(f32[8,32,128]{2,1,0:T(8,128)} %shard_map.200), calls=%async_computation.1 | async-start | bytes 262144 | tf_op jit(solution)/shard_map/all_to_all | solution.py:415
  57.6 0.0 copy-start.6
  57.6 0.0 copy-start.8
  57.6 0.0 copy-done.1
  57.6 0.0 copy-done.3
  57.6 0.0 copy-done.4
  57.6 0.0 copy-done.5
  57.7 0.0 copy-done.7
  57.7 0.0 copy-done.9
  57.7 0.0 copy-done
  57.7 0.6 copy-done.6
  58.3 0.0 copy-done.8
  58.3 2.4 %shard_map.201 = (f32[8,192,128]{2,1,0:T(8,128)S(1)}, bf16[8,192,128]{2,1,0:T(8,128)(2,1)S(1)}) custom-call(f32[384,128]{1,0:T(8,128)S(1)} %collective-permute-done.low_ref, f32[384,128]{1,0:T(8,128)S(1)} %copy-done.2, f32[384,128]{1,0:T(8,128)S(1)} %collective-permute-done.1.high_ref, f32[384,128]{1,0:T(8,128)S(1)} %bitcast.47, f32[192,128]{1,0:T(8,128)S(1)} %bitcast.48, ...), custom_call_target="tpu_custom_call" | custom-call | flops 100000000 | bytes 2310720 | tf_op jit(solution)/shard_map/pallas_call | solution.py:308
  60.7 6.3 %all-to-all-done.1.parts_ref = f32[8,32,128]{2,1,0:T(8,128)S(1)} async-done(((f32[8,32,128]{2,1,0:T(8,128)}), f32[8,32,128]{2,1,0:T(8,128)S(1)}, u32[]{:S(2)}, u32[]{:S(2)}) %all-to-all-start.1) | async-done | bytes 131104 | tf_op jit(solution)/shard_map/all_to_all | solution.py:415
  67.0 1.2 %shard_map.202 = f32[8,192,128]{2,1,0:T(8,128)} custom-call(f32[8,32,128]{2,1,0:T(8,128)S(1)} %all-to-all-done.1.parts_ref, f32[8,192,128]{2,1,0:T(8,128)S(1)} %get-tuple-element.27.fixed_ref, bf16[8,192,128]{2,1,0:T(8,128)(2,1)S(1)} %get-tuple-element.28.slope_ref), custom_call_target="tpu_custom_call" | custom-call | flops 50000000 | bytes 2097152 | tf_op jit(solution)/shard_map/pallas_call | solution.py:308
  (6 shorter events, 0.0 us)
Async XLA Ops:
  4.1 13.6 %copy-start.10 = (f32[1,96,128]{2,1,0:T(8,128)S(1)}, f32[1,96,128]{2,1,0:T(8,128)}, u32[]{:S(2)}) copy-start(f32[1,96,128]{2,1,0:T(8,128)} %get-tuple-element.19) | copy-start | bytes 147460
  4.1 21.4 %copy-start.2 = (f32[384,128]{1,0:T(8,128)S(1)}, f32[384,128]{1,0:T(8,128)}, u32[]{:S(2)}) copy-start(f32[384,128]{1,0:T(8,128)} %get-tuple-element.18.own_ref) | copy-start | bytes 589828
  4.2 41.7 %all-to-all-start = ((f32[32,40,128]{2,1,0:T(8,128)}), f32[32,40,128]{2,1,0:T(8,128)S(1)}, u32[]{:S(2)}, u32[]{:S(2)}) async-start(f32[32,40,128]{2,1,0:T(8,128)} %get-tuple-element.17), calls=%async_computation | async-start | bytes 1310720 | tf_op jit(solution)/shard_map/all_to_all | solution.py:383
  17.8 15.7 %collective-permute-start.2 = (f32[1,96,128]{2,0,1:T(1,128)S(1)}, f32[1,96,128]{2,0,1:T(1,128)S(1)}, u32[]{:S(2)}, u32[]{:S(2)}) collective-permute-start(f32[1,96,128]{2,0,1:T(1,128)S(1)} %bitcast.51), channel_id=1, source_target_pairs={{0,256},{64,320},{128,384},{192,448},{256,0},{320,64},{384,128},{4... | collective-permute-start | bytes 147464 | tf_op jit(solution)/shard_map/ppermute | solution.py:380
  25.5 20.4 %collective-permute-start = (f32[384,128]{1,0:T(8,128)S(1)}, f32[384,128]{1,0:T(8,128)S(1)}, u32[]{:S(2)}, u32[]{:S(2)}) collective-permute-start(f32[384,128]{1,0:T(8,128)S(1)} %copy-done.2), channel_id=1, source_target_pairs={{0,1},{1,2},{2,3},{3,4},{4,5},{5,6},{6,7},{7,8},{8,9},{9,10},{10,1... | collective-permute-start | bytes 589832 | tf_op jit(solution)/shard_map/ppermute | solution.py:386
  28.9 17.0 %collective-permute-start.1 = (f32[384,128]{1,0:T(8,128)S(1)}, f32[384,128]{1,0:T(8,128)S(1)}, u32[]{:S(2)}, u32[]{:S(2)}) collective-permute-start(f32[384,128]{1,0:T(8,128)S(1)} %copy-done.2), channel_id=1, source_target_pairs={{1,0},{2,1},{3,2},{4,3},{5,4},{6,5},{7,6},{8,7},{9,8},{10,9},{11,1... | collective-permute-start | bytes 589832 | tf_op jit(solution)/shard_map/ppermute | solution.py:387
  33.6 9.8 %collective-permute-start.3 = (f32[2,96,128]{2,0,1:T(2,128)S(1)}, f32[2,96,128]{2,0,1:T(2,128)S(1)}, u32[]{:S(2)}, u32[]{:S(2)}) collective-permute-start(f32[2,96,128]{2,0,1:T(2,128)S(1)} %pad_maximum_fusion), channel_id=1, source_target_pairs={{0,64},{64,128},{128,192},{192,256},{256,320},{320,384},{384,448},... | collective-permute-start | bytes 294920 | tf_op jit(solution)/shard_map/ppermute | solution.py:380
  36.2 9.7 %collective-permute-start.4 = (f32[2,96,128]{2,0,1:T(2,128)S(1)}, f32[2,96,128]{2,0,1:T(2,128)S(1)}, u32[]{:S(2)}, u32[]{:S(2)}) collective-permute-start(f32[2,96,128]{2,0,1:T(2,128)S(1)} %pad_maximum_fusion), channel_id=1, source_target_pairs={{0,128},{64,192},{128,256},{192,320},{256,384},{320,448},{384,0},{... | collective-permute-start | bytes 294920 | tf_op jit(solution)/shard_map/ppermute | solution.py:380
  38.9 7.0 %collective-permute-start.5 = (f32[2,96,128]{2,0,1:T(2,128)S(1)}, f32[2,96,128]{2,0,1:T(2,128)S(1)}, u32[]{:S(2)}, u32[]{:S(2)}) collective-permute-start(f32[2,96,128]{2,0,1:T(2,128)S(1)} %pad_maximum_fusion), channel_id=1, source_target_pairs={{0,448},{64,0},{128,64},{192,128},{256,192},{320,256},{384,320},{4... | collective-permute-start | bytes 294920 | tf_op jit(solution)/shard_map/ppermute | solution.py:380
  45.9 4.0 %collective-permute-start.6 = (f32[32,40,128]{2,1,0:T(8,128)S(1)}, f32[32,40,128]{2,1,0:T(8,128)S(1)}, u32[]{:S(2)}, u32[]{:S(2)}) collective-permute-start(f32[32,40,128]{2,1,0:T(8,128)S(1)} %all-to-all-done.refs_0_), channel_id=1, source_target_pairs={{0,32},{32,0},{1,33},{33,1},{2,34},{34,2},{3,35},{35,3},{4,36},{36... | collective-permute-start | bytes 1966088 | tf_op jit(solution)/shard_map/ppermute | solution.py:389
  49.9 7.7 %copy-start.1 = (f32[8,6,1024]{2,0,1:T(8,128)S(1)}, f32[8,6,1024]{2,0,1:T(8,128)}, u32[]{:S(2)}) copy-start(f32[8,6,1024]{2,0,1:T(8,128)} %param.26) | copy-start | bytes 589828
  49.9 7.7 %copy-start.3 = (f32[4,6,1024]{2,0,1:T(4,128)S(1)}, f32[4,6,1024]{2,0,1:T(4,128)}, u32[]{:S(2)}) copy-start(f32[4,6,1024]{2,0,1:T(4,128)} %param.27) | copy-start | bytes 294916
  49.9 7.7 %copy-start.4 = (f32[8,1024]{1,0:T(8,128)S(1)}, f32[8,1024]{1,0:T(8,128)}, u32[]{:S(2)}) copy-start(f32[8,1024]{1,0:T(8,128)} %param.38) | copy-start | bytes 98308
  49.9 7.8 %copy-start.5 = (f32[4,1024]{1,0:T(4,128)S(1)}, f32[4,1024]{1,0:T(4,128)}, u32[]{:S(2)}) copy-start(f32[4,1024]{1,0:T(4,128)} %param.39) | copy-start | bytes 49156
  49.9 7.8 %copy-start.7 = (s32[8,6]{1,0:T(8,128)S(1)}, s32[8,6]{1,0:T(8,128)}, u32[]{:S(2)}) copy-start(s32[8,6]{1,0:T(8,128)} %mask_leaf.1) | copy-start | bytes 580
  49.9 7.8 %copy-start.9 = (s32[4,6]{1,0:T(4,128)S(1)}, s32[4,6]{1,0:T(4,128)}, u32[]{:S(2)}) copy-start(s32[4,6]{1,0:T(4,128)} %mask_pair.1) | copy-start | bytes 292
  52.5 5.1 %copy-start = (f32[8,32,192]{2,1,0:T(8,128)S(1)}, f32[8,32,192]{2,1,0:T(8,128)}, u32[]{:S(2)}) copy-start(f32[8,32,192]{2,1,0:T(8,128)} %basis.1) | copy-start | bytes 589828
  52.5 14.4 %all-to-all-start.1 = ((f32[8,32,128]{2,1,0:T(8,128)}), f32[8,32,128]{2,1,0:T(8,128)S(1)}, u32[]{:S(2)}, u32[]{:S(2)}) async-start(f32[8,32,128]{2,1,0:T(8,128)} %shard_map.200), calls=%async_computation.1 | async-start | bytes 262144 | tf_op jit(solution)/shard_map/all_to_all | solution.py:415
  57.6 0.7 %copy-start.6 = (s32[8,6]{1,0:T(8,128)S(1)}, s32[8,6]{1,0:T(8,128)}, u32[]{:S(2)}) copy-start(s32[8,6]{1,0:T(8,128)} %list_leaf.1) | copy-start | bytes 580
  57.6 0.7 %copy-start.8 = (s32[4,6]{1,0:T(4,128)S(1)}, s32[4,6]{1,0:T(4,128)}, u32[]{:S(2)}) copy-start(s32[4,6]{1,0:T(4,128)} %list_pair.1) | copy-start | bytes 292

commit v5 on v2

--- a/solution.py
+++ b/solution.py
@@ -1,3 +1,5 @@
+import functools
+
 import jax
 import jax.numpy as jnp
 from jax import lax
@@ -73,45 +75,52 @@
         ref[pl.ds(start + q, ROWS8, stride=QUADS), :] = x[ROWS8 * q : ROWS8 * (q + 1)]
 
 
-def weights(couple, down, top, list_d, mask_d, list_t, mask_t, natural):
+def fetch(sources, held, sems):
+    copies = [pltpu.make_async_copy(s, h, sems.at[n]) for n, (s, h) in enumerate(zip(sources, held))]
+    for copy in copies:
+        copy.start()
+    return copies
+
+
+def weights_kernel(*refs):
+    sources, out_ref, held, sems, natural = refs[:7], refs[7], refs[8:15], refs[15], refs[16]
+    for copy in fetch(sources, held, sems):
+        copy.wait()
+    couple, down, top, list_d, mask_d, list_t, mask_t = held
     slots, top_slots = list_d.shape[1], list_t.shape[1]
-    flats = [couple[ROWS8 * k : ROWS8 * (k + 1), :] * mask_d[0, k].astype(F32) for k in range(slots)]
+
+    def entry(ref, k):
+        return ref[0:1, k : k + 1].astype(F32)
+
+    flats = [couple[ROWS8 * k : ROWS8 * (k + 1), :] * entry(mask_d, k) for k in range(slots)]
     lane = lanes(RANK)
     ids = jnp.zeros((RANK, COLS), F32)
     for k in range(slots):
-        ids = jnp.where(lane == 64 + k, list_d[0, k].astype(F32), ids)
+        ids = jnp.where(lane == 64 + k, entry(list_d, k), ids)
     for k in range(top_slots):
-        ids = jnp.where(lane == 64 + slots + k, list_t[0, k].astype(F32), ids)
-    tops = [
-        top[pl.ds(k, ROWS8, stride=top_slots), :] * mask_t[0, k].astype(F32) for k in range(top_slots)
-    ]
+        ids = jnp.where(lane == 64 + slots + k, entry(list_t, k), ids)
+    tops = [top[pl.ds(k, ROWS8, stride=top_slots), :] * entry(mask_t, k) for k in range(top_slots)]
     store_natural(natural, 0, beside(tops))
     top_high, top_low = split(natural[...])
-    return (
-        beside(flats[:4]),
-        jnp.where(lane < 64, beside(flats[4:]), ids),
-        dot_split(square(down[...]), top_high, top_low),
-    )
-
-
-def first_kernel(*refs):
-    count = 12
-    sources, (weight_ref, stack_ref, send_ref), scratch = refs[:count], refs[count : count + 3], refs[count + 3 :]
-    held, (sems, traction, traction_sems, natural) = scratch[:count - 1], scratch[count - 1 :]
-    copies = [pltpu.make_async_copy(s, h, sems.at[n]) for n, (s, h) in enumerate(zip(sources[1:], held))]
+    out_ref[0, 0:RANK, :] = beside(flats[:4])
+    out_ref[0, RANK : 2 * RANK, :] = jnp.where(lane < 64, beside(flats[4:]), ids)
+    out_ref[0, 2 * RANK : 3 * RANK, :] = dot_split(square(down[...]), top_high, top_low)
+
+
+def up_kernel(*refs):
+    sources, (stack_ref, send_ref), scratch = refs[:5], refs[5:7], refs[7:]
+    held, (sems, traction, traction_sems) = scratch[:4], scratch[4:]
     leaves = sources[0].shape[0]
     pairs = leaves // 2
+    copies = fetch(sources[1:], held, sems)
     tractions = [
         pltpu.make_async_copy(sources[0].at[i], traction.at[i], traction_sems.at[i]) for i in range(leaves)
     ]
-    for copy in copies + tractions:
+    for copy in tractions:
         copy.start()
-    couple, down, top, list_d, mask_d, list_t, mask_t, basis, up_leaf, up_pair, up_device = held
+    basis, up_leaf, up_pair, up_device = held
     for copy in copies:
         copy.wait()
-    for n, block in enumerate(weights(couple, down, top, list_d, mask_d, list_t, mask_t, natural)):
-        for t in range(weight_ref.shape[0]):
-            weight_ref[t, RANK * n : RANK * (n + 1), :] = block
     for i in range(leaves):
         tractions[i].wait()
         high, low = split(traction[i])
@@ -127,9 +136,9 @@
     value = [quad_rows(stack_ref, RANK * (leaves + p)) for p in range(pairs)]
     coeff = dot_first(jnp.concatenate(weight, axis=0), jnp.concatenate(value, axis=0))
     up = up_device[...]
-    for z in range(send_ref.shape[0]):
-        send_ref[z, 0:RANK, :] = coeff
-        send_ref[z, RANK : RANK + ROWS8, :] = up
+    for d in range(send_ref.shape[0]):
+        send_ref[d, 0:RANK, :] = coeff
+        send_ref[d, RANK : RANK + ROWS8, :] = up
 
 
 def far_kernel(
@@ -198,14 +207,22 @@
             ).astype(BF16)
 
 
-def part_kernel(
-    coeff_ref, weight_own, weight_other, ids_own, ids_other, out_ref, coeff_high, coeff_low, gathered
-):
-    rows_y = weight_own.shape[0]
+def shifts(count):
+    half = count // 2
+    return [s if s <= half // 2 else s - half for s in range(1, half)]
+
+
+def part_kernel(own, *refs):
+    buffers = (len(refs) - (5 if own else 6)) // 2
+    coeff_ref = refs[0]
+    weight_refs, ids_refs = refs[1 : 1 + buffers], refs[1 + buffers : 1 + 2 * buffers]
+    before_ref = None if own else refs[1 + 2 * buffers]
+    out_ref, coeff_high, coeff_low, gathered = refs[-4:]
     subs = coeff_ref.shape[0]
+    rows_y = 2 * buffers
     slots, top_slots = 6, 4
-    core = lax.axis_index("core")
-    group = lax.axis_index("y") * 2 + core
+    row, core = lax.axis_index("y"), lax.axis_index("core")
+    source = row * 2 + (core if own else 1 - core)
     none = jnp.zeros((RANK, COLS), BF16)
     for d in range(subs):
         value = coeff_ref[d, 0:RANK, :]
@@ -224,14 +241,16 @@
     for q in range(QUADS):
         top = top + every[RANK * q : RANK * (q + 1), COLS * q : COLS * (q + 1)]
     lane_group = lanes(RANK) // RANK
-    targets = [(w, ids, n, y) for n, (w, ids) in enumerate(((weight_own, ids_own), (weight_other, ids_other))) for y in range(rows_y)]
+    targets = []
+    for weight_ref, ids_ref, shift in zip(weight_refs, ids_refs, [0] + shifts(rows_y)):
+        targets += [(weight_ref, ids_ref, n, shift + n * buffers) for n in range(2)]
     top_weight = []
-    for weight_ref, ids_ref, _, y in targets:
+    for weight_ref, ids_ref, n, _ in targets:
         used = jnp.zeros((RANK, COLS), F32)
         for k in range(top_slots):
-            owner = ids_ref[y, 64 + slots + k].astype(jnp.int32)
-            used = jnp.where(lane_group == k, jnp.where(owner == group, 1.0, 0.0), used)
-        top_weight.append(weight_ref[y, 2 * RANK : 3 * RANK, :] * used)
+            owner = ids_ref[n, 64 + slots + k].astype(jnp.int32)
+            used = jnp.where(lane_group == k, jnp.where(owner == source, 1.0, 0.0), used)
+        top_weight.append(weight_ref[n, 2 * RANK : 3 * RANK, :] * used)
     top_high, top_low = split(top)
     top_part = dot_split(
         jnp.concatenate(top_weight, axis=0),
@@ -239,17 +258,17 @@
         jnp.concatenate([top_low] * 4, axis=0),
     )
 
-    def starts(ids_ref, y):
+    def starts(ids_ref, n):
         found = []
         for k in range(slots):
-            index = ids_ref[y, 64 + k].astype(jnp.int32)
-            block = jnp.where(index // subs == group, index % subs, subs)
+            index = ids_ref[n, 64 + k].astype(jnp.int32)
+            block = jnp.where(index // subs == source, index % subs, subs)
             found.append(pl.multiple_of(block * RANK, RANK))
         return found
 
-    for t in range(0, len(targets), 2):
+    for t in range(0, rows_y, 2):
         two = targets[t : t + 2]
-        pair = [starts(ids_ref, y) for _, ids_ref, _, y in two]
+        pair = [starts(ids_ref, n) for _, ids_ref, n, _ in two]
         rows = [
             jnp.concatenate(
                 [jnp.concatenate([ref[pl.ds(s, RANK), :] for s in one], axis=0) for one in pair], axis=1
@@ -257,13 +276,14 @@
             for ref in (coeff_high, coeff_low)
         ]
         weight = [
-            jnp.concatenate([w[y, 0:RANK, :], w[y, RANK : 2 * RANK, :64]], axis=1) for w, _, _, y in two
+            jnp.concatenate([w[n, 0:RANK, :], w[n, RANK : 2 * RANK, :64]], axis=1) for w, _, n, _ in two
         ]
         both = dot_split(jnp.concatenate(weight, axis=0), *rows)
-        for n, (_, _, other, y) in enumerate(two):
-            at = 2 * y + (1 - core if other else core)
-            mine = both[RANK * n : RANK * (n + 1), COLS * n : COLS * (n + 1)]
-            out_ref[at] = mine + top_part[RANK * (t + n) : RANK * (t + n + 1)]
+        for m, (_, _, _, offset) in enumerate(two):
+            at = (row + 2 * rows_y - offset) % rows_y
+            mine = both[RANK * m : RANK * (m + 1), COLS * m : COLS * (m + 1)]
+            mine = mine + top_part[RANK * (t + m) : RANK * (t + m + 1)]
+            out_ref[at] = mine if own else mine + before_ref[at]
 
 
 def last_kernel(parts_ref, fixed_ref, slope_ref, out_ref, natural):
@@ -331,37 +351,67 @@
     blocks = leaves + leaves // 2
     targets = lax.axis_size("y")
     subs = lax.axis_size("x") * lax.axis_size("z")
+    def fetched(args):
+        return [pltpu.VMEM(a.shape, a.dtype) for a in args] + [pltpu.SemaphoreType.DMA((len(args),))]
+
     first = (
-        traction_vectors, rows_of(couple_device), rows_of(down_device), rows_of(couple_top[0]),
+        rows_of(couple_device), rows_of(down_device), rows_of(couple_top[0]),
         list_device, mask_device, list_top, mask_top,
-        row_basis, rows_of(up_leaf), rows_of(up_pair), rows_of(up_device),
-    )
-    scalars = (4, 5, 6, 7)
-    held = [
-        (pltpu.SMEM if n in scalars else pltpu.VMEM)(a.shape, a.dtype) for n, a in enumerate(first) if n
-    ]
-    weights, stack, send = whole(
-        first_kernel,
-        (shape(targets, 3 * RANK, COLS), shape(blocks * RANK, COLS), shape(subs, RANK + ROWS8, COLS)),
+    )
+    weights = whole(
+        weights_kernel,
+        shape(1, 3 * RANK, COLS),
         first,
         hbm=range(len(first)),
+        scratch=[*fetched(first), pltpu.VMEM((RANK, COLS), F32)],
+        flops=10**6,
+        limit=ALMOST_ALL,
+    )
+    weights, traction_vectors = lax.optimization_barrier((weights, traction_vectors))
+    second = (traction_vectors, row_basis, rows_of(up_leaf), rows_of(up_pair), rows_of(up_device))
+    stack, send = whole(
+        up_kernel,
+        (shape(blocks * RANK, COLS), shape(subs, RANK + ROWS8, COLS)),
+        second,
+        hbm=range(len(second)),
         scratch=[
-            *held,
-            pltpu.SemaphoreType.DMA((len(held),)),
+            *fetched(second[1:]),
             pltpu.VMEM(traction_vectors.shape, F32),
             pltpu.SemaphoreType.DMA((leaves,)),
-            pltpu.VMEM((RANK, COLS), F32),
         ],
         flops=6 * 10**7,
         limit=ALMOST_ALL,
     )
-    weights = lax.all_to_all(weights, "y", 0, 0, tiled=True)
+
+    def over_y(block, step):
+        return lax.ppermute(block, "y", [(i, (i + step) % targets) for i in range(targets)])
+
+    weights = jnp.concatenate([weights, over_y(weights, targets // 2)], axis=0)
     coeffs = lax.all_to_all(send, ("x", "z"), 0, 0, tiled=True)
+    weights = [weights] + [over_y(weights, step) for step in shifts(targets)]
     leaf_axes = ("x", "z")
     low = lax.ppermute(stack, leaf_axes, [(i, i + 1) for i in range(subs - 1)])
     high = lax.ppermute(stack, leaf_axes, [(i + 1, i) for i in range(subs - 1)])
-    other = lax.ppermute(weights, "core", [(0, 1), (1, 0)])
-    coeffs, low, high = lax.optimization_barrier((coeffs, low, high))
+    coeffs, low, high, weights = lax.optimization_barrier((coeffs, low, high, weights))
+    other = lax.ppermute(coeffs, "core", [(0, 1), (1, 0)])
+    weights = [*weights, *(block[:, RANK, :] for block in weights)]
+    count = len(weights) // 2
+    parts = []
+    for own, gathered in ((True, coeffs), (False, other)):
+        parts = whole(
+            functools.partial(part_kernel, own),
+            shape(targets, RANK, COLS),
+            (gathered, *weights, *([] if own else [parts])),
+            smem=range(1 + count, 1 + 2 * count),
+            scratch=[
+                pltpu.VMEM(((subs + 1) * RANK, COLS), BF16),
+                pltpu.VMEM(((subs + 1) * RANK, COLS), BF16),
+                pltpu.VMEM((subs * RANK, COLS), F32),
+            ],
+            flops=5 * 10**7,
+        )
+    parts, low = lax.optimization_barrier((parts, low))
+    parts = lax.all_to_all(parts, "y", 0, 0, tiled=True)
     near = pltpu.VMEM(((3 * blocks + 1) * RANK, COLS), BF16)
     fixed, slope = whole(
         far_kernel,
@@ -375,19 +425,6 @@
         scratch=[near, near, pltpu.VMEM((2 * RANK * blocks, COLS), F32)],
         flops=10**8,
     )
-    parts = whole(
-        part_kernel,
-        shape(2 * targets, RANK, COLS),
-        (coeffs, weights, other, weights[:, RANK, :], other[:, RANK, :]),
-        smem=(3, 4),
-        scratch=[
-            pltpu.VMEM(((subs + 1) * RANK, COLS), BF16),
-            pltpu.VMEM(((subs + 1) * RANK, COLS), BF16),
-            pltpu.VMEM((subs * RANK, COLS), F32),
-        ],
-        flops=10**8,
-    )
-    parts = lax.all_to_all(parts, ("y", "core"), 0, 0, tiled=True)
     return whole(
         last_kernel,
         shape(leaves, entries, COLS),

time: 80.4 us -> 68.9 us (0.86)
  the two profiles are of different devices: /device:TPU:1 before, /device:TPU:6 now
where the time goes in v5:
time: 68.9 us; the launch traced here: 68.3 us
  starting transfers between devices  42.2 us (61%)
  Pallas kernels  12.7 us (18%)
  waiting for transfers between devices  12.3 us (18%)
  local copies, waits for them, and re-layouts  0.7 us (1%)
    ppermute x4, starting transfers between devices, over_y(): lax.ppermute(block, 'y', [(i, (i + step) % targets) for i in range(target...  16.3 us
    all_to_all x1, starting transfers between devices, body(): coeffs = lax.all_to_all(send, ('x', 'z'), 0, 0, tiled=True)  13.6 us
    pallas_call x6, Pallas kernels, whole(): pl.pallas_call(kernel, out_shape=out, in_specs=[scalars if n in smem else...  12.7 us
    all_to_all x1, waiting for transfers between devices, body(): parts = lax.all_to_all(parts, 'y', 0, 0, tiled=True)  6.34 us
    ppermute x4, waiting for transfers between devices, over_y(): lax.ppermute(block, 'y', [(i, (i + step) % targets) for i in range(target...  5.47 us
    ppermute x1, starting transfers between devices, body(): high = lax.ppermute(stack, leaf_axes, [(i + 1, i) for i in range(subs - 1)])  4.87 us
    all_to_all x1, starting transfers between devices, body(): parts = lax.all_to_all(parts, 'y', 0, 0, tiled=True)  3.62 us
    ppermute x1, starting transfers between devices, body(): low = lax.ppermute(stack, leaf_axes, [(i, i + 1) for i in range(subs - 1)])  1.92 us
  transfers between devices with their start and end apart: 9, of which 4 were waited for; matrix products, arithmetic and copies ran while one was open for 0% of the time, Pallas kernels for 6%

profile of v5, /device:TPU:6, one launch (start us, length us, event | category | flops | bytes accessed | tf_op | source)
XLA Modules:
  0.0 68.3 jit_solution(16796293908306889715)
XLA Ops:
  0.0 1.7 %shard_map.199 = f32[1,96,128]{2,1,0:T(8,128)} custom-call(f32[48,128]{1,0:T(8,128)} %bitcast.54, f32[8,128]{1,0:T(8,128)} %bitcast.58, f32[32,128]{1,0:T(8,128)} %bitcast.56, s32[1,6]{1,0:T(1,128)} %refs_3_.1, s32[1,6]{1,0:T(1,128)} %refs_4_.1, s32[1,4]{1,0:T(1,128)} %refs_5_.1, s32[1,4]{1,0:T(1,128)} %refs_6_.1), custom_call_target="tpu_custom_call" | custom-call | flops 1000000 | bytes 94288 | tf_op jit(solution)/shard_map/pallas_call | solution.py:307
  1.7 3.8 %shard_map.200 = (f32[384,128]{1,0:T(8,128)}, f32[32,40,128]{2,1,0:T(8,128)}) custom-call(f32[8,192,128]{2,1,0:T(8,128)} %refs_0_, f32[8,32,192]{2,1,0:T(8,128)} %refs_1_.1, f32[64,128]{1,0:T(8,128)} %bitcast.53, f32[32,128]{1,0:T(8,128)} %bitcast.55, f32[8,128]{1,0:T(8,128)} %bitcast.57), custom_call_target="tpu_custom_call" | custom-call | flops 60000000 | bytes 1888256 | tf_op jit(solution)/shard_map/pallas_call | solution.py:307
  5.5 0.0 copy-start.10
  5.6 0.0 copy-start.2
  5.6 13.6 %all-to-all-start = ((f32[32,40,128]{2,1,0:T(8,128)}), f32[32,40,128]{2,1,0:T(8,128)S(1)}, u32[]{:S(2)}, u32[]{:S(2)}) async-start(f32[32,40,128]{2,1,0:T(8,128)} %get-tuple-element.21), calls=%async_computation | async-start | bytes 1310720 | tf_op jit(solution)/shard_map/all_to_all | solution.py:390
  19.2 0.0 copy-done.10
  19.2 7.7 %collective-permute-start.2 = (f32[1,96,128]{2,0,1:T(1,128)S(1)}, f32[1,96,128]{2,0,1:T(1,128)S(1)}, u32[]{:S(2)}, u32[]{:S(2)}) collective-permute-start(f32[1,96,128]{2,0,1:T(1,128)S(1)} %bitcast.51), channel_id=1, source_target_pairs={{0,256},{64,320},{128,384},{192,448},{256,0},{320,64},{384,128},{4... | collective-permute-start | bytes 147464 | tf_op jit(solution)/shard_map/ppermute | solution.py:387
  26.9 0.0 copy-done.2
  26.9 4.9 %collective-permute-start.1 = (f32[384,128]{1,0:T(8,128)S(1)}, f32[384,128]{1,0:T(8,128)S(1)}, u32[]{:S(2)}, u32[]{:S(2)}) collective-permute-start(f32[384,128]{1,0:T(8,128)S(1)} %copy-done.2), channel_id=1, source_target_pairs={{1,0},{2,1},{3,2},{4,3},{5,4},{6,5},{7,6},{8,7},{9,8},{10,9},{11,1... | collective-permute-start | bytes 589832 | tf_op jit(solution)/shard_map/ppermute | solution.py:394
  31.8 1.9 %collective-permute-start = (f32[384,128]{1,0:T(8,128)S(1)}, f32[384,128]{1,0:T(8,128)S(1)}, u32[]{:S(2)}, u32[]{:S(2)}) collective-permute-start(f32[384,128]{1,0:T(8,128)S(1)} %copy-done.2), channel_id=1, source_target_pairs={{0,1},{1,2},{2,3},{3,4},{4,5},{5,6},{6,7},{7,8},{8,9},{9,10},{10,1... | collective-permute-start | bytes 589832 | tf_op jit(solution)/shard_map/ppermute | solution.py:393
  33.7 0.0 collective-permute-done.2
  33.7 0.1 pad_maximum_fusion
  33.8 2.4 %collective-permute-start.5 = (f32[2,96,128]{2,0,1:T(2,128)S(1)}, f32[2,96,128]{2,0,1:T(2,128)S(1)}, u32[]{:S(2)}, u32[]{:S(2)}) collective-permute-start(f32[2,96,128]{2,0,1:T(2,128)S(1)} %pad_maximum_fusion), channel_id=1, source_target_pairs={{0,448},{64,0},{128,64},{192,128},{256,192},{320,256},{384,320},{4... | collective-permute-start | bytes 294920 | tf_op jit(solution)/shard_map/ppermute | solution.py:387
  36.2 3.6 %collective-permute-start.4 = (f32[2,96,128]{2,0,1:T(2,128)S(1)}, f32[2,96,128]{2,0,1:T(2,128)S(1)}, u32[]{:S(2)}, u32[]{:S(2)}) collective-permute-start(f32[2,96,128]{2,0,1:T(2,128)S(1)} %pad_maximum_fusion), channel_id=1, source_target_pairs={{0,128},{64,192},{128,256},{192,320},{256,384},{320,448},{384,0},{... | collective-permute-start | bytes 294920 | tf_op jit(solution)/shard_map/ppermute | solution.py:387
  39.8 2.6 %collective-permute-start.3 = (f32[2,96,128]{2,0,1:T(2,128)S(1)}, f32[2,96,128]{2,0,1:T(2,128)S(1)}, u32[]{:S(2)}, u32[]{:S(2)}) collective-permute-start(f32[2,96,128]{2,0,1:T(2,128)S(1)} %pad_maximum_fusion), channel_id=1, source_target_pairs={{0,64},{64,128},{128,192},{192,256},{256,320},{320,384},{384,448},... | collective-permute-start | bytes 294920 | tf_op jit(solution)/shard_map/ppermute | solution.py:387
  42.4 0.0 collective-permute-done.5
  42.4 3.0 %collective-permute-done.4 = f32[2,96,128]{2,0,1:T(2,128)S(1)} collective-permute-done((f32[2,96,128]{2,0,1:T(2,128)S(1)}, f32[2,96,128]{2,0,1:T(2,128)S(1)}, u32[]{:S(2)}, u32[]{:S(2)}) %collective-permute-start.4) | collective-permute-done | bytes 98336 | tf_op jit(solution)/shard_map/ppermute | solution.py:387
  45.5 2.4 %collective-permute-done.3 = f32[2,96,128]{2,0,1:T(2,128)S(1)} collective-permute-done((f32[2,96,128]{2,0,1:T(2,128)S(1)}, f32[2,96,128]{2,0,1:T(2,128)S(1)}, u32[]{:S(2)}, u32[]{:S(2)}) %collective-permute-start.3) | collective-permute-done | bytes 98336 | tf_op jit(solution)/shard_map/ppermute | solution.py:387
  47.9 0.0 collective-permute-done.1.high_ref
  47.9 0.0 collective-permute-done.low_ref
  47.9 0.0 all-to-all-done.refs_0_
  47.9 1.9 %collective-permute-start.6 = (f32[32,40,128]{2,1,0:T(8,128)S(1)}, f32[32,40,128]{2,1,0:T(8,128)S(1)}, u32[]{:S(2)}, u32[]{:S(2)}) collective-permute-start(f32[32,40,128]{2,1,0:T(8,128)S(1)} %all-to-all-done.refs_0_), channel_id=1, source_target_pairs={{0,32},{32,0},{1,33},{33,1},{2,34},{34,2},{3,35},{35,3},{4,36},{36... | collective-permute-start | bytes 1966088 | tf_op jit(solution)/shard_map/ppermute | solution.py:396
  49.9 1.5 %shard_map.201.refs_9_ = f32[8,32,128]{2,1,0:T(8,128)S(1)} custom-call(f32[32,40,128]{2,1,0:T(8,128)S(1)} %all-to-all-done.refs_0_, f32[2,96,128]{2,1,0:T(8,128)S(1)} %copy.30.refs_1_, f32[2,96,128]{2,1,0:T(8,128)S(1)} %copy.31.refs_2_, f32[2,96,128]{2,1,0:T(8,128)S(1)} %copy.32.refs_3_, f32[2,96,128]{2,1,0:T(8,128)S(1)} %copy.33.refs_4_, ...), custom_call_target="tpu_custom_call" | custom-call | flops 50000000 | bytes 1183744 | tf_op jit(solution)/shard_map/pallas_call | solution.py:307
  51.4 0.5 collective-permute-done.6.refs_0_
  51.9 0.0 copy-start.1
  51.9 0.0 copy-start.3
  51.9 0.0 copy-start.4
  51.9 0.0 copy-start.5
  51.9 0.0 copy-start.7
  51.9 0.0 copy-start.9
  51.9 2.2 %shard_map.202 = f32[8,32,128]{2,1,0:T(8,128)} custom-call(f32[32,40,128]{2,1,0:T(8,128)S(1)} %collective-permute-done.6.refs_0_, f32[2,96,128]{2,1,0:T(8,128)S(1)} %copy.30.refs_1_, f32[2,96,128]{2,1,0:T(8,128)S(1)} %copy.31.refs_2_, f32[2,96,128]{2,1,0:T(8,128)S(1)} %copy.32.refs_3_, f32[2,96,128]{2,1,0:T(8,128)S(1)} %copy.33.refs_4_, ...), custom_call_target="tpu_custom_call" | custom-call | flops 50000000 | bytes 1314816 | tf_op jit(solution)/shard_map/pallas_call | solution.py:307
  54.1 0.0 copy-start
  54.1 3.6 %all-to-all-start.1 = ((f32[8,32,128]{2,1,0:T(8,128)}), f32[8,32,128]{2,1,0:T(8,128)S(1)}, u32[]{:S(2)}, u32[]{:S(2)}) async-start(f32[8,32,128]{2,1,0:T(8,128)} %shard_map.202), calls=%async_computation.1 | async-start | bytes 262144 | tf_op jit(solution)/shard_map/all_to_all | solution.py:414
  57.7 0.0 copy-start.6
  57.7 0.0 copy-start.8
  57.7 0.0 copy-done.1
  57.7 0.0 copy-done.3
  57.8 0.0 copy-done.4
  57.8 0.0 copy-done.5
  57.8 0.0 copy-done.7
  57.8 0.0 copy-done.9
  57.8 0.0 copy-done
  57.8 0.6 copy-done.6
  58.4 0.0 copy-done.8
  58.4 2.4 %shard_map.203 = (f32[8,192,128]{2,1,0:T(8,128)S(1)}, bf16[8,192,128]{2,1,0:T(8,128)(2,1)S(1)}) custom-call(f32[384,128]{1,0:T(8,128)S(1)} %collective-permute-done.low_ref, f32[384,128]{1,0:T(8,128)S(1)} %copy-done.2, f32[384,128]{1,0:T(8,128)S(1)} %collective-permute-done.1.high_ref, f32[384,128]{1,0:T(8,128)S(1)} %bitcast.47, f32[192,128]{1,0:T(8,128)S(1)} %bitcast.48, ...), custom_call_target="tpu_custom_call" | custom-call | flops 100000000 | bytes 2310720 | tf_op jit(solution)/shard_map/pallas_call | solution.py:307
  60.8 6.3 %all-to-all-done.1.parts_ref = f32[8,32,128]{2,1,0:T(8,128)S(1)} async-done(((f32[8,32,128]{2,1,0:T(8,128)}), f32[8,32,128]{2,1,0:T(8,128)S(1)}, u32[]{:S(2)}, u32[]{:S(2)}) %all-to-all-start.1) | async-done | bytes 131104 | tf_op jit(solution)/shard_map/all_to_all | solution.py:414
  67.2 1.2 %shard_map.204 = f32[8,192,128]{2,1,0:T(8,128)} custom-call(f32[8,32,128]{2,1,0:T(8,128)S(1)} %all-to-all-done.1.parts_ref, f32[8,192,128]{2,1,0:T(8,128)S(1)} %get-tuple-element.33.fixed_ref, bf16[8,192,128]{2,1,0:T(8,128)(2,1)S(1)} %get-tuple-element.34.slope_ref), custom_call_target="tpu_custom_call" | custom-call | flops 50000000 | bytes 2097152 | tf_op jit(solution)/shard_map/pallas_call | solution.py:307
  (6 shorter events, 0.0 us)
Async XLA Ops:
  5.5 13.6 %copy-start.10 = (f32[1,96,128]{2,1,0:T(8,128)S(1)}, f32[1,96,128]{2,1,0:T(8,128)}, u32[]{:S(2)}) copy-start(f32[1,96,128]{2,1,0:T(8,128)} %shard_map.199) | copy-start | bytes 147460
  5.6 21.4 %copy-start.2 = (f32[384,128]{1,0:T(8,128)S(1)}, f32[384,128]{1,0:T(8,128)}, u32[]{:S(2)}) copy-start(f32[384,128]{1,0:T(8,128)} %get-tuple-element.22.own_ref) | copy-start | bytes 589828
  5.6 42.3 %all-to-all-start = ((f32[32,40,128]{2,1,0:T(8,128)}), f32[32,40,128]{2,1,0:T(8,128)S(1)}, u32[]{:S(2)}, u32[]{:S(2)}) async-start(f32[32,40,128]{2,1,0:T(8,128)} %get-tuple-element.21), calls=%async_computation | async-start | bytes 1310720 | tf_op jit(solution)/shard_map/all_to_all | solution.py:390
  19.2 14.6 %collective-permute-start.2 = (f32[1,96,128]{2,0,1:T(1,128)S(1)}, f32[1,96,128]{2,0,1:T(1,128)S(1)}, u32[]{:S(2)}, u32[]{:S(2)}) collective-permute-start(f32[1,96,128]{2,0,1:T(1,128)S(1)} %bitcast.51), channel_id=1, source_target_pairs={{0,256},{64,320},{128,384},{192,448},{256,0},{320,64},{384,128},{4... | collective-permute-start | bytes 147464 | tf_op jit(solution)/shard_map/ppermute | solution.py:387
  26.9 21.0 %collective-permute-start.1 = (f32[384,128]{1,0:T(8,128)S(1)}, f32[384,128]{1,0:T(8,128)S(1)}, u32[]{:S(2)}, u32[]{:S(2)}) collective-permute-start(f32[384,128]{1,0:T(8,128)S(1)} %copy-done.2), channel_id=1, source_target_pairs={{1,0},{2,1},{3,2},{4,3},{5,4},{6,5},{7,6},{8,7},{9,8},{10,9},{11,1... | collective-permute-start | bytes 589832 | tf_op jit(solution)/shard_map/ppermute | solution.py:394
  31.8 16.1 %collective-permute-start = (f32[384,128]{1,0:T(8,128)S(1)}, f32[384,128]{1,0:T(8,128)S(1)}, u32[]{:S(2)}, u32[]{:S(2)}) collective-permute-start(f32[384,128]{1,0:T(8,128)S(1)} %copy-done.2), channel_id=1, source_target_pairs={{0,1},{1,2},{2,3},{3,4},{4,5},{5,6},{6,7},{7,8},{8,9},{9,10},{10,1... | collective-permute-start | bytes 589832 | tf_op jit(solution)/shard_map/ppermute | solution.py:393
  33.8 8.6 %collective-permute-start.5 = (f32[2,96,128]{2,0,1:T(2,128)S(1)}, f32[2,96,128]{2,0,1:T(2,128)S(1)}, u32[]{:S(2)}, u32[]{:S(2)}) collective-permute-start(f32[2,96,128]{2,0,1:T(2,128)S(1)} %pad_maximum_fusion), channel_id=1, source_target_pairs={{0,448},{64,0},{128,64},{192,128},{256,192},{320,256},{384,320},{4... | collective-permute-start | bytes 294920 | tf_op jit(solution)/shard_map/ppermute | solution.py:387
  36.2 9.2 %collective-permute-start.4 = (f32[2,96,128]{2,0,1:T(2,128)S(1)}, f32[2,96,128]{2,0,1:T(2,128)S(1)}, u32[]{:S(2)}, u32[]{:S(2)}) collective-permute-start(f32[2,96,128]{2,0,1:T(2,128)S(1)} %pad_maximum_fusion), channel_id=1, source_target_pairs={{0,128},{64,192},{128,256},{192,320},{256,384},{320,448},{384,0},{... | collective-permute-start | bytes 294920 | tf_op jit(solution)/shard_map/ppermute | solution.py:387
  39.8 8.1 %collective-permute-start.3 = (f32[2,96,128]{2,0,1:T(2,128)S(1)}, f32[2,96,128]{2,0,1:T(2,128)S(1)}, u32[]{:S(2)}, u32[]{:S(2)}) collective-permute-start(f32[2,96,128]{2,0,1:T(2,128)S(1)} %pad_maximum_fusion), channel_id=1, source_target_pairs={{0,64},{64,128},{128,192},{192,256},{256,320},{320,384},{384,448},... | collective-permute-start | bytes 294920 | tf_op jit(solution)/shard_map/ppermute | solution.py:387
  47.9 4.0 %collective-permute-start.6 = (f32[32,40,128]{2,1,0:T(8,128)S(1)}, f32[32,40,128]{2,1,0:T(8,128)S(1)}, u32[]{:S(2)}, u32[]{:S(2)}) collective-permute-start(f32[32,40,128]{2,1,0:T(8,128)S(1)} %all-to-all-done.refs_0_), channel_id=1, source_target_pairs={{0,32},{32,0},{1,33},{33,1},{2,34},{34,2},{3,35},{35,3},{4,36},{36... | collective-permute-start | bytes 1966088 | tf_op jit(solution)/shard_map/ppermute | solution.py:396
  51.9 5.9 %copy-start.1 = (f32[8,6,1024]{2,0,1:T(8,128)S(1)}, f32[8,6,1024]{2,0,1:T(8,128)}, u32[]{:S(2)}) copy-start(f32[8,6,1024]{2,0,1:T(8,128)} %param.26) | copy-start | bytes 589828
  51.9 5.9 %copy-start.3 = (f32[4,6,1024]{2,0,1:T(4,128)S(1)}, f32[4,6,1024]{2,0,1:T(4,128)}, u32[]{:S(2)}) copy-start(f32[4,6,1024]{2,0,1:T(4,128)} %param.27) | copy-start | bytes 294916
  51.9 5.9 %copy-start.4 = (f32[8,1024]{1,0:T(8,128)S(1)}, f32[8,1024]{1,0:T(8,128)}, u32[]{:S(2)}) copy-start(f32[8,1024]{1,0:T(8,128)} %param.38) | copy-start | bytes 98308
  51.9 5.9 %copy-start.5 = (f32[4,1024]{1,0:T(4,128)S(1)}, f32[4,1024]{1,0:T(4,128)}, u32[]{:S(2)}) copy-start(f32[4,1024]{1,0:T(4,128)} %param.39) | copy-start | bytes 49156
  51.9 5.9 %copy-start.7 = (s32[8,6]{1,0:T(8,128)S(1)}, s32[8,6]{1,0:T(8,128)}, u32[]{:S(2)}) copy-start(s32[8,6]{1,0:T(8,128)} %mask_leaf.1) | copy-start | bytes 580
  51.9 5.9 %copy-start.9 = (s32[4,6]{1,0:T(4,128)S(1)}, s32[4,6]{1,0:T(4,128)}, u32[]{:S(2)}) copy-start(s32[4,6]{1,0:T(4,128)} %mask_pair.1) | copy-start | bytes 292
  54.1 3.7 %copy-start = (f32[8,32,192]{2,1,0:T(8,128)S(1)}, f32[8,32,192]{2,1,0:T(8,128)}, u32[]{:S(2)}) copy-start(f32[8,32,192]{2,1,0:T(8,128)} %basis.1) | copy-start | bytes 589828
  54.1 13.1 %all-to-all-start.1 = ((f32[8,32,128]{2,1,0:T(8,128)}), f32[8,32,128]{2,1,0:T(8,128)S(1)}, u32[]{:S(2)}, u32[]{:S(2)}) async-start(f32[8,32,128]{2,1,0:T(8,128)} %shard_map.202), calls=%async_computation.1 | async-start | bytes 262144 | tf_op jit(solution)/shard_map/all_to_all | solution.py:414
  57.7 0.7 %copy-start.6 = (s32[8,6]{1,0:T(8,128)S(1)}, s32[8,6]{1,0:T(8,128)}, u32[]{:S(2)}) copy-start(s32[8,6]{1,0:T(8,128)} %list_leaf.1) | copy-start | bytes 580
  57.7 0.7 %copy-start.8 = (s32[4,6]{1,0:T(4,128)S(1)}, s32[4,6]{1,0:T(4,128)}, u32[]{:S(2)}) copy-start(s32[4,6]{1,0:T(4,128)} %list_pair.1) | copy-start | bytes 292

commit v6 on v5

--- a/solution.py
+++ b/solution.py
@@ -386,7 +386,9 @@
     def over_y(block, step):
         return lax.ppermute(block, "y", [(i, (i + step) % targets) for i in range(targets)])
 
-    weights = jnp.concatenate([weights, over_y(weights, targets // 2)], axis=0)
+    come = over_y(weights, targets // 2)
+    come, send = lax.optimization_barrier((come, send))
+    weights = jnp.concatenate([weights, come], axis=0)
     coeffs = lax.all_to_all(send, ("x", "z"), 0, 0, tiled=True)
     weights = [weights] + [over_y(weights, step) for step in shifts(targets)]
     leaf_axes = ("x", "z")

time: 68.9 us -> 71 us (1.030)
  starting transfers between devices: 42.2 us -> 44.4 us
    all_to_all x1, starting transfers between devices: 3.62 us -> 5.12 us  [body(): parts = lax.all_to_all(parts, 'y', 0, 0, tiled=True)]
  transfers between devices with their start and end apart: 9 -> 9, of which waited for: 4 -> 4; matrix products, arithmetic and copies ran while one was open for 0% -> 0% of each run, Pallas kernels for 6% -> 11%
where the time goes in v6:
time: 71 us; the launch traced here: 70.5 us
  starting transfers between devices  44.4 us (63%)
  Pallas kernels  12.7 us (18%)
  waiting for transfers between devices  12.2 us (17%)
    ppermute x4, starting transfers between devices, over_y(): lax.ppermute(block, 'y', [(i, (i + step) % targets) for i in range(target...  17 us
    all_to_all x1, starting transfers between devices, body(): coeffs = lax.all_to_all(send, ('x', 'z'), 0, 0, tiled=True)  13.6 us
    pallas_call x6, Pallas kernels, whole(): pl.pallas_call(kernel, out_shape=out, in_specs=[scalars if n in smem else...  12.7 us
    all_to_all x1, waiting for transfers between devices, body(): parts = lax.all_to_all(parts, 'y', 0, 0, tiled=True)  6.27 us
    ppermute x4, waiting for transfers between devices, over_y(): lax.ppermute(block, 'y', [(i, (i + step) % targets) for i in range(target...  5.5 us
    all_to_all x1, starting transfers between devices, body(): parts = lax.all_to_all(parts, 'y', 0, 0, tiled=True)  5.12 us
    ppermute x1, starting transfers between devices, body(): high = lax.ppermute(stack, leaf_axes, [(i + 1, i) for i in range(subs - 1)])  4.87 us
    ppermute x1, starting transfers between devices, body(): low = lax.ppermute(stack, leaf_axes, [(i, i + 1) for i in range(subs - 1)])  1.92 us
  transfers between devices with their start and end apart: 9, of which 4 were waited for; matrix products, arithmetic and copies ran while one was open for 0% of the time, Pallas kernels for 11%

profile of v6, /device:TPU:6, one launch (start us, length us, event | category | flops | bytes accessed | tf_op | source)
XLA Modules:
  0.0 70.5 jit_solution(15310518965352616274)
XLA Ops:
  0.0 1.7 %shard_map.199 = f32[1,96,128]{2,1,0:T(8,128)} custom-call(f32[48,128]{1,0:T(8,128)} %bitcast.54, f32[8,128]{1,0:T(8,128)} %bitcast.58, f32[32,128]{1,0:T(8,128)} %bitcast.56, s32[1,6]{1,0:T(1,128)} %refs_3_.1, s32[1,6]{1,0:T(1,128)} %refs_4_.1, s32[1,4]{1,0:T(1,128)} %refs_5_.1, s32[1,4]{1,0:T(1,128)} %refs_6_.1), custom_call_target="tpu_custom_call" | custom-call | flops 1000000 | bytes 94288 | tf_op jit(solution)/shard_map/pallas_call | solution.py:307
  1.7 7.7 %collective-permute-start = (f32[1,96,128]{2,0,1:T(1,128)}, f32[1,96,128]{2,0,1:T(1,128)S(1)}, u32[]{:S(2)}, u32[]{:S(2)}) collective-permute-start(f32[1,96,128]{2,0,1:T(1,128)} %bitcast.51), channel_id=1, source_target_pairs={{0,256},{64,320},{128,384},{192,448},{256,0},{320,64},{384,128},{4... | collective-permute-start | bytes 147464 | tf_op jit(solution)/shard_map/ppermute | solution.py:387
  9.5 3.8 %shard_map.200 = (f32[384,128]{1,0:T(8,128)}, f32[32,40,128]{2,1,0:T(8,128)}) custom-call(f32[8,192,128]{2,1,0:T(8,128)} %refs_0_, f32[8,32,192]{2,1,0:T(8,128)} %refs_1_.1, f32[64,128]{1,0:T(8,128)} %bitcast.53, f32[32,128]{1,0:T(8,128)} %bitcast.55, f32[8,128]{1,0:T(8,128)} %bitcast.57), custom_call_target="tpu_custom_call" | custom-call | flops 60000000 | bytes 1888256 | tf_op jit(solution)/shard_map/pallas_call | solution.py:307
  13.3 0.0 collective-permute-done
  13.3 0.0 copy-start.2
  13.3 0.0 copy-start.10
  13.3 13.6 %all-to-all-start = ((f32[32,40,128]{2,1,0:T(8,128)}), f32[32,40,128]{2,1,0:T(8,128)S(1)}, u32[]{:S(2)}, u32[]{:S(2)}) async-start(f32[32,40,128]{2,1,0:T(8,128)} %get-tuple-element.25), calls=%async_computation | async-start | bytes 1310720 | tf_op jit(solution)/shard_map/all_to_all | solution.py:392
  26.9 0.0 copy-done.2
  26.9 4.9 %collective-permute-start.2 = (f32[384,128]{1,0:T(8,128)S(1)}, f32[384,128]{1,0:T(8,128)S(1)}, u32[]{:S(2)}, u32[]{:S(2)}) collective-permute-start(f32[384,128]{1,0:T(8,128)S(1)} %copy-done.2), channel_id=1, source_target_pairs={{1,0},{2,1},{3,2},{4,3},{5,4},{6,5},{7,6},{8,7},{9,8},{10,9},{11,1... | collective-permute-start | bytes 589832 | tf_op jit(solution)/shard_map/ppermute | solution.py:396
  31.8 1.9 %collective-permute-start.1 = (f32[384,128]{1,0:T(8,128)S(1)}, f32[384,128]{1,0:T(8,128)S(1)}, u32[]{:S(2)}, u32[]{:S(2)}) collective-permute-start(f32[384,128]{1,0:T(8,128)S(1)} %copy-done.2), channel_id=1, source_target_pairs={{0,1},{1,2},{2,3},{3,4},{4,5},{5,6},{6,7},{7,8},{8,9},{9,10},{10,1... | collective-permute-start | bytes 589832 | tf_op jit(solution)/shard_map/ppermute | solution.py:395
  33.7 0.0 copy-done.10
  33.7 0.1 pad_maximum_fusion
  33.8 4.4 %collective-permute-start.5 = (f32[2,96,128]{2,0,1:T(2,128)S(1)}, f32[2,96,128]{2,0,1:T(2,128)S(1)}, u32[]{:S(2)}, u32[]{:S(2)}) collective-permute-start(f32[2,96,128]{2,0,1:T(2,128)S(1)} %pad_maximum_fusion), channel_id=1, source_target_pairs={{0,448},{64,0},{128,64},{192,128},{256,192},{320,256},{384,320},{4... | collective-permute-start | bytes 294920 | tf_op jit(solution)/shard_map/ppermute | solution.py:387
  38.3 1.9 %collective-permute-start.4 = (f32[2,96,128]{2,0,1:T(2,128)S(1)}, f32[2,96,128]{2,0,1:T(2,128)S(1)}, u32[]{:S(2)}, u32[]{:S(2)}) collective-permute-start(f32[2,96,128]{2,0,1:T(2,128)S(1)} %pad_maximum_fusion), channel_id=1, source_target_pairs={{0,128},{64,192},{128,256},{192,320},{256,384},{320,448},{384,0},{... | collective-permute-start | bytes 294920 | tf_op jit(solution)/shard_map/ppermute | solution.py:387
  40.2 2.9 %collective-permute-start.3 = (f32[2,96,128]{2,0,1:T(2,128)S(1)}, f32[2,96,128]{2,0,1:T(2,128)S(1)}, u32[]{:S(2)}, u32[]{:S(2)}) collective-permute-start(f32[2,96,128]{2,0,1:T(2,128)S(1)} %pad_maximum_fusion), channel_id=1, source_target_pairs={{0,64},{64,128},{128,192},{192,256},{256,320},{320,384},{384,448},... | collective-permute-start | bytes 294920 | tf_op jit(solution)/shard_map/ppermute | solution.py:387
  43.1 0.0 collective-permute-done.5
  43.1 4.6 %collective-permute-done.4 = f32[2,96,128]{2,0,1:T(2,128)S(1)} collective-permute-done((f32[2,96,128]{2,0,1:T(2,128)S(1)}, f32[2,96,128]{2,0,1:T(2,128)S(1)}, u32[]{:S(2)}, u32[]{:S(2)}) %collective-permute-start.4) | collective-permute-done | bytes 98336 | tf_op jit(solution)/shard_map/ppermute | solution.py:387
  47.7 0.9 %collective-permute-done.3 = f32[2,96,128]{2,0,1:T(2,128)S(1)} collective-permute-done((f32[2,96,128]{2,0,1:T(2,128)S(1)}, f32[2,96,128]{2,0,1:T(2,128)S(1)}, u32[]{:S(2)}, u32[]{:S(2)}) %collective-permute-start.3) | collective-permute-done | bytes 98336 | tf_op jit(solution)/shard_map/ppermute | solution.py:387
  48.6 0.0 collective-permute-done.2.high_ref
  48.6 0.0 collective-permute-done.1.low_ref
  48.6 0.0 all-to-all-done.refs_0_
  48.6 1.9 %collective-permute-start.6 = (f32[32,40,128]{2,1,0:T(8,128)S(1)}, f32[32,40,128]{2,1,0:T(8,128)S(1)}, u32[]{:S(2)}, u32[]{:S(2)}) collective-permute-start(f32[32,40,128]{2,1,0:T(8,128)S(1)} %all-to-all-done.refs_0_), channel_id=1, source_target_pairs={{0,32},{32,0},{1,33},{33,1},{2,34},{34,2},{3,35},{35,3},{4,36},{36... | collective-permute-start | bytes 1966088 | tf_op jit(solution)/shard_map/ppermute | solution.py:398
  50.6 1.5 %shard_map.201.refs_9_ = f32[8,32,128]{2,1,0:T(8,128)S(1)} custom-call(f32[32,40,128]{2,1,0:T(8,128)S(1)} %all-to-all-done.refs_0_, f32[2,96,128]{2,1,0:T(8,128)S(1)} %copy.30.refs_1_, f32[2,96,128]{2,1,0:T(8,128)S(1)} %copy.31.refs_2_, f32[2,96,128]{2,1,0:T(8,128)S(1)} %copy.32.refs_3_, f32[2,96,128]{2,1,0:T(8,128)S(1)} %copy.33.refs_4_, ...), custom_call_target="tpu_custom_call" | custom-call | flops 50000000 | bytes 1183744 | tf_op jit(solution)/shard_map/pallas_call | solution.py:307
  52.1 0.5 collective-permute-done.6.refs_0_
  52.6 0.0 copy-start.1
  52.6 0.0 copy-start.3
  52.6 0.0 copy-start.4
  52.6 0.0 copy-start.5
  52.6 0.0 copy-start.7
  52.6 0.0 copy-start.9
  52.7 2.2 %shard_map.202 = f32[8,32,128]{2,1,0:T(8,128)} custom-call(f32[32,40,128]{2,1,0:T(8,128)S(1)} %collective-permute-done.6.refs_0_, f32[2,96,128]{2,1,0:T(8,128)S(1)} %copy.30.refs_1_, f32[2,96,128]{2,1,0:T(8,128)S(1)} %copy.31.refs_2_, f32[2,96,128]{2,1,0:T(8,128)S(1)} %copy.32.refs_3_, f32[2,96,128]{2,1,0:T(8,128)S(1)} %copy.33.refs_4_, ...), custom_call_target="tpu_custom_call" | custom-call | flops 50000000 | bytes 1314816 | tf_op jit(solution)/shard_map/pallas_call | solution.py:307
  54.8 0.0 copy-start
  54.8 5.1 %all-to-all-start.1 = ((f32[8,32,128]{2,1,0:T(8,128)}), f32[8,32,128]{2,1,0:T(8,128)S(1)}, u32[]{:S(2)}, u32[]{:S(2)}) async-start(f32[8,32,128]{2,1,0:T(8,128)} %shard_map.202), calls=%async_computation.1 | async-start | bytes 262144 | tf_op jit(solution)/shard_map/all_to_all | solution.py:416
  60.0 0.0 copy-start.6
  60.0 0.0 copy-start.8
  60.0 0.0 copy-done.1
  60.0 0.0 copy-done.3
  60.0 0.0 copy-done.4
  60.0 0.0 copy-done.5
  60.0 0.0 copy-done.7
  60.0 0.0 copy-done.9
  60.0 0.0 copy-done
  60.0 0.6 copy-done.6
  60.6 0.0 copy-done.8
  60.6 2.4 %shard_map.203 = (f32[8,192,128]{2,1,0:T(8,128)S(1)}, bf16[8,192,128]{2,1,0:T(8,128)(2,1)S(1)}) custom-call(f32[384,128]{1,0:T(8,128)S(1)} %collective-permute-done.1.low_ref, f32[384,128]{1,0:T(8,128)S(1)} %copy-done.2, f32[384,128]{1,0:T(8,128)S(1)} %collective-permute-done.2.high_ref, f32[384,128]{1,0:T(8,128)S(1)} %bitcast.47, f32[192,128]{1,0:T(8,128)S(1)} %bitcast.48, ...), custom_call_target="tpu_custom_call" | custom-call | flops 100000000 | bytes 2310720 | tf_op jit(solution)/shard_map/pallas_call | solution.py:307
  63.1 6.3 %all-to-all-done.1.parts_ref = f32[8,32,128]{2,1,0:T(8,128)S(1)} async-done(((f32[8,32,128]{2,1,0:T(8,128)}), f32[8,32,128]{2,1,0:T(8,128)S(1)}, u32[]{:S(2)}, u32[]{:S(2)}) %all-to-all-start.1) | async-done | bytes 131104 | tf_op jit(solution)/shard_map/all_to_all | solution.py:416
  69.3 1.2 %shard_map.204 = f32[8,192,128]{2,1,0:T(8,128)} custom-call(f32[8,32,128]{2,1,0:T(8,128)S(1)} %all-to-all-done.1.parts_ref, f32[8,192,128]{2,1,0:T(8,128)S(1)} %get-tuple-element.37.fixed_ref, bf16[8,192,128]{2,1,0:T(8,128)(2,1)S(1)} %get-tuple-element.38.slope_ref), custom_call_target="tpu_custom_call" | custom-call | flops 50000000 | bytes 2097152 | tf_op jit(solution)/shard_map/pallas_call | solution.py:307
  (6 shorter events, 0.0 us)
Async XLA Ops:
  1.7 11.6 %collective-permute-start = (f32[1,96,128]{2,0,1:T(1,128)}, f32[1,96,128]{2,0,1:T(1,128)S(1)}, u32[]{:S(2)}, u32[]{:S(2)}) collective-permute-start(f32[1,96,128]{2,0,1:T(1,128)} %bitcast.51), channel_id=1, source_target_pairs={{0,256},{64,320},{128,384},{192,448},{256,0},{320,64},{384,128},{4... | collective-permute-start | bytes 147464 | tf_op jit(solution)/shard_map/ppermute | solution.py:387
  13.3 13.6 %copy-start.2 = (f32[384,128]{1,0:T(8,128)S(1)}, f32[384,128]{1,0:T(8,128)}, u32[]{:S(2)}) copy-start(f32[384,128]{1,0:T(8,128)} %get-tuple-element.26.own_ref) | copy-start | bytes 589828
  13.3 20.4 %copy-start.10 = (f32[1,96,128]{2,1,0:T(8,128)S(1)}, f32[1,96,128]{2,1,0:T(8,128)}, u32[]{:S(2)}) copy-start(f32[1,96,128]{2,1,0:T(8,128)} %shard_map.199) | copy-start | bytes 147460
  13.3 35.3 %all-to-all-start = ((f32[32,40,128]{2,1,0:T(8,128)}), f32[32,40,128]{2,1,0:T(8,128)S(1)}, u32[]{:S(2)}, u32[]{:S(2)}) async-start(f32[32,40,128]{2,1,0:T(8,128)} %get-tuple-element.25), calls=%async_computation | async-start | bytes 1310720 | tf_op jit(solution)/shard_map/all_to_all | solution.py:392
  26.9 21.7 %collective-permute-start.2 = (f32[384,128]{1,0:T(8,128)S(1)}, f32[384,128]{1,0:T(8,128)S(1)}, u32[]{:S(2)}, u32[]{:S(2)}) collective-permute-start(f32[384,128]{1,0:T(8,128)S(1)} %copy-done.2), channel_id=1, source_target_pairs={{1,0},{2,1},{3,2},{4,3},{5,4},{6,5},{7,6},{8,7},{9,8},{10,9},{11,1... | collective-permute-start | bytes 589832 | tf_op jit(solution)/shard_map/ppermute | solution.py:396
  31.8 16.8 %collective-permute-start.1 = (f32[384,128]{1,0:T(8,128)S(1)}, f32[384,128]{1,0:T(8,128)S(1)}, u32[]{:S(2)}, u32[]{:S(2)}) collective-permute-start(f32[384,128]{1,0:T(8,128)S(1)} %copy-done.2), channel_id=1, source_target_pairs={{0,1},{1,2},{2,3},{3,4},{4,5},{5,6},{6,7},{7,8},{8,9},{9,10},{10,1... | collective-permute-start | bytes 589832 | tf_op jit(solution)/shard_map/ppermute | solution.py:395
  33.8 9.3 %collective-permute-start.5 = (f32[2,96,128]{2,0,1:T(2,128)S(1)}, f32[2,96,128]{2,0,1:T(2,128)S(1)}, u32[]{:S(2)}, u32[]{:S(2)}) collective-permute-start(f32[2,96,128]{2,0,1:T(2,128)S(1)} %pad_maximum_fusion), channel_id=1, source_target_pairs={{0,448},{64,0},{128,64},{192,128},{256,192},{320,256},{384,320},{4... | collective-permute-start | bytes 294920 | tf_op jit(solution)/shard_map/ppermute | solution.py:387
  38.3 9.5 %collective-permute-start.4 = (f32[2,96,128]{2,0,1:T(2,128)S(1)}, f32[2,96,128]{2,0,1:T(2,128)S(1)}, u32[]{:S(2)}, u32[]{:S(2)}) collective-permute-start(f32[2,96,128]{2,0,1:T(2,128)S(1)} %pad_maximum_fusion), channel_id=1, source_target_pairs={{0,128},{64,192},{128,256},{192,320},{256,384},{320,448},{384,0},{... | collective-permute-start | bytes 294920 | tf_op jit(solution)/shard_map/ppermute | solution.py:387
  40.2 8.4 %collective-permute-start.3 = (f32[2,96,128]{2,0,1:T(2,128)S(1)}, f32[2,96,128]{2,0,1:T(2,128)S(1)}, u32[]{:S(2)}, u32[]{:S(2)}) collective-permute-start(f32[2,96,128]{2,0,1:T(2,128)S(1)} %pad_maximum_fusion), channel_id=1, source_target_pairs={{0,64},{64,128},{128,192},{192,256},{256,320},{320,384},{384,448},... | collective-permute-start | bytes 294920 | tf_op jit(solution)/shard_map/ppermute | solution.py:387
  48.6 4.0 %collective-permute-start.6 = (f32[32,40,128]{2,1,0:T(8,128)S(1)}, f32[32,40,128]{2,1,0:T(8,128)S(1)}, u32[]{:S(2)}, u32[]{:S(2)}) collective-permute-start(f32[32,40,128]{2,1,0:T(8,128)S(1)} %all-to-all-done.refs_0_), channel_id=1, source_target_pairs={{0,32},{32,0},{1,33},{33,1},{2,34},{34,2},{3,35},{35,3},{4,36},{36... | collective-permute-start | bytes 1966088 | tf_op jit(solution)/shard_map/ppermute | solution.py:398
  52.6 7.3 %copy-start.1 = (f32[8,6,1024]{2,0,1:T(8,128)S(1)}, f32[8,6,1024]{2,0,1:T(8,128)}, u32[]{:S(2)}) copy-start(f32[8,6,1024]{2,0,1:T(8,128)} %param.26) | copy-start | bytes 589828
  52.6 7.4 %copy-start.3 = (f32[4,6,1024]{2,0,1:T(4,128)S(1)}, f32[4,6,1024]{2,0,1:T(4,128)}, u32[]{:S(2)}) copy-start(f32[4,6,1024]{2,0,1:T(4,128)} %param.27) | copy-start | bytes 294916
  52.6 7.4 %copy-start.4 = (f32[8,1024]{1,0:T(8,128)S(1)}, f32[8,1024]{1,0:T(8,128)}, u32[]{:S(2)}) copy-start(f32[8,1024]{1,0:T(8,128)} %param.38) | copy-start | bytes 98308
  52.6 7.4 %copy-start.5 = (f32[4,1024]{1,0:T(4,128)S(1)}, f32[4,1024]{1,0:T(4,128)}, u32[]{:S(2)}) copy-start(f32[4,1024]{1,0:T(4,128)} %param.39) | copy-start | bytes 49156
  52.6 7.4 %copy-start.7 = (s32[8,6]{1,0:T(8,128)S(1)}, s32[8,6]{1,0:T(8,128)}, u32[]{:S(2)}) copy-start(s32[8,6]{1,0:T(8,128)} %mask_leaf.1) | copy-start | bytes 580
  52.6 7.4 %copy-start.9 = (s32[4,6]{1,0:T(4,128)S(1)}, s32[4,6]{1,0:T(4,128)}, u32[]{:S(2)}) copy-start(s32[4,6]{1,0:T(4,128)} %mask_pair.1) | copy-start | bytes 292
  54.8 5.2 %copy-start = (f32[8,32,192]{2,1,0:T(8,128)S(1)}, f32[8,32,192]{2,1,0:T(8,128)}, u32[]{:S(2)}) copy-start(f32[8,32,192]{2,1,0:T(8,128)} %basis.1) | copy-start | bytes 589828
  54.8 14.5 %all-to-all-start.1 = ((f32[8,32,128]{2,1,0:T(8,128)}), f32[8,32,128]{2,1,0:T(8,128)S(1)}, u32[]{:S(2)}, u32[]{:S(2)}) async-start(f32[8,32,128]{2,1,0:T(8,128)} %shard_map.202), calls=%async_computation.1 | async-start | bytes 262144 | tf_op jit(solution)/shard_map/all_to_all | solution.py:416
  60.0 0.7 copy-start.6
  60.0 0.7 copy-start.8

commit v7 on v5

--- a/solution.py
+++ b/solution.py
@@ -82,10 +82,7 @@
     return copies
 
 
-def weights_kernel(*refs):
-    sources, out_ref, held, sems, natural = refs[:7], refs[7], refs[8:15], refs[15], refs[16]
-    for copy in fetch(sources, held, sems):
-        copy.wait()
+def weights_of(held, natural):
     couple, down, top, list_d, mask_d, list_t, mask_t = held
     slots, top_slots = list_d.shape[1], list_t.shape[1]
 
@@ -102,25 +99,34 @@
     tops = [top[pl.ds(k, ROWS8, stride=top_slots), :] * entry(mask_t, k) for k in range(top_slots)]
     store_natural(natural, 0, beside(tops))
     top_high, top_low = split(natural[...])
-    out_ref[0, 0:RANK, :] = beside(flats[:4])
-    out_ref[0, RANK : 2 * RANK, :] = jnp.where(lane < 64, beside(flats[4:]), ids)
-    out_ref[0, 2 * RANK : 3 * RANK, :] = dot_split(square(down[...]), top_high, top_low)
-
-
-def up_kernel(*refs):
-    sources, (stack_ref, send_ref), scratch = refs[:5], refs[5:7], refs[7:]
-    held, (sems, traction, traction_sems) = scratch[:4], scratch[4:]
+    return (
+        beside(flats[:4]),
+        jnp.where(lane < 64, beside(flats[4:]), ids),
+        dot_split(square(down[...]), top_high, top_low),
+    )
+
+
+def first_kernel(*refs):
+    sources, outs, scratch = refs[:12], refs[12:15], refs[15:]
+    held, (sems, traction, traction_sems, natural) = scratch[:11], scratch[11:15]
+    results, out_sems = scratch[15:18], scratch[18]
     leaves = sources[0].shape[0]
     pairs = leaves // 2
-    copies = fetch(sources[1:], held, sems)
     tractions = [
         pltpu.make_async_copy(sources[0].at[i], traction.at[i], traction_sems.at[i]) for i in range(leaves)
     ]
+    basis_copy, *copies = fetch(sources[1:], held, sems)
     for copy in tractions:
         copy.start()
-    basis, up_leaf, up_pair, up_device = held
+    basis, up_leaf, up_pair, up_device = held[:4]
+    weight_ref, stack_ref, send_ref = results
+    writes = [pltpu.make_async_copy(r, o, out_sems.at[n]) for n, (r, o) in enumerate(zip(results, outs))]
     for copy in copies:
         copy.wait()
+    for n, block in enumerate(weights_of(held[4:], natural)):
+        weight_ref[0, RANK * n : RANK * (n + 1), :] = block
+    writes[0].start()
+    basis_copy.wait()
     for i in range(leaves):
         tractions[i].wait()
         high, low = split(traction[i])
@@ -132,6 +138,7 @@
         stack_ref[at : at + RANK, :] = dot_first(
             jnp.concatenate(weight, axis=0), jnp.concatenate(value, axis=0)
         )
+    writes[1].start()
     weight = [square(up_pair[pl.ds(p, ROWS8, stride=pairs), :]) for p in range(pairs)]
     value = [quad_rows(stack_ref, RANK * (leaves + p)) for p in range(pairs)]
     coeff = dot_first(jnp.concatenate(weight, axis=0), jnp.concatenate(value, axis=0))
@@ -139,6 +146,9 @@
     for d in range(send_ref.shape[0]):
         send_ref[d, 0:RANK, :] = coeff
         send_ref[d, RANK : RANK + ROWS8, :] = up
+    writes[2].start()
+    for write in writes:
+        write.wait()
 
 
 def far_kernel(
@@ -280,27 +290,32 @@
         ]
         both = dot_split(jnp.concatenate(weight, axis=0), *rows)
         for m, (_, _, _, offset) in enumerate(two):
-            at = (row + 2 * rows_y - offset) % rows_y
+            at = (row + 2 * rows_y - offset * (1 - 2 * core)) % rows_y
             mine = both[RANK * m : RANK * (m + 1), COLS * m : COLS * (m + 1)]
             mine = mine + top_part[RANK * (t + m) : RANK * (t + m + 1)]
             out_ref[at] = mine if own else mine + before_ref[at]
 
 
-def last_kernel(parts_ref, fixed_ref, slope_ref, out_ref, natural):
+def last_kernel(parts_ref, fixed_ref, slope_ref, out_ref, natural, held, sems):
     total = parts_ref[0]
     for t in range(1, parts_ref.shape[0]):
         total = total + parts_ref[t]
     store_natural(natural, 0, total)
     high, low = split(natural[...])
     rows = jnp.concatenate([high, low, high, jnp.zeros((RANK, COLS), BF16)], axis=0)
-    for i in range(out_ref.shape[0]):
-        out_ref[i] = fixed_ref[i] + dot(slope_ref[i], rows)
-
-
-def whole(kernel, out, args, smem=(), hbm=(), scratch=(), flops=0, limit=VMEM_LIMIT):
+    writes = [pltpu.make_async_copy(held.at[i], out_ref.at[i], sems.at[i]) for i in range(held.shape[0])]
+    for i, write in enumerate(writes):
+        held[i] = fixed_ref[i] + dot(slope_ref[i], rows)
+        write.start()
+    for write in writes:
+        write.wait()
+
+
+def whole(kernel, out, args, smem=(), hbm=(), scratch=(), flops=0, limit=VMEM_LIMIT, out_hbm=False):
     vmem = pl.BlockSpec(memory_space=pltpu.VMEM)
     scalars = pl.BlockSpec(memory_space=pltpu.SMEM)
     far = pl.BlockSpec(memory_space=pltpu.HBM)
+    place = far if out_hbm else vmem
     size = sum(a.size * a.dtype.itemsize for a in args)
     outs = out if isinstance(out, tuple) else (out,)
     size += sum(o.size * o.dtype.itemsize for o in outs)
@@ -308,7 +323,7 @@
         kernel,
         out_shape=out,
         in_specs=[scalars if n in smem else far if n in hbm else vmem for n in range(len(args))],
-        out_specs=tuple(vmem for _ in out) if isinstance(out, tuple) else vmem,
+        out_specs=tuple(place for _ in out) if isinstance(out, tuple) else place,
         scratch_shapes=list(scratch),
         compiler_params=pltpu.CompilerParams(vmem_limit_bytes=limit),
         cost_estimate=pl.CostEstimate(flops=flops, bytes_accessed=size, transcendentals=0),
@@ -355,36 +370,34 @@
         return [pltpu.VMEM(a.shape, a.dtype) for a in args] + [pltpu.SemaphoreType.DMA((len(args),))]
 
     first = (
+        traction_vectors, row_basis, rows_of(up_leaf), rows_of(up_pair), rows_of(up_device),
         rows_of(couple_device), rows_of(down_device), rows_of(couple_top[0]),
         list_device, mask_device, list_top, mask_top,
     )
-    weights = whole(
-        weights_kernel,
-        shape(1, 3 * RANK, COLS),
+    results = (shape(1, 3 * RANK, COLS), shape(blocks * RANK, COLS), shape(subs, RANK + ROWS8, COLS))
+    weights, stack, send = whole(
+        first_kernel,
+        results,
         first,
         hbm=range(len(first)),
-        scratch=[*fetched(first), pltpu.VMEM((RANK, COLS), F32)],
-        flops=10**6,
-        limit=ALMOST_ALL,
-    )
-    weights, traction_vectors = lax.optimization_barrier((weights, traction_vectors))
-    second = (traction_vectors, row_basis, rows_of(up_leaf), rows_of(up_pair), rows_of(up_device))
-    stack, send = whole(
-        up_kernel,
-        (shape(blocks * RANK, COLS), shape(subs, RANK + ROWS8, COLS)),
-        second,
-        hbm=range(len(second)),
+        out_hbm=True,
         scratch=[
-            *fetched(second[1:]),
+            *fetched(first[1:]),
             pltpu.VMEM(traction_vectors.shape, F32),
             pltpu.SemaphoreType.DMA((leaves,)),
+            pltpu.VMEM((RANK, COLS), F32),
+            *fetched(results),
         ],
         flops=6 * 10**7,
         limit=ALMOST_ALL,
     )
 
     def over_y(block, step):
-        return lax.ppermute(block, "y", [(i, (i + step) % targets) for i in range(targets)])
+        moves = []
+        for y in range(targets):
+            moves.append((2 * y, 2 * ((y + step) % targets)))
+            moves.append((2 * y + 1, 2 * ((y - step) % targets) + 1))
+        return lax.ppermute(block, ("y", "core"), moves)
 
     weights = jnp.concatenate([weights, over_y(weights, targets // 2)], axis=0)
     coeffs = lax.all_to_all(send, ("x", "z"), 0, 0, tiled=True)
@@ -429,7 +442,12 @@
         last_kernel,
         shape(leaves, entries, COLS),
         (parts, fixed, slope),
-        scratch=[pltpu.VMEM((RANK, COLS), F32)],
+        out_hbm=True,
+        scratch=[
+            pltpu.VMEM((RANK, COLS), F32),
+            pltpu.VMEM((leaves, entries, COLS), F32),
+            pltpu.SemaphoreType.DMA((leaves,)),
+        ],
         flops=5 * 10**7,
     )
 

time: 68.9 us -> 67 us (0.972)
  Pallas kernels: 12.7 us -> 11.3 us
    pallas_call x6 -> x5, Pallas kernels: 12.7 us -> 11.3 us  [whole(): pl.pallas_call(kernel, out_shape=out, in_specs=[scalars if n in smem else...]
where the time goes in v7:
time: 67 us; the launch traced here: 66.5 us
  starting transfers between devices  42.1 us (63%)
  waiting for transfers between devices  12 us (18%)
  Pallas kernels  11.3 us (17%)
  local copies, waits for them, and re-layouts  0.69 us (1%)
    ppermute x4, starting transfers between devices, over_y(): return lax.ppermute(block, ('y', 'core'), moves)  16.3 us
    all_to_all x1, starting transfers between devices, body(): coeffs = lax.all_to_all(send, ('x', 'z'), 0, 0, tiled=True)  13.6 us
    pallas_call x5, Pallas kernels, whole(): pl.pallas_call(kernel, out_shape=out, in_specs=[scalars if n in smem else...  11.3 us
    all_to_all x1, waiting for transfers between devices, body(): parts = lax.all_to_all(parts, 'y', 0, 0, tiled=True)  6.44 us
    ppermute x4, waiting for transfers between devices, over_y(): return lax.ppermute(block, ('y', 'core'), moves)  5.12 us
    ppermute x1, starting transfers between devices, body(): high = lax.ppermute(stack, leaf_axes, [(i + 1, i) for i in range(subs - 1)])  4.87 us
    all_to_all x1, starting transfers between devices, body(): parts = lax.all_to_all(parts, 'y', 0, 0, tiled=True)  3.5 us
    ppermute x1, starting transfers between devices, body(): other = lax.ppermute(coeffs, 'core', [(0, 1), (1, 0)])  1.92 us
  transfers between devices with their start and end apart: 9, of which 4 were waited for; matrix products, arithmetic and copies ran while one was open for 0% of the time, Pallas kernels for 6%

profile of v7, /device:TPU:6, one launch (start us, length us, event | category | flops | bytes accessed | tf_op | source)
XLA Modules:
  0.0 66.5 jit_solution(4334701717934055041)
XLA Ops:
  0.0 4.1 %shard_map.199 = (f32[1,96,128]{2,1,0:T(8,128)}, f32[384,128]{1,0:T(8,128)}, f32[32,40,128]{2,1,0:T(8,128)}) custom-call(f32[8,192,128]{2,1,0:T(8,128)} %refs_0_.1, f32[8,32,192]{2,1,0:T(8,128)} %refs_1_.1, f32[64,128]{1,0:T(8,128)} %bitcast.53, f32[32,128]{1,0:T(8,128)} %bitcast.55, f32[8,128]{1,0:T(8,128)} %bitcast.57, f32[48,128]{1,0:T(8,128)} %bitcast.54, ...), custom_call_target="tpu_custom_call" | custom-call | flops 60000000 | bytes 1982544 | tf_op jit(solution)/shard_map/pallas_call | solution.py:322
  4.1 0.0 copy-start.10
  4.1 0.0 copy-start.2
  4.1 13.6 %all-to-all-start = ((f32[32,40,128]{2,1,0:T(8,128)}), f32[32,40,128]{2,1,0:T(8,128)S(1)}, u32[]{:S(2)}, u32[]{:S(2)}) async-start(f32[32,40,128]{2,1,0:T(8,128)} %get-tuple-element.19), calls=%async_computation | async-start | bytes 1310720 | tf_op jit(solution)/shard_map/all_to_all | solution.py:403
  17.7 0.0 copy-done.10
  17.7 7.7 %collective-permute-start.2 = (f32[1,96,128]{2,0,1:T(1,128)S(1)}, f32[1,96,128]{2,0,1:T(1,128)S(1)}, u32[]{:S(2)}, u32[]{:S(2)}) collective-permute-start(f32[1,96,128]{2,0,1:T(1,128)S(1)} %bitcast.51), channel_id=1, source_target_pairs={{0,256},{32,288},{64,320},{96,352},{128,384},{160,416},{192,448},{... | collective-permute-start | bytes 147464 | tf_op jit(solution)/shard_map/ppermute | solution.py:400
  25.5 0.0 copy-done.2
  25.5 4.9 %collective-permute-start.1 = (f32[384,128]{1,0:T(8,128)S(1)}, f32[384,128]{1,0:T(8,128)S(1)}, u32[]{:S(2)}, u32[]{:S(2)}) collective-permute-start(f32[384,128]{1,0:T(8,128)S(1)} %copy-done.2), channel_id=1, source_target_pairs={{1,0},{2,1},{3,2},{4,3},{5,4},{6,5},{7,6},{8,7},{9,8},{10,9},{11,1... | collective-permute-start | bytes 589832 | tf_op jit(solution)/shard_map/ppermute | solution.py:407
  30.4 1.9 %collective-permute-start = (f32[384,128]{1,0:T(8,128)S(1)}, f32[384,128]{1,0:T(8,128)S(1)}, u32[]{:S(2)}, u32[]{:S(2)}) collective-permute-start(f32[384,128]{1,0:T(8,128)S(1)} %copy-done.2), channel_id=1, source_target_pairs={{0,1},{1,2},{2,3},{3,4},{4,5},{5,6},{6,7},{7,8},{8,9},{9,10},{10,1... | collective-permute-start | bytes 589832 | tf_op jit(solution)/shard_map/ppermute | solution.py:406
  32.3 0.0 collective-permute-done.2
  32.3 0.1 pad_maximum_fusion
  32.4 2.4 %collective-permute-start.5 = (f32[2,96,128]{2,0,1:T(2,128)S(1)}, f32[2,96,128]{2,0,1:T(2,128)S(1)}, u32[]{:S(2)}, u32[]{:S(2)}) collective-permute-start(f32[2,96,128]{2,0,1:T(2,128)S(1)} %pad_maximum_fusion), channel_id=1, source_target_pairs={{0,448},{32,96},{64,0},{96,160},{128,64},{160,224},{192,128},{224,... | collective-permute-start | bytes 294920 | tf_op jit(solution)/shard_map/ppermute | solution.py:400
  34.8 3.6 %collective-permute-start.4 = (f32[2,96,128]{2,0,1:T(2,128)S(1)}, f32[2,96,128]{2,0,1:T(2,128)S(1)}, u32[]{:S(2)}, u32[]{:S(2)}) collective-permute-start(f32[2,96,128]{2,0,1:T(2,128)S(1)} %pad_maximum_fusion), channel_id=1, source_target_pairs={{0,128},{32,416},{64,192},{96,480},{128,256},{160,32},{192,320},{2... | collective-permute-start | bytes 294920 | tf_op jit(solution)/shard_map/ppermute | solution.py:400
  38.4 2.6 %collective-permute-start.3 = (f32[2,96,128]{2,0,1:T(2,128)S(1)}, f32[2,96,128]{2,0,1:T(2,128)S(1)}, u32[]{:S(2)}, u32[]{:S(2)}) collective-permute-start(f32[2,96,128]{2,0,1:T(2,128)S(1)} %pad_maximum_fusion), channel_id=1, source_target_pairs={{0,64},{32,480},{64,128},{96,32},{128,192},{160,96},{192,256},{224... | collective-permute-start | bytes 294920 | tf_op jit(solution)/shard_map/ppermute | solution.py:400
  41.0 0.0 collective-permute-done.5
  41.0 3.0 %collective-permute-done.4 = f32[2,96,128]{2,0,1:T(2,128)S(1)} collective-permute-done((f32[2,96,128]{2,0,1:T(2,128)S(1)}, f32[2,96,128]{2,0,1:T(2,128)S(1)}, u32[]{:S(2)}, u32[]{:S(2)}) %collective-permute-start.4) | collective-permute-done | bytes 98336 | tf_op jit(solution)/shard_map/ppermute | solution.py:400
  44.0 2.1 %collective-permute-done.3 = f32[2,96,128]{2,0,1:T(2,128)S(1)} collective-permute-done((f32[2,96,128]{2,0,1:T(2,128)S(1)}, f32[2,96,128]{2,0,1:T(2,128)S(1)}, u32[]{:S(2)}, u32[]{:S(2)}) %collective-permute-start.3) | collective-permute-done | bytes 98336 | tf_op jit(solution)/shard_map/ppermute | solution.py:400
  46.1 0.0 collective-permute-done.1.high_ref
  46.1 0.0 collective-permute-done.low_ref
  46.1 0.0 all-to-all-done.refs_0_
  46.1 1.9 %collective-permute-start.6 = (f32[32,40,128]{2,1,0:T(8,128)S(1)}, f32[32,40,128]{2,1,0:T(8,128)S(1)}, u32[]{:S(2)}, u32[]{:S(2)}) collective-permute-start(f32[32,40,128]{2,1,0:T(8,128)S(1)} %all-to-all-done.refs_0_), channel_id=1, source_target_pairs={{0,32},{32,0},{1,33},{33,1},{2,34},{34,2},{3,35},{35,3},{4,36},{36... | collective-permute-start | bytes 1966088 | tf_op jit(solution)/shard_map/ppermute | solution.py:409
  48.1 1.5 %shard_map.200.refs_9_ = f32[8,32,128]{2,1,0:T(8,128)S(1)} custom-call(f32[32,40,128]{2,1,0:T(8,128)S(1)} %all-to-all-done.refs_0_, f32[2,96,128]{2,1,0:T(8,128)S(1)} %copy.30.refs_1_, f32[2,96,128]{2,1,0:T(8,128)S(1)} %copy.31.refs_2_, f32[2,96,128]{2,1,0:T(8,128)S(1)} %copy.32.refs_3_, f32[2,96,128]{2,1,0:T(8,128)S(1)} %copy.33.refs_4_, ...), custom_call_target="tpu_custom_call" | custom-call | flops 50000000 | bytes 1183744 | tf_op jit(solution)/shard_map/pallas_call | solution.py:322
  49.6 0.5 collective-permute-done.6.refs_0_
  50.1 0.0 copy-start.1
  50.1 0.0 copy-start.3
  50.1 0.0 copy-start.4
  50.1 0.0 copy-start.5
  50.1 0.0 copy-start.7
  50.1 0.0 copy-start.9
  50.1 2.2 %shard_map.201 = f32[8,32,128]{2,1,0:T(8,128)} custom-call(f32[32,40,128]{2,1,0:T(8,128)S(1)} %collective-permute-done.6.refs_0_, f32[2,96,128]{2,1,0:T(8,128)S(1)} %copy.30.refs_1_, f32[2,96,128]{2,1,0:T(8,128)S(1)} %copy.31.refs_2_, f32[2,96,128]{2,1,0:T(8,128)S(1)} %copy.32.refs_3_, f32[2,96,128]{2,1,0:T(8,128)S(1)} %copy.33.refs_4_, ...), custom_call_target="tpu_custom_call" | custom-call | flops 50000000 | bytes 1314816 | tf_op jit(solution)/shard_map/pallas_call | solution.py:322
  52.3 0.0 copy-start
  52.3 3.5 %all-to-all-start.1 = ((f32[8,32,128]{2,1,0:T(8,128)}), f32[8,32,128]{2,1,0:T(8,128)S(1)}, u32[]{:S(2)}, u32[]{:S(2)}) async-start(f32[8,32,128]{2,1,0:T(8,128)} %shard_map.201), calls=%async_computation.1 | async-start | bytes 262144 | tf_op jit(solution)/shard_map/all_to_all | solution.py:427
  55.8 0.0 copy-start.6
  55.8 0.0 copy-start.8
  55.9 0.0 copy-done.1
  55.9 0.0 copy-done.3
  55.9 0.0 copy-done.4
  55.9 0.0 copy-done.5
  55.9 0.0 copy-done.7
  55.9 0.0 copy-done.9
  55.9 0.0 copy-done
  55.9 0.6 copy-done.6
  56.5 0.0 copy-done.8
  56.5 2.4 %shard_map.202 = (f32[8,192,128]{2,1,0:T(8,128)S(1)}, bf16[8,192,128]{2,1,0:T(8,128)(2,1)S(1)}) custom-call(f32[384,128]{1,0:T(8,128)S(1)} %collective-permute-done.low_ref, f32[384,128]{1,0:T(8,128)S(1)} %copy-done.2, f32[384,128]{1,0:T(8,128)S(1)} %collective-permute-done.1.high_ref, f32[384,128]{1,0:T(8,128)S(1)} %bitcast.47, f32[192,128]{1,0:T(8,128)S(1)} %bitcast.48, ...), custom_call_target="tpu_custom_call" | custom-call | flops 100000000 | bytes 2310720 | tf_op jit(solution)/shard_map/pallas_call | solution.py:322
  58.9 6.4 %all-to-all-done.1.parts_ref = f32[8,32,128]{2,1,0:T(8,128)S(1)} async-done(((f32[8,32,128]{2,1,0:T(8,128)}), f32[8,32,128]{2,1,0:T(8,128)S(1)}, u32[]{:S(2)}, u32[]{:S(2)}) %all-to-all-start.1) | async-done | bytes 131104 | tf_op jit(solution)/shard_map/all_to_all | solution.py:427
  65.4 1.1 %shard_map.203 = f32[8,192,128]{2,1,0:T(8,128)} custom-call(f32[8,32,128]{2,1,0:T(8,128)S(1)} %all-to-all-done.1.parts_ref, f32[8,192,128]{2,1,0:T(8,128)S(1)} %get-tuple-element.31.fixed_ref, bf16[8,192,128]{2,1,0:T(8,128)(2,1)S(1)} %get-tuple-element.32.slope_ref), custom_call_target="tpu_custom_call" | custom-call | flops 50000000 | bytes 2097152 | tf_op jit(solution)/shard_map/pallas_call | solution.py:322
  (6 shorter events, 0.0 us)
Async XLA Ops:
  4.1 13.6 %copy-start.10 = (f32[1,96,128]{2,1,0:T(8,128)S(1)}, f32[1,96,128]{2,1,0:T(8,128)}, u32[]{:S(2)}) copy-start(f32[1,96,128]{2,1,0:T(8,128)} %get-tuple-element.21) | copy-start | bytes 147460
  4.1 21.4 %copy-start.2 = (f32[384,128]{1,0:T(8,128)S(1)}, f32[384,128]{1,0:T(8,128)}, u32[]{:S(2)}) copy-start(f32[384,128]{1,0:T(8,128)} %get-tuple-element.20.own_ref) | copy-start | bytes 589828
  4.1 42.0 %all-to-all-start = ((f32[32,40,128]{2,1,0:T(8,128)}), f32[32,40,128]{2,1,0:T(8,128)S(1)}, u32[]{:S(2)}, u32[]{:S(2)}) async-start(f32[32,40,128]{2,1,0:T(8,128)} %get-tuple-element.19), calls=%async_computation | async-start | bytes 1310720 | tf_op jit(solution)/shard_map/all_to_all | solution.py:403
  17.7 14.6 %collective-permute-start.2 = (f32[1,96,128]{2,0,1:T(1,128)S(1)}, f32[1,96,128]{2,0,1:T(1,128)S(1)}, u32[]{:S(2)}, u32[]{:S(2)}) collective-permute-start(f32[1,96,128]{2,0,1:T(1,128)S(1)} %bitcast.51), channel_id=1, source_target_pairs={{0,256},{32,288},{64,320},{96,352},{128,384},{160,416},{192,448},{... | collective-permute-start | bytes 147464 | tf_op jit(solution)/shard_map/ppermute | solution.py:400
  25.5 20.6 %collective-permute-start.1 = (f32[384,128]{1,0:T(8,128)S(1)}, f32[384,128]{1,0:T(8,128)S(1)}, u32[]{:S(2)}, u32[]{:S(2)}) collective-permute-start(f32[384,128]{1,0:T(8,128)S(1)} %copy-done.2), channel_id=1, source_target_pairs={{1,0},{2,1},{3,2},{4,3},{5,4},{6,5},{7,6},{8,7},{9,8},{10,9},{11,1... | collective-permute-start | bytes 589832 | tf_op jit(solution)/shard_map/ppermute | solution.py:407
  30.4 15.7 %collective-permute-start = (f32[384,128]{1,0:T(8,128)S(1)}, f32[384,128]{1,0:T(8,128)S(1)}, u32[]{:S(2)}, u32[]{:S(2)}) collective-permute-start(f32[384,128]{1,0:T(8,128)S(1)} %copy-done.2), channel_id=1, source_target_pairs={{0,1},{1,2},{2,3},{3,4},{4,5},{5,6},{6,7},{7,8},{8,9},{9,10},{10,1... | collective-permute-start | bytes 589832 | tf_op jit(solution)/shard_map/ppermute | solution.py:406
  32.4 8.6 %collective-permute-start.5 = (f32[2,96,128]{2,0,1:T(2,128)S(1)}, f32[2,96,128]{2,0,1:T(2,128)S(1)}, u32[]{:S(2)}, u32[]{:S(2)}) collective-permute-start(f32[2,96,128]{2,0,1:T(2,128)S(1)} %pad_maximum_fusion), channel_id=1, source_target_pairs={{0,448},{32,96},{64,0},{96,160},{128,64},{160,224},{192,128},{224,... | collective-permute-start | bytes 294920 | tf_op jit(solution)/shard_map/ppermute | solution.py:400
  34.8 9.2 %collective-permute-start.4 = (f32[2,96,128]{2,0,1:T(2,128)S(1)}, f32[2,96,128]{2,0,1:T(2,128)S(1)}, u32[]{:S(2)}, u32[]{:S(2)}) collective-permute-start(f32[2,96,128]{2,0,1:T(2,128)S(1)} %pad_maximum_fusion), channel_id=1, source_target_pairs={{0,128},{32,416},{64,192},{96,480},{128,256},{160,32},{192,320},{2... | collective-permute-start | bytes 294920 | tf_op jit(solution)/shard_map/ppermute | solution.py:400
  38.4 7.7 %collective-permute-start.3 = (f32[2,96,128]{2,0,1:T(2,128)S(1)}, f32[2,96,128]{2,0,1:T(2,128)S(1)}, u32[]{:S(2)}, u32[]{:S(2)}) collective-permute-start(f32[2,96,128]{2,0,1:T(2,128)S(1)} %pad_maximum_fusion), channel_id=1, source_target_pairs={{0,64},{32,480},{64,128},{96,32},{128,192},{160,96},{192,256},{224... | collective-permute-start | bytes 294920 | tf_op jit(solution)/shard_map/ppermute | solution.py:400
  46.1 4.0 %collective-permute-start.6 = (f32[32,40,128]{2,1,0:T(8,128)S(1)}, f32[32,40,128]{2,1,0:T(8,128)S(1)}, u32[]{:S(2)}, u32[]{:S(2)}) collective-permute-start(f32[32,40,128]{2,1,0:T(8,128)S(1)} %all-to-all-done.refs_0_), channel_id=1, source_target_pairs={{0,32},{32,0},{1,33},{33,1},{2,34},{34,2},{3,35},{35,3},{4,36},{36... | collective-permute-start | bytes 1966088 | tf_op jit(solution)/shard_map/ppermute | solution.py:409
  50.1 5.7 %copy-start.1 = (f32[8,6,1024]{2,0,1:T(8,128)S(1)}, f32[8,6,1024]{2,0,1:T(8,128)}, u32[]{:S(2)}) copy-start(f32[8,6,1024]{2,0,1:T(8,128)} %param.26) | copy-start | bytes 589828
  50.1 5.8 %copy-start.3 = (f32[4,6,1024]{2,0,1:T(4,128)S(1)}, f32[4,6,1024]{2,0,1:T(4,128)}, u32[]{:S(2)}) copy-start(f32[4,6,1024]{2,0,1:T(4,128)} %param.27) | copy-start | bytes 294916
  50.1 5.8 %copy-start.4 = (f32[8,1024]{1,0:T(8,128)S(1)}, f32[8,1024]{1,0:T(8,128)}, u32[]{:S(2)}) copy-start(f32[8,1024]{1,0:T(8,128)} %param.38) | copy-start | bytes 98308
  50.1 5.8 %copy-start.5 = (f32[4,1024]{1,0:T(4,128)S(1)}, f32[4,1024]{1,0:T(4,128)}, u32[]{:S(2)}) copy-start(f32[4,1024]{1,0:T(4,128)} %param.39) | copy-start | bytes 49156
  50.1 5.8 %copy-start.7 = (s32[8,6]{1,0:T(8,128)S(1)}, s32[8,6]{1,0:T(8,128)}, u32[]{:S(2)}) copy-start(s32[8,6]{1,0:T(8,128)} %mask_leaf.1) | copy-start | bytes 580
  50.1 5.8 %copy-start.9 = (s32[4,6]{1,0:T(4,128)S(1)}, s32[4,6]{1,0:T(4,128)}, u32[]{:S(2)}) copy-start(s32[4,6]{1,0:T(4,128)} %mask_pair.1) | copy-start | bytes 292
  52.3 3.6 %copy-start = (f32[8,32,192]{2,1,0:T(8,128)S(1)}, f32[8,32,192]{2,1,0:T(8,128)}, u32[]{:S(2)}) copy-start(f32[8,32,192]{2,1,0:T(8,128)} %basis.1) | copy-start | bytes 589828
  52.3 13.1 %all-to-all-start.1 = ((f32[8,32,128]{2,1,0:T(8,128)}), f32[8,32,128]{2,1,0:T(8,128)S(1)}, u32[]{:S(2)}, u32[]{:S(2)}) async-start(f32[8,32,128]{2,1,0:T(8,128)} %shard_map.201), calls=%async_computation.1 | async-start | bytes 262144 | tf_op jit(solution)/shard_map/all_to_all | solution.py:427
  55.8 0.7 %copy-start.6 = (s32[8,6]{1,0:T(8,128)S(1)}, s32[8,6]{1,0:T(8,128)}, u32[]{:S(2)}) copy-start(s32[8,6]{1,0:T(8,128)} %list_leaf.1) | copy-start | bytes 580
  55.8 0.7 %copy-start.8 = (s32[4,6]{1,0:T(4,128)S(1)}, s32[4,6]{1,0:T(4,128)}, u32[]{:S(2)}) copy-start(s32[4,6]{1,0:T(4,128)} %list_pair.1) | copy-start | bytes 292

commit v8 on v7

--- a/solution.py
+++ b/solution.py
@@ -405,7 +405,20 @@
     leaf_axes = ("x", "z")
     low = lax.ppermute(stack, leaf_axes, [(i, i + 1) for i in range(subs - 1)])
     high = lax.ppermute(stack, leaf_axes, [(i + 1, i) for i in range(subs - 1)])
-    coeffs, low, high, weights = lax.optimization_barrier((coeffs, low, high, weights))
+    near = pltpu.VMEM(((3 * blocks + 1) * RANK, COLS), BF16)
+    fixed, slope = whole(
+        far_kernel,
+        (shape(leaves, entries, COLS), shape(leaves, entries, COLS, dtype=BF16)),
+        (
+            low, stack, high, rows_of(couple_leaf), rows_of(pair_coupling_blocks),
+            rows_of(down_leaf), rows_of(down_pair), col_basis,
+            list_leaf, mask_leaf, list_pair, mask_pair,
+        ),
+        smem=(8, 9, 10, 11),
+        scratch=[near, near, pltpu.VMEM((2 * RANK * blocks, COLS), F32)],
+        flops=10**8,
+    )
+    coeffs, weights, fixed, slope = lax.optimization_barrier((coeffs, weights, fixed, slope))
     other = lax.ppermute(coeffs, "core", [(0, 1), (1, 0)])
     weights = [*weights, *(block[:, RANK, :] for block in weights)]
     count = len(weights) // 2
@@ -423,21 +436,7 @@
             ],
             flops=5 * 10**7,
         )
-    parts, low = lax.optimization_barrier((parts, low))
     parts = lax.all_to_all(parts, "y", 0, 0, tiled=True)
-    near = pltpu.VMEM(((3 * blocks + 1) * RANK, COLS), BF16)
-    fixed, slope = whole(
-        far_kernel,
-        (shape(leaves, entries, COLS), shape(leaves, entries, COLS, dtype=BF16)),
-        (
-            low, stack, high, rows_of(couple_leaf), rows_of(pair_coupling_blocks),
-            rows_of(down_leaf), rows_of(down_pair), col_basis,
-            list_leaf, mask_leaf, list_pair, mask_pair,
-        ),
-        smem=(8, 9, 10, 11),
-        scratch=[near, near, pltpu.VMEM((2 * RANK * blocks, COLS), F32)],
-        flops=10**8,
-    )
     return whole(
         last_kernel,
         shape(leaves, entries, COLS),

time: 67 us -> 65.8 us (0.982)
  blocking collectives: 0 us -> 12.4 us
  waiting for transfers between devices: 12 us -> 2.49 us
  starting transfers between devices: 42.1 us -> 38.7 us
  Pallas kernels: 11.3 us -> 10.6 us
    all_to_all x0 -> x1, blocking collectives: none -> 12.4 us  [body(): parts = lax.all_to_all(parts, 'y', 0, 0, tiled=True)]
    all_to_all x1 -> x0, waiting for transfers between devices: 6.44 us -> none  [body(): parts = lax.all_to_all(parts, 'y', 0, 0, tiled=True)]
    all_to_all x1 -> x0, starting transfers between devices: 3.5 us -> none  [body(): parts = lax.all_to_all(parts, 'y', 0, 0, tiled=True)]
    ppermute x4, waiting for transfers between devices: 5.12 us -> 2.01 us  [over_y(): return lax.ppermute(block, ('y', 'core'), moves)]
    pallas_call x5, Pallas kernels: 11.3 us -> 10.6 us  [whole(): pl.pallas_call(kernel, out_shape=out, in_specs=[scalars if n in smem else...]
  transfers between devices with their start and end apart: 9 -> 8, of which waited for: 4 -> 2; matrix products, arithmetic and copies ran while one was open for 0% -> 0% of each run, Pallas kernels for 6% -> 6%
where the time goes in v8:
time: 65.8 us; the launch traced here: 65.3 us
  starting transfers between devices  38.7 us (59%)
  blocking collectives  12.4 us (19%)
  Pallas kernels  10.6 us (16%)
  waiting for transfers between devices  2.49 us (4%)
  local copies, waits for them, and re-layouts  0.7 us (1%)
    ppermute x4, starting transfers between devices, over_y(): return lax.ppermute(block, ('y', 'core'), moves)  16.4 us
    all_to_all x1, starting transfers between devices, body(): coeffs = lax.all_to_all(send, ('x', 'z'), 0, 0, tiled=True)  13.6 us
    all_to_all x1, blocking collectives, body(): parts = lax.all_to_all(parts, 'y', 0, 0, tiled=True)  12.4 us
    pallas_call x5, Pallas kernels, whole(): pl.pallas_call(kernel, out_shape=out, in_specs=[scalars if n in smem else...  10.6 us
    ppermute x1, starting transfers between devices, body(): high = lax.ppermute(stack, leaf_axes, [(i + 1, i) for i in range(subs - 1)])  4.87 us
    ppermute x4, waiting for transfers between devices, over_y(): return lax.ppermute(block, ('y', 'core'), moves)  2.01 us
    ppermute x1, starting transfers between devices, body(): low = lax.ppermute(stack, leaf_axes, [(i, i + 1) for i in range(subs - 1)])  1.92 us
    ppermute x1, starting transfers between devices, body(): other = lax.ppermute(coeffs, 'core', [(0, 1), (1, 0)])  1.91 us
  transfers between devices with their start and end apart: 8, of which 2 were waited for; matrix products, arithmetic and copies ran while one was open for 0% of the time, Pallas kernels for 6%

profile of v8, /device:TPU:6, one launch (start us, length us, event | category | flops | bytes accessed | tf_op | source)
XLA Modules:
  0.0 65.3 jit_solution(6054473713084750718)
XLA Ops:
  0.0 4.1 %shard_map.199 = (f32[1,96,128]{2,1,0:T(8,128)}, f32[384,128]{1,0:T(8,128)}, f32[32,40,128]{2,1,0:T(8,128)}) custom-call(f32[8,192,128]{2,1,0:T(8,128)} %refs_0_.1, f32[8,32,192]{2,1,0:T(8,128)} %refs_1_.1, f32[64,128]{1,0:T(8,128)} %bitcast.53, f32[32,128]{1,0:T(8,128)} %bitcast.55, f32[8,128]{1,0:T(8,128)} %bitcast.57, f32[48,128]{1,0:T(8,128)} %bitcast.54, ...), custom_call_target="tpu_custom_call" | custom-call | flops 60000000 | bytes 1982544 | tf_op jit(solution)/shard_map/pallas_call | solution.py:322
  4.1 0.0 copy-start.10
  4.1 0.0 copy-start.2
  4.1 0.0 copy-start
  4.1 0.0 copy-start.3
  4.2 0.0 copy-start.4
  4.2 0.0 copy-start.5
  4.2 13.6 %all-to-all-start = ((f32[32,40,128]{2,1,0:T(8,128)}), f32[32,40,128]{2,1,0:T(8,128)S(1)}, u32[]{:S(2)}, u32[]{:S(2)}) async-start(f32[32,40,128]{2,1,0:T(8,128)} %get-tuple-element.17), calls=%async_computation | async-start | bytes 1310720 | tf_op jit(solution)/shard_map/all_to_all | solution.py:403
  17.8 0.0 copy-start.1
  17.8 0.0 copy-done.10
  17.8 7.9 %collective-permute-start = (f32[1,96,128]{2,0,1:T(1,128)S(1)}, f32[1,96,128]{2,0,1:T(1,128)S(1)}, u32[]{:S(2)}, u32[]{:S(2)}) collective-permute-start(f32[1,96,128]{2,0,1:T(1,128)S(1)} %bitcast.51), channel_id=1, source_target_pairs={{0,256},{32,288},{64,320},{96,352},{128,384},{160,416},{192,448},{... | collective-permute-start | bytes 147464 | tf_op jit(solution)/shard_map/ppermute | solution.py:400
  25.7 0.0 copy-done.2
  25.7 4.9 %collective-permute-start.5 = (f32[384,128]{1,0:T(8,128)S(1)}, f32[384,128]{1,0:T(8,128)S(1)}, u32[]{:S(2)}, u32[]{:S(2)}) collective-permute-start(f32[384,128]{1,0:T(8,128)S(1)} %copy-done.2), channel_id=1, source_target_pairs={{1,0},{2,1},{3,2},{4,3},{5,4},{6,5},{7,6},{8,7},{9,8},{10,9},{11,1... | collective-permute-start | bytes 589832 | tf_op jit(solution)/shard_map/ppermute | solution.py:407
  30.6 1.9 %collective-permute-start.4 = (f32[384,128]{1,0:T(8,128)S(1)}, f32[384,128]{1,0:T(8,128)S(1)}, u32[]{:S(2)}, u32[]{:S(2)}) collective-permute-start(f32[384,128]{1,0:T(8,128)S(1)} %copy-done.2), channel_id=1, source_target_pairs={{0,1},{1,2},{2,3},{3,4},{4,5},{5,6},{6,7},{7,8},{8,9},{9,10},{10,1... | collective-permute-start | bytes 589832 | tf_op jit(solution)/shard_map/ppermute | solution.py:406
  32.5 0.0 collective-permute-done
  32.5 0.0 copy-start.7
  32.5 0.0 copy-start.9
  32.5 0.1 pad_maximum_fusion
  32.6 0.0 copy-start.6
  32.6 2.4 %collective-permute-start.3 = (f32[2,96,128]{2,0,1:T(2,128)S(1)}, f32[2,96,128]{2,0,1:T(2,128)S(1)}, u32[]{:S(2)}, u32[]{:S(2)}) collective-permute-start(f32[2,96,128]{2,0,1:T(2,128)S(1)} %pad_maximum_fusion), channel_id=1, source_target_pairs={{0,448},{32,96},{64,0},{96,160},{128,64},{160,224},{192,128},{224,... | collective-permute-start | bytes 294920 | tf_op jit(solution)/shard_map/ppermute | solution.py:400
  35.0 3.6 %collective-permute-start.2 = (f32[2,96,128]{2,0,1:T(2,128)S(1)}, f32[2,96,128]{2,0,1:T(2,128)S(1)}, u32[]{:S(2)}, u32[]{:S(2)}) collective-permute-start(f32[2,96,128]{2,0,1:T(2,128)S(1)} %pad_maximum_fusion), channel_id=1, source_target_pairs={{0,128},{32,416},{64,192},{96,480},{128,256},{160,32},{192,320},{2... | collective-permute-start | bytes 294920 | tf_op jit(solution)/shard_map/ppermute | solution.py:400
  38.6 2.6 %collective-permute-start.1 = (f32[2,96,128]{2,0,1:T(2,128)S(1)}, f32[2,96,128]{2,0,1:T(2,128)S(1)}, u32[]{:S(2)}, u32[]{:S(2)}) collective-permute-start(f32[2,96,128]{2,0,1:T(2,128)S(1)} %pad_maximum_fusion), channel_id=1, source_target_pairs={{0,64},{32,480},{64,128},{96,32},{128,192},{160,96},{192,256},{224... | collective-permute-start | bytes 294920 | tf_op jit(solution)/shard_map/ppermute | solution.py:400
  41.2 0.0 collective-permute-done.5.high_ref
  41.2 0.0 collective-permute-done.4.low_ref
  41.2 0.0 copy-start.8
  41.2 0.0 copy-done
  41.3 0.0 copy-done.3
  41.3 0.0 copy-done.4
  41.3 0.0 copy-done.5
  41.3 0.0 copy-done.1
  41.3 0.0 copy-done.7
  41.3 0.0 copy-done.9
  41.3 0.0 copy-done.6
  41.3 0.6 copy-done.8
  41.9 2.4 %shard_map.200 = (f32[8,192,128]{2,1,0:T(8,128)S(1)}, bf16[8,192,128]{2,1,0:T(8,128)(2,1)S(1)}) custom-call(f32[384,128]{1,0:T(8,128)S(1)} %collective-permute-done.4.low_ref, f32[384,128]{1,0:T(8,128)S(1)} %copy-done.2, f32[384,128]{1,0:T(8,128)S(1)} %collective-permute-done.5.high_ref, f32[384,128]{1,0:T(8,128)S(1)} %bitcast.47, f32[192,128]{1,0:T(8,128)S(1)} %bitcast.48, ...), custom_call_target="tpu_custom_call" | custom-call | flops 100000000 | bytes 2310720 | tf_op jit(solution)/shard_map/pallas_call | solution.py:322
  44.3 0.0 collective-permute-done.3
  44.3 0.0 collective-permute-done.2
  44.3 2.0 %collective-permute-done.1 = f32[2,96,128]{2,0,1:T(2,128)S(1)} collective-permute-done((f32[2,96,128]{2,0,1:T(2,128)S(1)}, f32[2,96,128]{2,0,1:T(2,128)S(1)}, u32[]{:S(2)}, u32[]{:S(2)}) %collective-permute-start.1) | collective-permute-done | bytes 98336 | tf_op jit(solution)/shard_map/ppermute | solution.py:400
  46.3 0.0 all-to-all-done.refs_0_
  46.3 1.9 %collective-permute-start.6 = (f32[32,40,128]{2,1,0:T(8,128)S(1)}, f32[32,40,128]{2,1,0:T(8,128)S(1)}, u32[]{:S(2)}, u32[]{:S(2)}) collective-permute-start(f32[32,40,128]{2,1,0:T(8,128)S(1)} %all-to-all-done.refs_0_), channel_id=1, source_target_pairs={{0,32},{32,0},{1,33},{33,1},{2,34},{34,2},{3,35},{35,3},{4,36},{36... | collective-permute-start | bytes 1966088 | tf_op jit(solution)/shard_map/ppermute | solution.py:422
  48.3 1.5 %shard_map.201.refs_9_ = f32[8,32,128]{2,1,0:T(8,128)S(1)} custom-call(f32[32,40,128]{2,1,0:T(8,128)S(1)} %all-to-all-done.refs_0_, f32[2,96,128]{2,1,0:T(8,128)S(1)} %copy.32.refs_1_, f32[2,96,128]{2,1,0:T(8,128)S(1)} %copy.33.refs_2_, f32[2,96,128]{2,1,0:T(8,128)S(1)} %copy.34.refs_3_, f32[2,96,128]{2,1,0:T(8,128)S(1)} %copy.35.refs_4_, ...), custom_call_target="tpu_custom_call" | custom-call | flops 50000000 | bytes 1183744 | tf_op jit(solution)/shard_map/pallas_call | solution.py:322
  49.9 0.5 collective-permute-done.6.refs_0_
  50.3 1.5 %shard_map.202 = f32[8,32,128]{2,1,0:T(8,128)S(1)} custom-call(f32[32,40,128]{2,1,0:T(8,128)S(1)} %collective-permute-done.6.refs_0_, f32[2,96,128]{2,1,0:T(8,128)S(1)} %copy.32.refs_1_, f32[2,96,128]{2,1,0:T(8,128)S(1)} %copy.33.refs_2_, f32[2,96,128]{2,1,0:T(8,128)S(1)} %copy.34.refs_3_, f32[2,96,128]{2,1,0:T(8,128)S(1)} %copy.35.refs_4_, ...), custom_call_target="tpu_custom_call" | custom-call | flops 50000000 | bytes 1314816 | tf_op jit(solution)/shard_map/pallas_call | solution.py:322
  51.8 12.4 %all_to_all.10.parts_ref = f32[8,32,128]{2,1,0:T(8,128)S(1)} all-to-all(f32[8,32,128]{2,1,0:T(8,128)S(1)} %shard_map.202), channel_id=1, replica_groups=mesh['y'=8,'core'=2,'x'=4,'z'=8] {'y'}, dimensions={0} | all-to-all | bytes 262144 | tf_op jit(solution)/shard_map/all_to_all | solution.py:439
  64.2 1.1 %shard_map.203 = f32[8,192,128]{2,1,0:T(8,128)} custom-call(f32[8,32,128]{2,1,0:T(8,128)S(1)} %all_to_all.10.parts_ref, f32[8,192,128]{2,1,0:T(8,128)S(1)} %get-tuple-element.27.fixed_ref, bf16[8,192,128]{2,1,0:T(8,128)(2,1)S(1)} %get-tuple-element.28.slope_ref), custom_call_target="tpu_custom_call" | custom-call | flops 50000000 | bytes 2097152 | tf_op jit(solution)/shard_map/pallas_call | solution.py:322
  (6 shorter events, 0.0 us)
Async XLA Ops:
  4.1 13.7 %copy-start.10 = (f32[1,96,128]{2,1,0:T(8,128)S(1)}, f32[1,96,128]{2,1,0:T(8,128)}, u32[]{:S(2)}) copy-start(f32[1,96,128]{2,1,0:T(8,128)} %get-tuple-element.18) | copy-start | bytes 147460
  4.1 21.6 %copy-start.2 = (f32[384,128]{1,0:T(8,128)S(1)}, f32[384,128]{1,0:T(8,128)}, u32[]{:S(2)}) copy-start(f32[384,128]{1,0:T(8,128)} %get-tuple-element.19.own_ref) | copy-start | bytes 589828
  4.1 37.1 %copy-start = (f32[8,32,192]{2,1,0:T(8,128)S(1)}, f32[8,32,192]{2,1,0:T(8,128)}, u32[]{:S(2)}) copy-start(f32[8,32,192]{2,1,0:T(8,128)} %basis.1) | copy-start | bytes 589828
  4.1 37.1 %copy-start.3 = (f32[4,6,1024]{2,0,1:T(4,128)S(1)}, f32[4,6,1024]{2,0,1:T(4,128)}, u32[]{:S(2)}) copy-start(f32[4,6,1024]{2,0,1:T(4,128)} %param.27) | copy-start | bytes 294916
  4.2 37.1 %copy-start.4 = (f32[8,1024]{1,0:T(8,128)S(1)}, f32[8,1024]{1,0:T(8,128)}, u32[]{:S(2)}) copy-start(f32[8,1024]{1,0:T(8,128)} %param.38) | copy-start | bytes 98308
  4.2 37.1 %copy-start.5 = (f32[4,1024]{1,0:T(4,128)S(1)}, f32[4,1024]{1,0:T(4,128)}, u32[]{:S(2)}) copy-start(f32[4,1024]{1,0:T(4,128)} %param.39) | copy-start | bytes 49156
  4.2 42.2 %all-to-all-start = ((f32[32,40,128]{2,1,0:T(8,128)}), f32[32,40,128]{2,1,0:T(8,128)S(1)}, u32[]{:S(2)}, u32[]{:S(2)}) async-start(f32[32,40,128]{2,1,0:T(8,128)} %get-tuple-element.17), calls=%async_computation | async-start | bytes 1310720 | tf_op jit(solution)/shard_map/all_to_all | solution.py:403
  17.8 23.5 %copy-start.1 = (f32[8,6,1024]{2,0,1:T(8,128)S(1)}, f32[8,6,1024]{2,0,1:T(8,128)}, u32[]{:S(2)}) copy-start(f32[8,6,1024]{2,0,1:T(8,128)} %param.26) | copy-start | bytes 589828
  17.8 14.7 %collective-permute-start = (f32[1,96,128]{2,0,1:T(1,128)S(1)}, f32[1,96,128]{2,0,1:T(1,128)S(1)}, u32[]{:S(2)}, u32[]{:S(2)}) collective-permute-start(f32[1,96,128]{2,0,1:T(1,128)S(1)} %bitcast.51), channel_id=1, source_target_pairs={{0,256},{32,288},{64,320},{96,352},{128,384},{160,416},{192,448},{... | collective-permute-start | bytes 147464 | tf_op jit(solution)/shard_map/ppermute | solution.py:400
  25.7 15.5 %collective-permute-start.5 = (f32[384,128]{1,0:T(8,128)S(1)}, f32[384,128]{1,0:T(8,128)S(1)}, u32[]{:S(2)}, u32[]{:S(2)}) collective-permute-start(f32[384,128]{1,0:T(8,128)S(1)} %copy-done.2), channel_id=1, source_target_pairs={{1,0},{2,1},{3,2},{4,3},{5,4},{6,5},{7,6},{8,7},{9,8},{10,9},{11,1... | collective-permute-start | bytes 589832 | tf_op jit(solution)/shard_map/ppermute | solution.py:407
  30.6 10.7 %collective-permute-start.4 = (f32[384,128]{1,0:T(8,128)S(1)}, f32[384,128]{1,0:T(8,128)S(1)}, u32[]{:S(2)}, u32[]{:S(2)}) collective-permute-start(f32[384,128]{1,0:T(8,128)S(1)} %copy-done.2), channel_id=1, source_target_pairs={{0,1},{1,2},{2,3},{3,4},{4,5},{5,6},{6,7},{7,8},{8,9},{9,10},{10,1... | collective-permute-start | bytes 589832 | tf_op jit(solution)/shard_map/ppermute | solution.py:406
  32.5 8.8 %copy-start.7 = (s32[8,6]{1,0:T(8,128)S(1)}, s32[8,6]{1,0:T(8,128)}, u32[]{:S(2)}) copy-start(s32[8,6]{1,0:T(8,128)} %mask_leaf.1) | copy-start | bytes 580
  32.5 8.8 %copy-start.9 = (s32[4,6]{1,0:T(4,128)S(1)}, s32[4,6]{1,0:T(4,128)}, u32[]{:S(2)}) copy-start(s32[4,6]{1,0:T(4,128)} %mask_pair.1) | copy-start | bytes 292
  32.6 8.7 %copy-start.6 = (s32[8,6]{1,0:T(8,128)S(1)}, s32[8,6]{1,0:T(8,128)}, u32[]{:S(2)}) copy-start(s32[8,6]{1,0:T(8,128)} %list_leaf.1) | copy-start | bytes 580
  32.6 11.7 %collective-permute-start.3 = (f32[2,96,128]{2,0,1:T(2,128)S(1)}, f32[2,96,128]{2,0,1:T(2,128)S(1)}, u32[]{:S(2)}, u32[]{:S(2)}) collective-permute-start(f32[2,96,128]{2,0,1:T(2,128)S(1)} %pad_maximum_fusion), channel_id=1, source_target_pairs={{0,448},{32,96},{64,0},{96,160},{128,64},{160,224},{192,128},{224,... | collective-permute-start | bytes 294920 | tf_op jit(solution)/shard_map/ppermute | solution.py:400
  35.0 9.3 %collective-permute-start.2 = (f32[2,96,128]{2,0,1:T(2,128)S(1)}, f32[2,96,128]{2,0,1:T(2,128)S(1)}, u32[]{:S(2)}, u32[]{:S(2)}) collective-permute-start(f32[2,96,128]{2,0,1:T(2,128)S(1)} %pad_maximum_fusion), channel_id=1, source_target_pairs={{0,128},{32,416},{64,192},{96,480},{128,256},{160,32},{192,320},{2... | collective-permute-start | bytes 294920 | tf_op jit(solution)/shard_map/ppermute | solution.py:400
  38.6 7.7 %collective-permute-start.1 = (f32[2,96,128]{2,0,1:T(2,128)S(1)}, f32[2,96,128]{2,0,1:T(2,128)S(1)}, u32[]{:S(2)}, u32[]{:S(2)}) collective-permute-start(f32[2,96,128]{2,0,1:T(2,128)S(1)} %pad_maximum_fusion), channel_id=1, source_target_pairs={{0,64},{32,480},{64,128},{96,32},{128,192},{160,96},{192,256},{224... | collective-permute-start | bytes 294920 | tf_op jit(solution)/shard_map/ppermute | solution.py:400
  41.2 0.7 %copy-start.8 = (s32[4,6]{1,0:T(4,128)S(1)}, s32[4,6]{1,0:T(4,128)}, u32[]{:S(2)}) copy-start(s32[4,6]{1,0:T(4,128)} %list_pair.1) | copy-start | bytes 292
  46.3 4.0 %collective-permute-start.6 = (f32[32,40,128]{2,1,0:T(8,128)S(1)}, f32[32,40,128]{2,1,0:T(8,128)S(1)}, u32[]{:S(2)}, u32[]{:S(2)}) collective-permute-start(f32[32,40,128]{2,1,0:T(8,128)S(1)} %all-to-all-done.refs_0_), channel_id=1, source_target_pairs={{0,32},{32,0},{1,33},{33,1},{2,34},{34,2},{3,35},{35,3},{4,36},{36... | collective-permute-start | bytes 1966088 | tf_op jit(solution)/shard_map/ppermute | solution.py:422

commit v9 on v8

--- a/solution.py
+++ b/solution.py
@@ -124,7 +124,7 @@
     for copy in copies:
         copy.wait()
     for n, block in enumerate(weights_of(held[4:], natural)):
-        weight_ref[0, RANK * n : RANK * (n + 1), :] = block
+        weight_ref[RANK * n : RANK * (n + 1), :] = block
     writes[0].start()
     basis_copy.wait()
     for i in range(leaves):
@@ -217,19 +217,18 @@
             ).astype(BF16)
 
 
-def shifts(count):
-    half = count // 2
-    return [s if s <= half // 2 else s - half for s in range(1, half)]
+NEAR = (0, 1, -1)
+OFFSETS = (NEAR, tuple(3 + o for o in NEAR), tuple(-3 + o for o in NEAR[:2]))
 
 
 def part_kernel(own, *refs):
-    buffers = (len(refs) - (5 if own else 6)) // 2
+    buffers = len(OFFSETS)
     coeff_ref = refs[0]
     weight_refs, ids_refs = refs[1 : 1 + buffers], refs[1 + buffers : 1 + 2 * buffers]
     before_ref = None if own else refs[1 + 2 * buffers]
     out_ref, coeff_high, coeff_low, gathered = refs[-4:]
     subs = coeff_ref.shape[0]
-    rows_y = 2 * buffers
+    rows_y = lax.axis_size("y")
     slots, top_slots = 6, 4
     row, core = lax.axis_index("y"), lax.axis_index("core")
     source = row * 2 + (core if own else 1 - core)
@@ -252,15 +251,16 @@
         top = top + every[RANK * q : RANK * (q + 1), COLS * q : COLS * (q + 1)]
     lane_group = lanes(RANK) // RANK
     targets = []
-    for weight_ref, ids_ref, shift in zip(weight_refs, ids_refs, [0] + shifts(rows_y)):
-        targets += [(weight_ref, ids_ref, n, shift + n * buffers) for n in range(2)]
+    for weight_ref, ids_ref, offsets in zip(weight_refs, ids_refs, OFFSETS):
+        targets += [(weight_ref, ids_ref, n, offset) for n, offset in enumerate(offsets)]
     top_weight = []
     for weight_ref, ids_ref, n, _ in targets:
         used = jnp.zeros((RANK, COLS), F32)
         for k in range(top_slots):
             owner = ids_ref[n, 64 + slots + k].astype(jnp.int32)
             used = jnp.where(lane_group == k, jnp.where(owner == source, 1.0, 0.0), used)
-        top_weight.append(weight_ref[n, 2 * RANK : 3 * RANK, :] * used)
+        at = RANK * (3 * n + 2)
+        top_weight.append(weight_ref[at : at + RANK, :] * used)
     top_high, top_low = split(top)
     top_part = dot_split(
         jnp.concatenate(top_weight, axis=0),
@@ -286,7 +286,11 @@
             for ref in (coeff_high, coeff_low)
         ]
         weight = [
-            jnp.concatenate([w[n, 0:RANK, :], w[n, RANK : 2 * RANK, :64]], axis=1) for w, _, n, _ in two
+            jnp.concatenate(
+                [w[3 * RANK * n : RANK * (3 * n + 1), :], w[RANK * (3 * n + 1) : RANK * (3 * n + 2), :64]],
+                axis=1,
+            )
+            for w, _, n, _ in two
         ]
         both = dot_split(jnp.concatenate(weight, axis=0), *rows)
         for m, (_, _, _, offset) in enumerate(two):
@@ -374,7 +378,7 @@
         rows_of(couple_device), rows_of(down_device), rows_of(couple_top[0]),
         list_device, mask_device, list_top, mask_top,
     )
-    results = (shape(1, 3 * RANK, COLS), shape(blocks * RANK, COLS), shape(subs, RANK + ROWS8, COLS))
+    results = (shape(3 * RANK, COLS), shape(blocks * RANK, COLS), shape(subs, RANK + ROWS8, COLS))
     weights, stack, send = whole(
         first_kernel,
         results,
@@ -399,9 +403,9 @@
             moves.append((2 * y + 1, 2 * ((y - step) % targets) + 1))
         return lax.ppermute(block, ("y", "core"), moves)
 
-    weights = jnp.concatenate([weights, over_y(weights, targets // 2)], axis=0)
+    weights = jnp.concatenate([weights, over_y(weights, 1), over_y(weights, -1)], axis=0)
     coeffs = lax.all_to_all(send, ("x", "z"), 0, 0, tiled=True)
-    weights = [weights] + [over_y(weights, step) for step in shifts(targets)]
+    weights = [weights, over_y(weights, 3), over_y(weights[: 2 * 3 * RANK], -3)]
     leaf_axes = ("x", "z")
     low = lax.ppermute(stack, leaf_axes, [(i, i + 1) for i in range(subs - 1)])
     high = lax.ppermute(stack, leaf_axes, [(i + 1, i) for i in range(subs - 1)])
@@ -420,7 +424,7 @@
     )
     coeffs, weights, fixed, slope = lax.optimization_barrier((coeffs, weights, fixed, slope))
     other = lax.ppermute(coeffs, "core", [(0, 1), (1, 0)])
-    weights = [*weights, *(block[:, RANK, :] for block in weights)]
+    weights = [*weights, *(block[RANK :: 3 * RANK] for block in weights)]
     count = len(weights) // 2
     parts = []
     for own, gathered in ((True, coeffs), (False, other)):

time: 65.8 us -> 71.5 us (1.087)
  blocking collectives: 12.4 us -> 15.6 us
  starting transfers between devices: 38.7 us -> 40 us
  waiting for transfers between devices: 2.49 us -> 3.69 us
    all_to_all x1, blocking collectives: 12.4 us -> 15.6 us  [body(): parts = lax.all_to_all(parts, 'y', 0, 0, tiled=True)]
    ppermute x1, starting transfers between devices: 1.92 us -> 3.38 us  [body(): low = lax.ppermute(stack, leaf_axes, [(i, i + 1) for i in range(subs - 1)])]
    ppermute x4, waiting for transfers between devices: 2.01 us -> 3.31 us  [over_y(): return lax.ppermute(block, ('y', 'core'), moves)]
  transfers between devices with their start and end apart: 8 -> 8, of which waited for: 2 -> 3; matrix products, arithmetic and copies ran while one was open for 0% -> 0% of each run, Pallas kernels for 6% -> 6%
where the time goes in v9:
time: 71.5 us; the launch traced here: 71 us
  starting transfers between devices  40 us (56%)
  blocking collectives  15.6 us (22%)
  Pallas kernels  10.6 us (15%)
  waiting for transfers between devices  3.69 us (5%)
  local copies, waits for them, and re-layouts  0.74 us (1%)
    ppermute x4, starting transfers between devices, over_y(): return lax.ppermute(block, ('y', 'core'), moves)  16.4 us
    all_to_all x1, blocking collectives, body(): parts = lax.all_to_all(parts, 'y', 0, 0, tiled=True)  15.6 us
    all_to_all x1, starting transfers between devices, body(): coeffs = lax.all_to_all(send, ('x', 'z'), 0, 0, tiled=True)  13.6 us
    pallas_call x5, Pallas kernels, whole(): pl.pallas_call(kernel, out_shape=out, in_specs=[scalars if n in smem else...  10.6 us
    ppermute x1, starting transfers between devices, body(): high = lax.ppermute(stack, leaf_axes, [(i + 1, i) for i in range(subs - 1)])  4.57 us
    ppermute x1, starting transfers between devices, body(): low = lax.ppermute(stack, leaf_axes, [(i, i + 1) for i in range(subs - 1)])  3.38 us
    ppermute x4, waiting for transfers between devices, over_y(): return lax.ppermute(block, ('y', 'core'), moves)  3.31 us
    ppermute x1, starting transfers between devices, body(): other = lax.ppermute(coeffs, 'core', [(0, 1), (1, 0)])  2.02 us
  transfers between devices with their start and end apart: 8, of which 3 were waited for; matrix products, arithmetic and copies ran while one was open for 0% of the time, Pallas kernels for 6%

profile of v9, /device:TPU:6, one launch (start us, length us, event | category | flops | bytes accessed | tf_op | source)
XLA Modules:
  0.0 71.0 jit_solution(13717238114075737991)
XLA Ops:
  0.0 4.1 %shard_map.199 = (f32[96,128]{1,0:T(8,128)}, f32[384,128]{1,0:T(8,128)}, f32[32,40,128]{2,1,0:T(8,128)}) custom-call(f32[8,192,128]{2,1,0:T(8,128)} %refs_0_.1, f32[8,32,192]{2,1,0:T(8,128)} %refs_1_.1, f32[64,128]{1,0:T(8,128)} %bitcast.42, f32[32,128]{1,0:T(8,128)} %bitcast.44, f32[8,128]{1,0:T(8,128)} %bitcast.46, f32[48,128]{1,0:T(8,128)} %bitcast.43, ...), custom_call_target="tpu_custom_call" | custom-call | flops 60000000 | bytes 1982544 | tf_op jit(solution)/shard_map/pallas_call | solution.py:326
  4.1 0.0 copy-start.10
  4.1 0.0 copy-start.2
  4.1 0.0 copy-start.3
  4.1 0.0 copy-start.5
  4.2 0.0 copy-start.9
  4.2 13.6 %all-to-all-start = ((f32[32,40,128]{2,1,0:T(8,128)}), f32[32,40,128]{2,1,0:T(8,128)S(1)}, u32[]{:S(2)}, u32[]{:S(2)}) async-start(f32[32,40,128]{2,1,0:T(8,128)} %get-tuple-element.16), calls=%async_computation | async-start | bytes 1310720 | tf_op jit(solution)/shard_map/all_to_all | solution.py:407
  17.8 0.0 copy-start
  17.8 0.0 copy-done.10
  17.8 3.6 %collective-permute-start = (f32[96,128]{1,0:T(8,128)S(1)}, f32[96,128]{1,0:T(8,128)S(1)}, u32[]{:S(2)}, u32[]{:S(2)}) collective-permute-start(f32[96,128]{1,0:T(8,128)S(1)} %copy-done.10), channel_id=1, source_target_pairs={{0,64},{32,480},{64,128},{96,32},{128,192},{160,96},{192,256},{224... | collective-permute-start | bytes 147464 | tf_op jit(solution)/shard_map/ppermute | solution.py:404
  21.4 3.8 %collective-permute-start.1 = (f32[96,128]{1,0:T(8,128)S(1)}, f32[96,128]{1,0:T(8,128)S(1)}, u32[]{:S(2)}, u32[]{:S(2)}) collective-permute-start(f32[96,128]{1,0:T(8,128)S(1)} %copy-done.10), channel_id=1, source_target_pairs={{0,448},{32,96},{64,0},{96,160},{128,64},{160,224},{192,128},{224,... | collective-permute-start | bytes 147464 | tf_op jit(solution)/shard_map/ppermute | solution.py:404
  25.2 0.0 copy-done.2
  25.2 3.4 %collective-permute-start.4 = (f32[384,128]{1,0:T(8,128)S(1)}, f32[384,128]{1,0:T(8,128)S(1)}, u32[]{:S(2)}, u32[]{:S(2)}) collective-permute-start(f32[384,128]{1,0:T(8,128)S(1)} %copy-done.2), channel_id=1, source_target_pairs={{0,1},{1,2},{2,3},{3,4},{4,5},{5,6},{6,7},{7,8},{8,9},{9,10},{10,1... | collective-permute-start | bytes 589832 | tf_op jit(solution)/shard_map/ppermute | solution.py:410
  28.6 4.6 %collective-permute-start.5 = (f32[384,128]{1,0:T(8,128)S(1)}, f32[384,128]{1,0:T(8,128)S(1)}, u32[]{:S(2)}, u32[]{:S(2)}) collective-permute-start(f32[384,128]{1,0:T(8,128)S(1)} %copy-done.2), channel_id=1, source_target_pairs={{1,0},{2,1},{3,2},{4,3},{5,4},{6,5},{7,6},{8,7},{9,8},{10,9},{11,1... | collective-permute-start | bytes 589832 | tf_op jit(solution)/shard_map/ppermute | solution.py:411
  33.2 0.0 copy-start.1
  33.2 0.0 collective-permute-done
  33.3 0.0 collective-permute-done.1
  33.3 0.0 copy-start.4
  33.3 5.0 %collective-permute-start.2 = (f32[288,128]{1,0:T(8,128)S(1)}, f32[288,128]{1,0:T(8,128)S(1)}, u32[]{:S(2)}, u32[]{:S(2)}) collective-permute-start(f32[288,128]{1,0:T(8,128)S(1)} %constant_dynamic-update-slice_fusion.refs_1_), channel_id=1, source_target_pairs={{0,192},{32,352},{64,256},{96,416},{128,320},{160,480},{192,384},{... | collective-permute-start | bytes 442376 | tf_op jit(solution)/shard_map/ppermute | solution.py:404
  38.3 0.0 copy-start.7
  38.3 0.0 copy-start.6
  38.3 4.0 %collective-permute-start.3 = (f32[192,128]{1,0:T(8,128)S(1)}, f32[192,128]{1,0:T(8,128)S(1)}, u32[]{:S(2)}, u32[]{:S(2)}) collective-permute-start(f32[192,128]{1,0:T(8,128)S(1)} %pad_maximum_fusion), channel_id=1, source_target_pairs={{0,320},{32,224},{64,384},{96,288},{128,448},{160,352},{192,0},{22... | collective-permute-start | bytes 294920 | tf_op jit(solution)/shard_map/ppermute | solution.py:404
  42.3 0.0 collective-permute-done.4.low_ref
  42.4 0.0 collective-permute-done.5.high_ref
  42.4 0.0 copy-start.8
  42.4 0.0 copy-done.3
  42.4 0.0 copy-done.5
  42.4 0.0 copy-done.9
  42.4 0.0 copy-done
  42.4 0.0 copy-done.1
  42.4 0.0 copy-done.4
  42.4 0.0 copy-done.7
  42.4 0.0 copy-done.6
  42.5 0.6 copy-done.8
  43.0 2.4 %shard_map.200 = (f32[8,192,128]{2,1,0:T(8,128)S(1)}, bf16[8,192,128]{2,1,0:T(8,128)(2,1)S(1)}) custom-call(f32[384,128]{1,0:T(8,128)S(1)} %collective-permute-done.4.low_ref, f32[384,128]{1,0:T(8,128)S(1)} %copy-done.2, f32[384,128]{1,0:T(8,128)S(1)} %collective-permute-done.5.high_ref, f32[384,128]{1,0:T(8,128)S(1)} %bitcast.38, f32[192,128]{1,0:T(8,128)S(1)} %bitcast.39, ...), custom_call_target="tpu_custom_call" | custom-call | flops 100000000 | bytes 2310720 | tf_op jit(solution)/shard_map/pallas_call | solution.py:326
  45.4 1.4 %collective-permute-done.3.refs_3_ = f32[192,128]{1,0:T(8,128)S(1)} collective-permute-done((f32[192,128]{1,0:T(8,128)S(1)}, f32[192,128]{1,0:T(8,128)S(1)}, u32[]{:S(2)}, u32[]{:S(2)}) %collective-permute-start.3) | collective-permute-done | bytes 98336 | tf_op jit(solution)/shard_map/ppermute | solution.py:404
  46.8 1.9 %collective-permute-done.2.refs_2_ = f32[288,128]{1,0:T(8,128)S(1)} collective-permute-done((f32[288,128]{1,0:T(8,128)S(1)}, f32[288,128]{1,0:T(8,128)S(1)}, u32[]{:S(2)}, u32[]{:S(2)}) %collective-permute-start.2) | collective-permute-done | bytes 147488 | tf_op jit(solution)/shard_map/ppermute | solution.py:404
  48.8 0.0 all-to-all-done.refs_0_
  48.8 2.0 %collective-permute-start.6 = (f32[32,40,128]{2,1,0:T(8,128)S(1)}, f32[32,40,128]{2,1,0:T(8,128)S(1)}, u32[]{:S(2)}, u32[]{:S(2)}) collective-permute-start(f32[32,40,128]{2,1,0:T(8,128)S(1)} %all-to-all-done.refs_0_), channel_id=1, source_target_pairs={{0,32},{32,0},{1,33},{33,1},{2,34},{34,2},{3,35},{35,3},{4,36},{36... | collective-permute-start | bytes 1966088 | tf_op jit(solution)/shard_map/ppermute | solution.py:426
  50.8 1.5 %shard_map.201.refs_7_ = f32[8,32,128]{2,1,0:T(8,128)S(1)} custom-call(f32[32,40,128]{2,1,0:T(8,128)S(1)} %all-to-all-done.refs_0_, f32[288,128]{1,0:T(8,128)S(1)} %constant_dynamic-update-slice_fusion.refs_1_, f32[288,128]{1,0:T(8,128)S(1)} %collective-permute-done.2.refs_2_, f32[192,128]{1,0:T(8,128)S(1)} %collective-permute-done.3.refs_3_, ...), custom_call_target="tpu_custom_call" | custom-call | flops 50000000 | bytes 1183744 | tf_op jit(solution)/shard_map/pallas_call | solution.py:326
  52.4 0.4 collective-permute-done.6.refs_0_
  52.7 1.5 %shard_map.202 = f32[8,32,128]{2,1,0:T(8,128)S(1)} custom-call(f32[32,40,128]{2,1,0:T(8,128)S(1)} %collective-permute-done.6.refs_0_, f32[288,128]{1,0:T(8,128)S(1)} %constant_dynamic-update-slice_fusion.refs_1_, f32[288,128]{1,0:T(8,128)S(1)} %collective-permute-done.2.refs_2_, f32[192,128]{1,0:T(8,128)S(1)} %collective-permute-done.3.refs_3_, ...), custom_call_target="tpu_custom_call" | custom-call | flops 50000000 | bytes 1314816 | tf_op jit(solution)/shard_map/pallas_call | solution.py:326
  54.3 15.6 %all_to_all.10.parts_ref = f32[8,32,128]{2,1,0:T(8,128)S(1)} all-to-all(f32[8,32,128]{2,1,0:T(8,128)S(1)} %shard_map.202), channel_id=1, replica_groups=mesh['y'=8,'core'=2,'x'=4,'z'=8] {'y'}, dimensions={0} | all-to-all | bytes 262144 | tf_op jit(solution)/shard_map/all_to_all | solution.py:443
  69.9 1.1 %shard_map.203 = f32[8,192,128]{2,1,0:T(8,128)} custom-call(f32[8,32,128]{2,1,0:T(8,128)S(1)} %all_to_all.10.parts_ref, f32[8,192,128]{2,1,0:T(8,128)S(1)} %get-tuple-element.25.fixed_ref, bf16[8,192,128]{2,1,0:T(8,128)(2,1)S(1)} %get-tuple-element.26.slope_ref), custom_call_target="tpu_custom_call" | custom-call | flops 50000000 | bytes 2097152 | tf_op jit(solution)/shard_map/pallas_call | solution.py:326
  (7 shorter events, 0.1 us)
Async XLA Ops:
  4.1 13.7 %copy-start.10 = (f32[96,128]{1,0:T(8,128)S(1)}, f32[96,128]{1,0:T(8,128)}, u32[]{:S(2)}) copy-start(f32[96,128]{1,0:T(8,128)} %get-tuple-element.17) | copy-start | bytes 147460
  4.1 21.1 %copy-start.2 = (f32[384,128]{1,0:T(8,128)S(1)}, f32[384,128]{1,0:T(8,128)}, u32[]{:S(2)}) copy-start(f32[384,128]{1,0:T(8,128)} %get-tuple-element.18.own_ref) | copy-start | bytes 589828
  4.1 38.2 %copy-start.3 = (f32[4,6,1024]{2,0,1:T(4,128)S(1)}, f32[4,6,1024]{2,0,1:T(4,128)}, u32[]{:S(2)}) copy-start(f32[4,6,1024]{2,0,1:T(4,128)} %param.27) | copy-start | bytes 294916
  4.1 38.2 %copy-start.5 = (f32[4,1024]{1,0:T(4,128)S(1)}, f32[4,1024]{1,0:T(4,128)}, u32[]{:S(2)}) copy-start(f32[4,1024]{1,0:T(4,128)} %param.39) | copy-start | bytes 49156
  4.2 38.2 %copy-start.9 = (s32[4,6]{1,0:T(4,128)S(1)}, s32[4,6]{1,0:T(4,128)}, u32[]{:S(2)}) copy-start(s32[4,6]{1,0:T(4,128)} %mask_pair.1) | copy-start | bytes 292
  4.2 44.6 %all-to-all-start = ((f32[32,40,128]{2,1,0:T(8,128)}), f32[32,40,128]{2,1,0:T(8,128)S(1)}, u32[]{:S(2)}, u32[]{:S(2)}) async-start(f32[32,40,128]{2,1,0:T(8,128)} %get-tuple-element.16), calls=%async_computation | async-start | bytes 1310720 | tf_op jit(solution)/shard_map/all_to_all | solution.py:407
  17.8 24.6 %copy-start = (f32[8,32,192]{2,1,0:T(8,128)S(1)}, f32[8,32,192]{2,1,0:T(8,128)}, u32[]{:S(2)}) copy-start(f32[8,32,192]{2,1,0:T(8,128)} %basis.1) | copy-start | bytes 589828
  17.8 15.5 %collective-permute-start = (f32[96,128]{1,0:T(8,128)S(1)}, f32[96,128]{1,0:T(8,128)S(1)}, u32[]{:S(2)}, u32[]{:S(2)}) collective-permute-start(f32[96,128]{1,0:T(8,128)S(1)} %copy-done.10), channel_id=1, source_target_pairs={{0,64},{32,480},{64,128},{96,32},{128,192},{160,96},{192,256},{224... | collective-permute-start | bytes 147464 | tf_op jit(solution)/shard_map/ppermute | solution.py:404
  21.4 11.9 %collective-permute-start.1 = (f32[96,128]{1,0:T(8,128)S(1)}, f32[96,128]{1,0:T(8,128)S(1)}, u32[]{:S(2)}, u32[]{:S(2)}) collective-permute-start(f32[96,128]{1,0:T(8,128)S(1)} %copy-done.10), channel_id=1, source_target_pairs={{0,448},{32,96},{64,0},{96,160},{128,64},{160,224},{192,128},{224,... | collective-permute-start | bytes 147464 | tf_op jit(solution)/shard_map/ppermute | solution.py:404
  25.2 17.1 %collective-permute-start.4 = (f32[384,128]{1,0:T(8,128)S(1)}, f32[384,128]{1,0:T(8,128)S(1)}, u32[]{:S(2)}, u32[]{:S(2)}) collective-permute-start(f32[384,128]{1,0:T(8,128)S(1)} %copy-done.2), channel_id=1, source_target_pairs={{0,1},{1,2},{2,3},{3,4},{4,5},{5,6},{6,7},{7,8},{8,9},{9,10},{10,1... | collective-permute-start | bytes 589832 | tf_op jit(solution)/shard_map/ppermute | solution.py:410
  28.6 13.7 %collective-permute-start.5 = (f32[384,128]{1,0:T(8,128)S(1)}, f32[384,128]{1,0:T(8,128)S(1)}, u32[]{:S(2)}, u32[]{:S(2)}) collective-permute-start(f32[384,128]{1,0:T(8,128)S(1)} %copy-done.2), channel_id=1, source_target_pairs={{1,0},{2,1},{3,2},{4,3},{5,4},{6,5},{7,6},{8,7},{9,8},{10,9},{11,1... | collective-permute-start | bytes 589832 | tf_op jit(solution)/shard_map/ppermute | solution.py:411
  33.2 9.2 %copy-start.1 = (f32[8,6,1024]{2,0,1:T(8,128)S(1)}, f32[8,6,1024]{2,0,1:T(8,128)}, u32[]{:S(2)}) copy-start(f32[8,6,1024]{2,0,1:T(8,128)} %param.26) | copy-start | bytes 589828
  33.3 9.1 %copy-start.4 = (f32[8,1024]{1,0:T(8,128)S(1)}, f32[8,1024]{1,0:T(8,128)}, u32[]{:S(2)}) copy-start(f32[8,1024]{1,0:T(8,128)} %param.38) | copy-start | bytes 98308
  33.3 15.4 %collective-permute-start.2 = (f32[288,128]{1,0:T(8,128)S(1)}, f32[288,128]{1,0:T(8,128)S(1)}, u32[]{:S(2)}, u32[]{:S(2)}) collective-permute-start(f32[288,128]{1,0:T(8,128)S(1)} %constant_dynamic-update-slice_fusion.refs_1_), channel_id=1, source_target_pairs={{0,192},{32,352},{64,256},{96,416},{128,320},{160,480},{192,384},{... | collective-permute-start | bytes 442376 | tf_op jit(solution)/shard_map/ppermute | solution.py:404
  38.3 4.2 %copy-start.7 = (s32[8,6]{1,0:T(8,128)S(1)}, s32[8,6]{1,0:T(8,128)}, u32[]{:S(2)}) copy-start(s32[8,6]{1,0:T(8,128)} %mask_leaf.1) | copy-start | bytes 580
  38.3 4.1 %copy-start.6 = (s32[8,6]{1,0:T(8,128)S(1)}, s32[8,6]{1,0:T(8,128)}, u32[]{:S(2)}) copy-start(s32[8,6]{1,0:T(8,128)} %list_leaf.1) | copy-start | bytes 580
  38.3 8.5 %collective-permute-start.3 = (f32[192,128]{1,0:T(8,128)S(1)}, f32[192,128]{1,0:T(8,128)S(1)}, u32[]{:S(2)}, u32[]{:S(2)}) collective-permute-start(f32[192,128]{1,0:T(8,128)S(1)} %pad_maximum_fusion), channel_id=1, source_target_pairs={{0,320},{32,224},{64,384},{96,288},{128,448},{160,352},{192,0},{22... | collective-permute-start | bytes 294920 | tf_op jit(solution)/shard_map/ppermute | solution.py:404
  42.4 0.7 copy-start.8
  48.8 4.0 %collective-permute-start.6 = (f32[32,40,128]{2,1,0:T(8,128)S(1)}, f32[32,40,128]{2,1,0:T(8,128)S(1)}, u32[]{:S(2)}, u32[]{:S(2)}) collective-permute-start(f32[32,40,128]{2,1,0:T(8,128)S(1)} %all-to-all-done.refs_0_), channel_id=1, source_target_pairs={{0,32},{32,0},{1,33},{33,1},{2,34},{34,2},{3,35},{35,3},{4,36},{36... | collective-permute-start | bytes 1966088 | tf_op jit(solution)/shard_map/ppermute | solution.py:426

commit v10 on v8

--- a/solution.py
+++ b/solution.py
@@ -162,10 +162,12 @@
     leaf = lax.axis_index("x") * lax.axis_size("z") + lax.axis_index("z")
     position = top * (lax.axis_size("x") * lax.axis_size("z")) + leaf
     size = blocks * RANK
-    for n, ref in enumerate((low_ref, own_ref, high_ref)):
+    swap = 2 * lax.axis_index("core")
+    for n, ref in ((swap, low_ref), (1, own_ref), (2 - swap, high_ref)):
         high, low = split(ref[...])
-        near_high[n * size : (n + 1) * size, :] = high
-        near_low[n * size : (n + 1) * size, :] = low
+        start = pl.multiple_of(n * size, size)
+        near_high[pl.ds(start, size), :] = high
+        near_low[pl.ds(start, size), :] = low
     none = jnp.zeros((RANK, COLS), BF16)
     near_high[3 * size : 3 * size + RANK, :] = none
     near_low[3 * size : 3 * size + RANK, :] = none
@@ -403,8 +405,14 @@
     coeffs = lax.all_to_all(send, ("x", "z"), 0, 0, tiled=True)
     weights = [weights] + [over_y(weights, step) for step in shifts(targets)]
     leaf_axes = ("x", "z")
-    low = lax.ppermute(stack, leaf_axes, [(i, i + 1) for i in range(subs - 1)])
-    high = lax.ppermute(stack, leaf_axes, [(i + 1, i) for i in range(subs - 1)])
+    up = [(i, i + 1) for i in range(subs - 1)]
+    down = [(i + 1, i) for i in range(subs - 1)]
+
+    def halo(first, second):
+        moves = first + [(subs + i, subs + j) for i, j in second]
+        return lax.ppermute(stack, ("core", *leaf_axes), moves)
+
+    low, high = halo(up, down), halo(down, up)
     near = pltpu.VMEM(((3 * blocks + 1) * RANK, COLS), BF16)
     fixed, slope = whole(
         far_kernel,

time: 65.8 us -> 65.8 us (level)
  no operation moved by 1% of the time
where the time goes in v10:
time: 65.8 us; the launch traced here: 65.3 us
  starting transfers between devices  38.7 us (59%)
  blocking collectives  12.4 us (19%)
  Pallas kernels  10.7 us (16%)
  waiting for transfers between devices  2.43 us (4%)
  local copies, waits for them, and re-layouts  0.7 us (1%)
    ppermute x4, starting transfers between devices, over_y(): return lax.ppermute(block, ('y', 'core'), moves)  16.4 us
    all_to_all x1, starting transfers between devices, body(): coeffs = lax.all_to_all(send, ('x', 'z'), 0, 0, tiled=True)  13.6 us
    all_to_all x1, blocking collectives, body(): parts = lax.all_to_all(parts, 'y', 0, 0, tiled=True)  12.4 us
    pallas_call x5, Pallas kernels, whole(): pl.pallas_call(kernel, out_shape=out, in_specs=[scalars if n in smem else...  10.7 us
    ppermute x2, starting transfers between devices, halo(): return lax.ppermute(stack, ('core', *leaf_axes), moves)  6.79 us
    ppermute x4, waiting for transfers between devices, over_y(): return lax.ppermute(block, ('y', 'core'), moves)  1.95 us
    ppermute x1, starting transfers between devices, body(): other = lax.ppermute(coeffs, 'core', [(0, 1), (1, 0)])  1.91 us
  transfers between devices with their start and end apart: 8, of which 2 were waited for; matrix products, arithmetic and copies ran while one was open for 0% of the time, Pallas kernels for 6%

profile of v10, /device:TPU:6, one launch (start us, length us, event | category | flops | bytes accessed | tf_op | source)
XLA Modules:
  0.0 65.3 jit_solution(3742324365369446146)
XLA Ops:
  0.0 4.1 %shard_map.199 = (f32[1,96,128]{2,1,0:T(8,128)}, f32[384,128]{1,0:T(8,128)}, f32[32,40,128]{2,1,0:T(8,128)}) custom-call(f32[8,192,128]{2,1,0:T(8,128)} %refs_0_.1, f32[8,32,192]{2,1,0:T(8,128)} %refs_1_.1, f32[64,128]{1,0:T(8,128)} %bitcast.53, f32[32,128]{1,0:T(8,128)} %bitcast.55, f32[8,128]{1,0:T(8,128)} %bitcast.57, f32[48,128]{1,0:T(8,128)} %bitcast.54, ...), custom_call_target="tpu_custom_call" | custom-call | flops 60000000 | bytes 1982544 | tf_op jit(solution)/shard_map/pallas_call | solution.py:324
  4.1 0.0 copy-start.10
  4.1 0.0 copy-start.2
  4.1 0.0 copy-start
  4.1 0.0 copy-start.3
  4.2 0.0 copy-start.4
  4.2 0.0 copy-start.5
  4.2 13.6 %all-to-all-start = ((f32[32,40,128]{2,1,0:T(8,128)}), f32[32,40,128]{2,1,0:T(8,128)S(1)}, u32[]{:S(2)}, u32[]{:S(2)}) async-start(f32[32,40,128]{2,1,0:T(8,128)} %get-tuple-element.17), calls=%async_computation | async-start | bytes 1310720 | tf_op jit(solution)/shard_map/all_to_all | solution.py:405
  17.8 0.0 copy-start.1
  17.8 0.0 copy-done.10
  17.8 7.9 %collective-permute-start = (f32[1,96,128]{2,0,1:T(1,128)S(1)}, f32[1,96,128]{2,0,1:T(1,128)S(1)}, u32[]{:S(2)}, u32[]{:S(2)}) collective-permute-start(f32[1,96,128]{2,0,1:T(1,128)S(1)} %bitcast.51), channel_id=1, source_target_pairs={{0,256},{32,288},{64,320},{96,352},{128,384},{160,416},{192,448},{... | collective-permute-start | bytes 147464 | tf_op jit(solution)/shard_map/ppermute | solution.py:402
  25.7 0.0 copy-done.2
  25.7 4.9 %collective-permute-start.5 = (f32[384,128]{1,0:T(8,128)S(1)}, f32[384,128]{1,0:T(8,128)S(1)}, u32[]{:S(2)}, u32[]{:S(2)}) collective-permute-start(f32[384,128]{1,0:T(8,128)S(1)} %copy-done.2), channel_id=1, source_target_pairs={{1,0},{2,1},{3,2},{4,3},{5,4},{6,5},{7,6},{8,7},{9,8},{10,9},{11,1... | collective-permute-start | bytes 589832 | tf_op jit(solution)/shard_map/ppermute | solution.py:413
  30.6 1.9 %collective-permute-start.4 = (f32[384,128]{1,0:T(8,128)S(1)}, f32[384,128]{1,0:T(8,128)S(1)}, u32[]{:S(2)}, u32[]{:S(2)}) collective-permute-start(f32[384,128]{1,0:T(8,128)S(1)} %copy-done.2), channel_id=1, source_target_pairs={{0,1},{1,2},{2,3},{3,4},{4,5},{5,6},{6,7},{7,8},{8,9},{9,10},{10,1... | collective-permute-start | bytes 589832 | tf_op jit(solution)/shard_map/ppermute | solution.py:413
  32.5 0.0 collective-permute-done
  32.5 0.0 copy-start.7
  32.5 0.0 copy-start.9
  32.5 0.1 pad_maximum_fusion
  32.6 0.0 copy-start.6
  32.6 2.4 %collective-permute-start.3 = (f32[2,96,128]{2,0,1:T(2,128)S(1)}, f32[2,96,128]{2,0,1:T(2,128)S(1)}, u32[]{:S(2)}, u32[]{:S(2)}) collective-permute-start(f32[2,96,128]{2,0,1:T(2,128)S(1)} %pad_maximum_fusion), channel_id=1, source_target_pairs={{0,448},{32,96},{64,0},{96,160},{128,64},{160,224},{192,128},{224,... | collective-permute-start | bytes 294920 | tf_op jit(solution)/shard_map/ppermute | solution.py:402
  35.0 3.6 %collective-permute-start.2 = (f32[2,96,128]{2,0,1:T(2,128)S(1)}, f32[2,96,128]{2,0,1:T(2,128)S(1)}, u32[]{:S(2)}, u32[]{:S(2)}) collective-permute-start(f32[2,96,128]{2,0,1:T(2,128)S(1)} %pad_maximum_fusion), channel_id=1, source_target_pairs={{0,128},{32,416},{64,192},{96,480},{128,256},{160,32},{192,320},{2... | collective-permute-start | bytes 294920 | tf_op jit(solution)/shard_map/ppermute | solution.py:402
  38.6 2.6 %collective-permute-start.1 = (f32[2,96,128]{2,0,1:T(2,128)S(1)}, f32[2,96,128]{2,0,1:T(2,128)S(1)}, u32[]{:S(2)}, u32[]{:S(2)}) collective-permute-start(f32[2,96,128]{2,0,1:T(2,128)S(1)} %pad_maximum_fusion), channel_id=1, source_target_pairs={{0,64},{32,480},{64,128},{96,32},{128,192},{160,96},{192,256},{224... | collective-permute-start | bytes 294920 | tf_op jit(solution)/shard_map/ppermute | solution.py:402
  41.2 0.0 collective-permute-done.5.high_ref
  41.2 0.0 collective-permute-done.4.low_ref
  41.2 0.0 copy-start.8
  41.2 0.0 copy-done
  41.3 0.0 copy-done.3
  41.3 0.0 copy-done.4
  41.3 0.0 copy-done.5
  41.3 0.0 copy-done.1
  41.3 0.0 copy-done.7
  41.3 0.0 copy-done.9
  41.3 0.0 copy-done.6
  41.3 0.6 copy-done.8
  41.9 2.5 %shard_map.200 = (f32[8,192,128]{2,1,0:T(8,128)S(1)}, bf16[8,192,128]{2,1,0:T(8,128)(2,1)S(1)}) custom-call(f32[384,128]{1,0:T(8,128)S(1)} %collective-permute-done.4.low_ref, f32[384,128]{1,0:T(8,128)S(1)} %copy-done.2, f32[384,128]{1,0:T(8,128)S(1)} %collective-permute-done.5.high_ref, f32[384,128]{1,0:T(8,128)S(1)} %bitcast.47, f32[192,128]{1,0:T(8,128)S(1)} %bitcast.48, ...), custom_call_target="tpu_custom_call" | custom-call | flops 100000000 | bytes 2310720 | tf_op jit(solution)/shard_map/pallas_call | solution.py:324
  44.4 0.0 collective-permute-done.3
  44.4 0.0 collective-permute-done.2
  44.4 1.9 %collective-permute-done.1 = f32[2,96,128]{2,0,1:T(2,128)S(1)} collective-permute-done((f32[2,96,128]{2,0,1:T(2,128)S(1)}, f32[2,96,128]{2,0,1:T(2,128)S(1)}, u32[]{:S(2)}, u32[]{:S(2)}) %collective-permute-start.1) | collective-permute-done | bytes 98336 | tf_op jit(solution)/shard_map/ppermute | solution.py:402
  46.3 0.0 all-to-all-done.refs_0_
  46.3 1.9 %collective-permute-start.6 = (f32[32,40,128]{2,1,0:T(8,128)S(1)}, f32[32,40,128]{2,1,0:T(8,128)S(1)}, u32[]{:S(2)}, u32[]{:S(2)}) collective-permute-start(f32[32,40,128]{2,1,0:T(8,128)S(1)} %all-to-all-done.refs_0_), channel_id=1, source_target_pairs={{0,32},{32,0},{1,33},{33,1},{2,34},{34,2},{3,35},{35,3},{4,36},{36... | collective-permute-start | bytes 1966088 | tf_op jit(solution)/shard_map/ppermute | solution.py:430
  48.3 1.5 %shard_map.201.refs_9_ = f32[8,32,128]{2,1,0:T(8,128)S(1)} custom-call(f32[32,40,128]{2,1,0:T(8,128)S(1)} %all-to-all-done.refs_0_, f32[2,96,128]{2,1,0:T(8,128)S(1)} %copy.32.refs_1_, f32[2,96,128]{2,1,0:T(8,128)S(1)} %copy.33.refs_2_, f32[2,96,128]{2,1,0:T(8,128)S(1)} %copy.34.refs_3_, f32[2,96,128]{2,1,0:T(8,128)S(1)} %copy.35.refs_4_, ...), custom_call_target="tpu_custom_call" | custom-call | flops 50000000 | bytes 1183744 | tf_op jit(solution)/shard_map/pallas_call | solution.py:324
  49.9 0.5 collective-permute-done.6.refs_0_
  50.3 1.5 %shard_map.202 = f32[8,32,128]{2,1,0:T(8,128)S(1)} custom-call(f32[32,40,128]{2,1,0:T(8,128)S(1)} %collective-permute-done.6.refs_0_, f32[2,96,128]{2,1,0:T(8,128)S(1)} %copy.32.refs_1_, f32[2,96,128]{2,1,0:T(8,128)S(1)} %copy.33.refs_2_, f32[2,96,128]{2,1,0:T(8,128)S(1)} %copy.34.refs_3_, f32[2,96,128]{2,1,0:T(8,128)S(1)} %copy.35.refs_4_, ...), custom_call_target="tpu_custom_call" | custom-call | flops 50000000 | bytes 1314816 | tf_op jit(solution)/shard_map/pallas_call | solution.py:324
  51.8 12.4 %all_to_all.10.parts_ref = f32[8,32,128]{2,1,0:T(8,128)S(1)} all-to-all(f32[8,32,128]{2,1,0:T(8,128)S(1)} %shard_map.202), channel_id=1, replica_groups=mesh['y'=8,'core'=2,'x'=4,'z'=8] {'y'}, dimensions={0} | all-to-all | bytes 262144 | tf_op jit(solution)/shard_map/all_to_all | solution.py:447
  64.2 1.1 %shard_map.203 = f32[8,192,128]{2,1,0:T(8,128)} custom-call(f32[8,32,128]{2,1,0:T(8,128)S(1)} %all_to_all.10.parts_ref, f32[8,192,128]{2,1,0:T(8,128)S(1)} %get-tuple-element.27.fixed_ref, bf16[8,192,128]{2,1,0:T(8,128)(2,1)S(1)} %get-tuple-element.28.slope_ref), custom_call_target="tpu_custom_call" | custom-call | flops 50000000 | bytes 2097152 | tf_op jit(solution)/shard_map/pallas_call | solution.py:324
  (6 shorter events, 0.0 us)
Async XLA Ops:
  4.1 13.7 %copy-start.10 = (f32[1,96,128]{2,1,0:T(8,128)S(1)}, f32[1,96,128]{2,1,0:T(8,128)}, u32[]{:S(2)}) copy-start(f32[1,96,128]{2,1,0:T(8,128)} %get-tuple-element.18) | copy-start | bytes 147460
  4.1 21.6 %copy-start.2 = (f32[384,128]{1,0:T(8,128)S(1)}, f32[384,128]{1,0:T(8,128)}, u32[]{:S(2)}) copy-start(f32[384,128]{1,0:T(8,128)} %get-tuple-element.19.own_ref) | copy-start | bytes 589828
  4.1 37.1 %copy-start = (f32[8,32,192]{2,1,0:T(8,128)S(1)}, f32[8,32,192]{2,1,0:T(8,128)}, u32[]{:S(2)}) copy-start(f32[8,32,192]{2,1,0:T(8,128)} %basis.1) | copy-start | bytes 589828
  4.1 37.1 %copy-start.3 = (f32[4,6,1024]{2,0,1:T(4,128)S(1)}, f32[4,6,1024]{2,0,1:T(4,128)}, u32[]{:S(2)}) copy-start(f32[4,6,1024]{2,0,1:T(4,128)} %param.27) | copy-start | bytes 294916
  4.2 37.1 %copy-start.4 = (f32[8,1024]{1,0:T(8,128)S(1)}, f32[8,1024]{1,0:T(8,128)}, u32[]{:S(2)}) copy-start(f32[8,1024]{1,0:T(8,128)} %param.38) | copy-start | bytes 98308
  4.2 37.1 %copy-start.5 = (f32[4,1024]{1,0:T(4,128)S(1)}, f32[4,1024]{1,0:T(4,128)}, u32[]{:S(2)}) copy-start(f32[4,1024]{1,0:T(4,128)} %param.39) | copy-start | bytes 49156
  4.2 42.2 %all-to-all-start = ((f32[32,40,128]{2,1,0:T(8,128)}), f32[32,40,128]{2,1,0:T(8,128)S(1)}, u32[]{:S(2)}, u32[]{:S(2)}) async-start(f32[32,40,128]{2,1,0:T(8,128)} %get-tuple-element.17), calls=%async_computation | async-start | bytes 1310720 | tf_op jit(solution)/shard_map/all_to_all | solution.py:405
  17.8 23.5 %copy-start.1 = (f32[8,6,1024]{2,0,1:T(8,128)S(1)}, f32[8,6,1024]{2,0,1:T(8,128)}, u32[]{:S(2)}) copy-start(f32[8,6,1024]{2,0,1:T(8,128)} %param.26) | copy-start | bytes 589828
  17.8 14.7 %collective-permute-start = (f32[1,96,128]{2,0,1:T(1,128)S(1)}, f32[1,96,128]{2,0,1:T(1,128)S(1)}, u32[]{:S(2)}, u32[]{:S(2)}) collective-permute-start(f32[1,96,128]{2,0,1:T(1,128)S(1)} %bitcast.51), channel_id=1, source_target_pairs={{0,256},{32,288},{64,320},{96,352},{128,384},{160,416},{192,448},{... | collective-permute-start | bytes 147464 | tf_op jit(solution)/shard_map/ppermute | solution.py:402
  25.7 15.5 %collective-permute-start.5 = (f32[384,128]{1,0:T(8,128)S(1)}, f32[384,128]{1,0:T(8,128)S(1)}, u32[]{:S(2)}, u32[]{:S(2)}) collective-permute-start(f32[384,128]{1,0:T(8,128)S(1)} %copy-done.2), channel_id=1, source_target_pairs={{1,0},{2,1},{3,2},{4,3},{5,4},{6,5},{7,6},{8,7},{9,8},{10,9},{11,1... | collective-permute-start | bytes 589832 | tf_op jit(solution)/shard_map/ppermute | solution.py:413
  30.6 10.7 %collective-permute-start.4 = (f32[384,128]{1,0:T(8,128)S(1)}, f32[384,128]{1,0:T(8,128)S(1)}, u32[]{:S(2)}, u32[]{:S(2)}) collective-permute-start(f32[384,128]{1,0:T(8,128)S(1)} %copy-done.2), channel_id=1, source_target_pairs={{0,1},{1,2},{2,3},{3,4},{4,5},{5,6},{6,7},{7,8},{8,9},{9,10},{10,1... | collective-permute-start | bytes 589832 | tf_op jit(solution)/shard_map/ppermute | solution.py:413
  32.5 8.8 %copy-start.7 = (s32[8,6]{1,0:T(8,128)S(1)}, s32[8,6]{1,0:T(8,128)}, u32[]{:S(2)}) copy-start(s32[8,6]{1,0:T(8,128)} %mask_leaf.1) | copy-start | bytes 580
  32.5 8.8 %copy-start.9 = (s32[4,6]{1,0:T(4,128)S(1)}, s32[4,6]{1,0:T(4,128)}, u32[]{:S(2)}) copy-start(s32[4,6]{1,0:T(4,128)} %mask_pair.1) | copy-start | bytes 292
  32.6 8.7 %copy-start.6 = (s32[8,6]{1,0:T(8,128)S(1)}, s32[8,6]{1,0:T(8,128)}, u32[]{:S(2)}) copy-start(s32[8,6]{1,0:T(8,128)} %list_leaf.1) | copy-start | bytes 580
  32.6 11.7 %collective-permute-start.3 = (f32[2,96,128]{2,0,1:T(2,128)S(1)}, f32[2,96,128]{2,0,1:T(2,128)S(1)}, u32[]{:S(2)}, u32[]{:S(2)}) collective-permute-start(f32[2,96,128]{2,0,1:T(2,128)S(1)} %pad_maximum_fusion), channel_id=1, source_target_pairs={{0,448},{32,96},{64,0},{96,160},{128,64},{160,224},{192,128},{224,... | collective-permute-start | bytes 294920 | tf_op jit(solution)/shard_map/ppermute | solution.py:402
  35.0 9.4 %collective-permute-start.2 = (f32[2,96,128]{2,0,1:T(2,128)S(1)}, f32[2,96,128]{2,0,1:T(2,128)S(1)}, u32[]{:S(2)}, u32[]{:S(2)}) collective-permute-start(f32[2,96,128]{2,0,1:T(2,128)S(1)} %pad_maximum_fusion), channel_id=1, source_target_pairs={{0,128},{32,416},{64,192},{96,480},{128,256},{160,32},{192,320},{2... | collective-permute-start | bytes 294920 | tf_op jit(solution)/shard_map/ppermute | solution.py:402
  38.6 7.7 %collective-permute-start.1 = (f32[2,96,128]{2,0,1:T(2,128)S(1)}, f32[2,96,128]{2,0,1:T(2,128)S(1)}, u32[]{:S(2)}, u32[]{:S(2)}) collective-permute-start(f32[2,96,128]{2,0,1:T(2,128)S(1)} %pad_maximum_fusion), channel_id=1, source_target_pairs={{0,64},{32,480},{64,128},{96,32},{128,192},{160,96},{192,256},{224... | collective-permute-start | bytes 294920 | tf_op jit(solution)/shard_map/ppermute | solution.py:402
  41.2 0.7 %copy-start.8 = (s32[4,6]{1,0:T(4,128)S(1)}, s32[4,6]{1,0:T(4,128)}, u32[]{:S(2)}) copy-start(s32[4,6]{1,0:T(4,128)} %list_pair.1) | copy-start | bytes 292
  46.3 4.0 %collective-permute-start.6 = (f32[32,40,128]{2,1,0:T(8,128)S(1)}, f32[32,40,128]{2,1,0:T(8,128)S(1)}, u32[]{:S(2)}, u32[]{:S(2)}) collective-permute-start(f32[32,40,128]{2,1,0:T(8,128)S(1)} %all-to-all-done.refs_0_), channel_id=1, source_target_pairs={{0,32},{32,0},{1,33},{33,1},{2,34},{34,2},{3,35},{35,3},{4,36},{36... | collective-permute-start | bytes 1966088 | tf_op jit(solution)/shard_map/ppermute | solution.py:430

commit v11 on v8

--- a/solution.py
+++ b/solution.py
@@ -123,9 +123,6 @@
     writes = [pltpu.make_async_copy(r, o, out_sems.at[n]) for n, (r, o) in enumerate(zip(results, outs))]
     for copy in copies:
         copy.wait()
-    for n, block in enumerate(weights_of(held[4:], natural)):
-        weight_ref[0, RANK * n : RANK * (n + 1), :] = block
-    writes[0].start()
     basis_copy.wait()
     for i in range(leaves):
         tractions[i].wait()
@@ -147,6 +144,9 @@
         send_ref[d, 0:RANK, :] = coeff
         send_ref[d, RANK : RANK + ROWS8, :] = up
     writes[2].start()
+    for n, block in enumerate(weights_of(held[4:], natural)):
+        weight_ref[0, RANK * n : RANK * (n + 1), :] = block
+    writes[0].start()
     for write in writes:
         write.wait()
 

time: 65.8 us -> 65.5 us (level)
  no operation moved by 1% of the time
where the time goes in v11:
time: 65.5 us; the launch traced here: 65 us
  starting transfers between devices  38.7 us (59%)
  blocking collectives  12.4 us (19%)
  Pallas kernels  10.3 us (16%)
  waiting for transfers between devices  2.49 us (4%)
  local copies, waits for them, and re-layouts  0.7 us (1%)
    ppermute x4, starting transfers between devices, over_y(): return lax.ppermute(block, ('y', 'core'), moves)  16.4 us
    all_to_all x1, starting transfers between devices, body(): coeffs = lax.all_to_all(send, ('x', 'z'), 0, 0, tiled=True)  13.6 us
    all_to_all x1, blocking collectives, body(): parts = lax.all_to_all(parts, 'y', 0, 0, tiled=True)  12.4 us
    pallas_call x5, Pallas kernels, whole(): pl.pallas_call(kernel, out_shape=out, in_specs=[scalars if n in smem else...  10.3 us
    ppermute x1, starting transfers between devices, body(): high = lax.ppermute(stack, leaf_axes, [(i + 1, i) for i in range(subs - 1)])  4.87 us
    ppermute x4, waiting for transfers between devices, over_y(): return lax.ppermute(block, ('y', 'core'), moves)  2.01 us
    ppermute x1, starting transfers between devices, body(): low = lax.ppermute(stack, leaf_axes, [(i, i + 1) for i in range(subs - 1)])  1.92 us
    ppermute x1, starting transfers between devices, body(): other = lax.ppermute(coeffs, 'core', [(0, 1), (1, 0)])  1.91 us
  transfers between devices with their start and end apart: 8, of which 2 were waited for; matrix products, arithmetic and copies ran while one was open for 0% of the time, Pallas kernels for 6%

profile of v11, /device:TPU:6, one launch (start us, length us, event | category | flops | bytes accessed | tf_op | source)
XLA Modules:
  0.0 65.0 jit_solution(12877036426064781023)
XLA Ops:
  0.0 3.8 %shard_map.199 = (f32[1,96,128]{2,1,0:T(8,128)}, f32[384,128]{1,0:T(8,128)}, f32[32,40,128]{2,1,0:T(8,128)}) custom-call(f32[8,192,128]{2,1,0:T(8,128)} %refs_0_.1, f32[8,32,192]{2,1,0:T(8,128)} %refs_1_.1, f32[64,128]{1,0:T(8,128)} %bitcast.53, f32[32,128]{1,0:T(8,128)} %bitcast.55, f32[8,128]{1,0:T(8,128)} %bitcast.57, f32[48,128]{1,0:T(8,128)} %bitcast.54, ...), custom_call_target="tpu_custom_call" | custom-call | flops 60000000 | bytes 1982544 | tf_op jit(solution)/shard_map/pallas_call | solution.py:322
  3.8 0.0 copy-start.10
  3.8 0.0 copy-start.2
  3.8 0.0 copy-start
  3.9 0.0 copy-start.3
  3.9 0.0 copy-start.4
  3.9 0.0 copy-start.5
  3.9 13.6 %all-to-all-start = ((f32[32,40,128]{2,1,0:T(8,128)}), f32[32,40,128]{2,1,0:T(8,128)S(1)}, u32[]{:S(2)}, u32[]{:S(2)}) async-start(f32[32,40,128]{2,1,0:T(8,128)} %get-tuple-element.17), calls=%async_computation | async-start | bytes 1310720 | tf_op jit(solution)/shard_map/all_to_all | solution.py:403
  17.5 0.0 copy-start.1
  17.5 0.0 copy-done.10
  17.5 7.9 %collective-permute-start = (f32[1,96,128]{2,0,1:T(1,128)S(1)}, f32[1,96,128]{2,0,1:T(1,128)S(1)}, u32[]{:S(2)}, u32[]{:S(2)}) collective-permute-start(f32[1,96,128]{2,0,1:T(1,128)S(1)} %bitcast.51), channel_id=1, source_target_pairs={{0,256},{32,288},{64,320},{96,352},{128,384},{160,416},{192,448},{... | collective-permute-start | bytes 147464 | tf_op jit(solution)/shard_map/ppermute | solution.py:400
  25.4 0.0 copy-done.2
  25.4 4.9 %collective-permute-start.5 = (f32[384,128]{1,0:T(8,128)S(1)}, f32[384,128]{1,0:T(8,128)S(1)}, u32[]{:S(2)}, u32[]{:S(2)}) collective-permute-start(f32[384,128]{1,0:T(8,128)S(1)} %copy-done.2), channel_id=1, source_target_pairs={{1,0},{2,1},{3,2},{4,3},{5,4},{6,5},{7,6},{8,7},{9,8},{10,9},{11,1... | collective-permute-start | bytes 589832 | tf_op jit(solution)/shard_map/ppermute | solution.py:407
  30.3 1.9 %collective-permute-start.4 = (f32[384,128]{1,0:T(8,128)S(1)}, f32[384,128]{1,0:T(8,128)S(1)}, u32[]{:S(2)}, u32[]{:S(2)}) collective-permute-start(f32[384,128]{1,0:T(8,128)S(1)} %copy-done.2), channel_id=1, source_target_pairs={{0,1},{1,2},{2,3},{3,4},{4,5},{5,6},{6,7},{7,8},{8,9},{9,10},{10,1... | collective-permute-start | bytes 589832 | tf_op jit(solution)/shard_map/ppermute | solution.py:406
  32.2 0.0 collective-permute-done
  32.2 0.0 copy-start.7
  32.2 0.0 copy-start.9
  32.2 0.1 pad_maximum_fusion
  32.3 0.0 copy-start.6
  32.4 2.4 %collective-permute-start.3 = (f32[2,96,128]{2,0,1:T(2,128)S(1)}, f32[2,96,128]{2,0,1:T(2,128)S(1)}, u32[]{:S(2)}, u32[]{:S(2)}) collective-permute-start(f32[2,96,128]{2,0,1:T(2,128)S(1)} %pad_maximum_fusion), channel_id=1, source_target_pairs={{0,448},{32,96},{64,0},{96,160},{128,64},{160,224},{192,128},{224,... | collective-permute-start | bytes 294920 | tf_op jit(solution)/shard_map/ppermute | solution.py:400
  34.7 3.6 %collective-permute-start.2 = (f32[2,96,128]{2,0,1:T(2,128)S(1)}, f32[2,96,128]{2,0,1:T(2,128)S(1)}, u32[]{:S(2)}, u32[]{:S(2)}) collective-permute-start(f32[2,96,128]{2,0,1:T(2,128)S(1)} %pad_maximum_fusion), channel_id=1, source_target_pairs={{0,128},{32,416},{64,192},{96,480},{128,256},{160,32},{192,320},{2... | collective-permute-start | bytes 294920 | tf_op jit(solution)/shard_map/ppermute | solution.py:400
  38.3 2.6 %collective-permute-start.1 = (f32[2,96,128]{2,0,1:T(2,128)S(1)}, f32[2,96,128]{2,0,1:T(2,128)S(1)}, u32[]{:S(2)}, u32[]{:S(2)}) collective-permute-start(f32[2,96,128]{2,0,1:T(2,128)S(1)} %pad_maximum_fusion), channel_id=1, source_target_pairs={{0,64},{32,480},{64,128},{96,32},{128,192},{160,96},{192,256},{224... | collective-permute-start | bytes 294920 | tf_op jit(solution)/shard_map/ppermute | solution.py:400
  40.9 0.0 collective-permute-done.5.high_ref
  40.9 0.0 collective-permute-done.4.low_ref
  40.9 0.0 copy-start.8
  41.0 0.0 copy-done
  41.0 0.0 copy-done.3
  41.0 0.0 copy-done.4
  41.0 0.0 copy-done.5
  41.0 0.0 copy-done.1
  41.0 0.0 copy-done.7
  41.0 0.0 copy-done.9
  41.0 0.0 copy-done.6
  41.0 0.6 copy-done.8
  41.6 2.4 %shard_map.200 = (f32[8,192,128]{2,1,0:T(8,128)S(1)}, bf16[8,192,128]{2,1,0:T(8,128)(2,1)S(1)}) custom-call(f32[384,128]{1,0:T(8,128)S(1)} %collective-permute-done.4.low_ref, f32[384,128]{1,0:T(8,128)S(1)} %copy-done.2, f32[384,128]{1,0:T(8,128)S(1)} %collective-permute-done.5.high_ref, f32[384,128]{1,0:T(8,128)S(1)} %bitcast.47, f32[192,128]{1,0:T(8,128)S(1)} %bitcast.48, ...), custom_call_target="tpu_custom_call" | custom-call | flops 100000000 | bytes 2310720 | tf_op jit(solution)/shard_map/pallas_call | solution.py:322
  44.0 0.0 collective-permute-done.3
  44.0 0.0 collective-permute-done.2
  44.0 2.0 %collective-permute-done.1 = f32[2,96,128]{2,0,1:T(2,128)S(1)} collective-permute-done((f32[2,96,128]{2,0,1:T(2,128)S(1)}, f32[2,96,128]{2,0,1:T(2,128)S(1)}, u32[]{:S(2)}, u32[]{:S(2)}) %collective-permute-start.1) | collective-permute-done | bytes 98336 | tf_op jit(solution)/shard_map/ppermute | solution.py:400
  46.1 0.0 all-to-all-done.refs_0_
  46.1 1.9 %collective-permute-start.6 = (f32[32,40,128]{2,1,0:T(8,128)S(1)}, f32[32,40,128]{2,1,0:T(8,128)S(1)}, u32[]{:S(2)}, u32[]{:S(2)}) collective-permute-start(f32[32,40,128]{2,1,0:T(8,128)S(1)} %all-to-all-done.refs_0_), channel_id=1, source_target_pairs={{0,32},{32,0},{1,33},{33,1},{2,34},{34,2},{3,35},{35,3},{4,36},{36... | collective-permute-start | bytes 1966088 | tf_op jit(solution)/shard_map/ppermute | solution.py:422
  48.1 1.5 %shard_map.201.refs_9_ = f32[8,32,128]{2,1,0:T(8,128)S(1)} custom-call(f32[32,40,128]{2,1,0:T(8,128)S(1)} %all-to-all-done.refs_0_, f32[2,96,128]{2,1,0:T(8,128)S(1)} %copy.32.refs_1_, f32[2,96,128]{2,1,0:T(8,128)S(1)} %copy.33.refs_2_, f32[2,96,128]{2,1,0:T(8,128)S(1)} %copy.34.refs_3_, f32[2,96,128]{2,1,0:T(8,128)S(1)} %copy.35.refs_4_, ...), custom_call_target="tpu_custom_call" | custom-call | flops 50000000 | bytes 1183744 | tf_op jit(solution)/shard_map/pallas_call | solution.py:322
  49.6 0.5 collective-permute-done.6.refs_0_
  50.0 1.5 %shard_map.202 = f32[8,32,128]{2,1,0:T(8,128)S(1)} custom-call(f32[32,40,128]{2,1,0:T(8,128)S(1)} %collective-permute-done.6.refs_0_, f32[2,96,128]{2,1,0:T(8,128)S(1)} %copy.32.refs_1_, f32[2,96,128]{2,1,0:T(8,128)S(1)} %copy.33.refs_2_, f32[2,96,128]{2,1,0:T(8,128)S(1)} %copy.34.refs_3_, f32[2,96,128]{2,1,0:T(8,128)S(1)} %copy.35.refs_4_, ...), custom_call_target="tpu_custom_call" | custom-call | flops 50000000 | bytes 1314816 | tf_op jit(solution)/shard_map/pallas_call | solution.py:322
  51.5 12.4 %all_to_all.10.parts_ref = f32[8,32,128]{2,1,0:T(8,128)S(1)} all-to-all(f32[8,32,128]{2,1,0:T(8,128)S(1)} %shard_map.202), channel_id=1, replica_groups=mesh['y'=8,'core'=2,'x'=4,'z'=8] {'y'}, dimensions={0} | all-to-all | bytes 262144 | tf_op jit(solution)/shard_map/all_to_all | solution.py:439
  63.9 1.1 %shard_map.203 = f32[8,192,128]{2,1,0:T(8,128)} custom-call(f32[8,32,128]{2,1,0:T(8,128)S(1)} %all_to_all.10.parts_ref, f32[8,192,128]{2,1,0:T(8,128)S(1)} %get-tuple-element.27.fixed_ref, bf16[8,192,128]{2,1,0:T(8,128)(2,1)S(1)} %get-tuple-element.28.slope_ref), custom_call_target="tpu_custom_call" | custom-call | flops 50000000 | bytes 2097152 | tf_op jit(solution)/shard_map/pallas_call | solution.py:322
  (6 shorter events, 0.0 us)
Async XLA Ops:
  3.8 13.7 %copy-start.10 = (f32[1,96,128]{2,1,0:T(8,128)S(1)}, f32[1,96,128]{2,1,0:T(8,128)}, u32[]{:S(2)}) copy-start(f32[1,96,128]{2,1,0:T(8,128)} %get-tuple-element.18) | copy-start | bytes 147460
  3.8 21.6 %copy-start.2 = (f32[384,128]{1,0:T(8,128)S(1)}, f32[384,128]{1,0:T(8,128)}, u32[]{:S(2)}) copy-start(f32[384,128]{1,0:T(8,128)} %get-tuple-element.19.own_ref) | copy-start | bytes 589828
  3.8 37.1 %copy-start = (f32[8,32,192]{2,1,0:T(8,128)S(1)}, f32[8,32,192]{2,1,0:T(8,128)}, u32[]{:S(2)}) copy-start(f32[8,32,192]{2,1,0:T(8,128)} %basis.1) | copy-start | bytes 589828
  3.9 37.1 %copy-start.3 = (f32[4,6,1024]{2,0,1:T(4,128)S(1)}, f32[4,6,1024]{2,0,1:T(4,128)}, u32[]{:S(2)}) copy-start(f32[4,6,1024]{2,0,1:T(4,128)} %param.27) | copy-start | bytes 294916
  3.9 37.1 %copy-start.4 = (f32[8,1024]{1,0:T(8,128)S(1)}, f32[8,1024]{1,0:T(8,128)}, u32[]{:S(2)}) copy-start(f32[8,1024]{1,0:T(8,128)} %param.38) | copy-start | bytes 98308
  3.9 37.1 %copy-start.5 = (f32[4,1024]{1,0:T(4,128)S(1)}, f32[4,1024]{1,0:T(4,128)}, u32[]{:S(2)}) copy-start(f32[4,1024]{1,0:T(4,128)} %param.39) | copy-start | bytes 49156
  3.9 42.2 %all-to-all-start = ((f32[32,40,128]{2,1,0:T(8,128)}), f32[32,40,128]{2,1,0:T(8,128)S(1)}, u32[]{:S(2)}, u32[]{:S(2)}) async-start(f32[32,40,128]{2,1,0:T(8,128)} %get-tuple-element.17), calls=%async_computation | async-start | bytes 1310720 | tf_op jit(solution)/shard_map/all_to_all | solution.py:403
  17.5 23.5 %copy-start.1 = (f32[8,6,1024]{2,0,1:T(8,128)S(1)}, f32[8,6,1024]{2,0,1:T(8,128)}, u32[]{:S(2)}) copy-start(f32[8,6,1024]{2,0,1:T(8,128)} %param.26) | copy-start | bytes 589828
  17.5 14.7 %collective-permute-start = (f32[1,96,128]{2,0,1:T(1,128)S(1)}, f32[1,96,128]{2,0,1:T(1,128)S(1)}, u32[]{:S(2)}, u32[]{:S(2)}) collective-permute-start(f32[1,96,128]{2,0,1:T(1,128)S(1)} %bitcast.51), channel_id=1, source_target_pairs={{0,256},{32,288},{64,320},{96,352},{128,384},{160,416},{192,448},{... | collective-permute-start | bytes 147464 | tf_op jit(solution)/shard_map/ppermute | solution.py:400
  25.4 15.5 %collective-permute-start.5 = (f32[384,128]{1,0:T(8,128)S(1)}, f32[384,128]{1,0:T(8,128)S(1)}, u32[]{:S(2)}, u32[]{:S(2)}) collective-permute-start(f32[384,128]{1,0:T(8,128)S(1)} %copy-done.2), channel_id=1, source_target_pairs={{1,0},{2,1},{3,2},{4,3},{5,4},{6,5},{7,6},{8,7},{9,8},{10,9},{11,1... | collective-permute-start | bytes 589832 | tf_op jit(solution)/shard_map/ppermute | solution.py:407
  30.3 10.7 %collective-permute-start.4 = (f32[384,128]{1,0:T(8,128)S(1)}, f32[384,128]{1,0:T(8,128)S(1)}, u32[]{:S(2)}, u32[]{:S(2)}) collective-permute-start(f32[384,128]{1,0:T(8,128)S(1)} %copy-done.2), channel_id=1, source_target_pairs={{0,1},{1,2},{2,3},{3,4},{4,5},{5,6},{6,7},{7,8},{8,9},{9,10},{10,1... | collective-permute-start | bytes 589832 | tf_op jit(solution)/shard_map/ppermute | solution.py:406
  32.2 8.8 %copy-start.7 = (s32[8,6]{1,0:T(8,128)S(1)}, s32[8,6]{1,0:T(8,128)}, u32[]{:S(2)}) copy-start(s32[8,6]{1,0:T(8,128)} %mask_leaf.1) | copy-start | bytes 580
  32.2 8.8 %copy-start.9 = (s32[4,6]{1,0:T(4,128)S(1)}, s32[4,6]{1,0:T(4,128)}, u32[]{:S(2)}) copy-start(s32[4,6]{1,0:T(4,128)} %mask_pair.1) | copy-start | bytes 292
  32.3 8.7 %copy-start.6 = (s32[8,6]{1,0:T(8,128)S(1)}, s32[8,6]{1,0:T(8,128)}, u32[]{:S(2)}) copy-start(s32[8,6]{1,0:T(8,128)} %list_leaf.1) | copy-start | bytes 580
  32.4 11.7 %collective-permute-start.3 = (f32[2,96,128]{2,0,1:T(2,128)S(1)}, f32[2,96,128]{2,0,1:T(2,128)S(1)}, u32[]{:S(2)}, u32[]{:S(2)}) collective-permute-start(f32[2,96,128]{2,0,1:T(2,128)S(1)} %pad_maximum_fusion), channel_id=1, source_target_pairs={{0,448},{32,96},{64,0},{96,160},{128,64},{160,224},{192,128},{224,... | collective-permute-start | bytes 294920 | tf_op jit(solution)/shard_map/ppermute | solution.py:400
  34.7 9.3 %collective-permute-start.2 = (f32[2,96,128]{2,0,1:T(2,128)S(1)}, f32[2,96,128]{2,0,1:T(2,128)S(1)}, u32[]{:S(2)}, u32[]{:S(2)}) collective-permute-start(f32[2,96,128]{2,0,1:T(2,128)S(1)} %pad_maximum_fusion), channel_id=1, source_target_pairs={{0,128},{32,416},{64,192},{96,480},{128,256},{160,32},{192,320},{2... | collective-permute-start | bytes 294920 | tf_op jit(solution)/shard_map/ppermute | solution.py:400
  38.3 7.7 %collective-permute-start.1 = (f32[2,96,128]{2,0,1:T(2,128)S(1)}, f32[2,96,128]{2,0,1:T(2,128)S(1)}, u32[]{:S(2)}, u32[]{:S(2)}) collective-permute-start(f32[2,96,128]{2,0,1:T(2,128)S(1)} %pad_maximum_fusion), channel_id=1, source_target_pairs={{0,64},{32,480},{64,128},{96,32},{128,192},{160,96},{192,256},{224... | collective-permute-start | bytes 294920 | tf_op jit(solution)/shard_map/ppermute | solution.py:400
  40.9 0.7 %copy-start.8 = (s32[4,6]{1,0:T(4,128)S(1)}, s32[4,6]{1,0:T(4,128)}, u32[]{:S(2)}) copy-start(s32[4,6]{1,0:T(4,128)} %list_pair.1) | copy-start | bytes 292
  46.1 4.0 %collective-permute-start.6 = (f32[32,40,128]{2,1,0:T(8,128)S(1)}, f32[32,40,128]{2,1,0:T(8,128)S(1)}, u32[]{:S(2)}, u32[]{:S(2)}) collective-permute-start(f32[32,40,128]{2,1,0:T(8,128)S(1)} %all-to-all-done.refs_0_), channel_id=1, source_target_pairs={{0,32},{32,0},{1,33},{33,1},{2,34},{34,2},{3,35},{35,3},{4,36},{36... | collective-permute-start | bytes 1966088 | tf_op jit(solution)/shard_map/ppermute | solution.py:422
